TPU v7x, 32 devices: a whole 2x2x4 slice. The times are simulated.
32 devices in a mesh: rows: 8 (over z, y), blk: 4 (over x, core).
Axes of the slice: x: 2, y: 2, z: 4, core: 2. Of those that a mesh axis runs over, the one named last changes fastest.
Arguments:
- features: bfloat16 [8192, 1024], P(('rows', 'blk')), may hold values from -6 to 6
- tiles: bfloat16 [32, 3, 256, 256], P(('rows', 'blk')), may hold values from -0.1875 to 0.1875
- tile_cols: int32 [32, 3], P(('rows', 'blk')), may hold values from 0 to 31, as said below
- tile_count: int32 [32], P(('rows', 'blk')), may hold values from 1 to 3
- weight: bfloat16 [1024, 1024], P(('rows', 'blk')), may hold values from -0.1875 to 0.1875
- cotangent: bfloat16 [8192, 1024], P(('rows', 'blk')), may hold values from -0.125 to 0.125
Outputs:
- output: bfloat16 [8192, 1024], P(('rows', 'blk'))
- weight_grad: float32 [1024, 1024], P(('rows', 'blk'))
Inputs may be any that keep to these rules, and one draw needn't show every extreme that they name: For each row block g, the first tile_count[g] entries of tile_cols[g] are distinct blocks of g's group of 4 blocks (blocks 4 * (g // 4) onward), each at most 1 positions from g around that group, g itself among them; the later entries are also blocks of that group and carry no tile.
All inputs are finite; a program needn't handle non-finite values.
Results may differ from a plain program's by a relative error of at most 0.0054.
Values may be sent and summed in bfloat16 or wider, within the bound.
No kernel may reach another device: no remote copies, remote signals or barrier semaphores. Data moves between devices by JAX's collectives and lax.ppermute only.
A program may use at most 64 MiB of HBM per device.

v0:
```python
import jax
import jax.numpy as jnp
from jax import lax
from jax.sharding import PartitionSpec as P


def passed_along(value, axis, by):
    length = lax.axis_size(axis)
    return lax.ppermute(value, axis, [(i, (i + by) % length) for i in range(length)])


def local(features, tiles, tile_cols, tile_count, weight, cotangent):
    cycle_len = lax.axis_size("blk")
    position = lax.axis_index("blk")
    per_dev = tiles.shape[0]
    slot_total = tiles.shape[1]
    tile_side = tiles.shape[2]
    group_len = cycle_len * per_dev
    slot_ids = jnp.arange(slot_total, dtype=jnp.int32)
    columns = tile_cols % group_len

    def apply_panel(totals, panel_now, source):
        running = totals[0]
        in_use = slot_ids < tile_count[0]
        wanted = source * per_dev + 0
        match = jnp.logical_and(in_use, columns[0] == wanted)
        present = jnp.any(match)
        chosen_slot = jnp.sum(jnp.where(match, slot_ids, 0))
        chosen = lax.dynamic_index_in_dim(tiles[0], chosen_slot, 0, keepdims=False)
        rows_there = panel_now

        def multiply(chosen=chosen, rows_there=rows_there):
            return jnp.dot(chosen, rows_there, preferred_element_type=jnp.float32)

        def nothing():
            return jnp.zeros(running.shape, jnp.float32)

        running = running + lax.cond(present, multiply, nothing)
        updated = [running]
        return tuple(updated)

    empty = jnp.zeros((tile_side, features.shape[1]), jnp.float32)
    totals = tuple((empty for block_here in range(per_dev)))
    totals = apply_panel(totals, features, position)
    reach_blocks = min(3, (group_len - 1) // 2)
    reach_dev = (reach_blocks + per_dev - 1) // per_dev
    from_left = features
    from_right = features
    for offset in range(1, reach_dev + 1):
        from_left = passed_along(from_left, "blk", 1)
        totals = apply_panel(totals, from_left, (position - offset + cycle_len) % cycle_len)
        from_right = passed_along(from_right, "blk", -1)
        totals = apply_panel(totals, from_right, (position + offset) % cycle_len)
    aggregated = totals[0].astype(jnp.bfloat16)
    pre_act = lax.dot_general(
        aggregated,
        lax.all_gather(weight, ("rows", "blk"), axis=0, tiled=True),
        (((1,), (1,)), ((), ())),
        preferred_element_type=jnp.float32,
    )
    output = jax.nn.silu(pre_act).astype(jnp.bfloat16)
    sigmoid_y = jax.nn.sigmoid(pre_act)
    grad_pre = (
        cotangent.astype(jnp.float32) * sigmoid_y * (1.0 + pre_act * (1.0 - sigmoid_y))
    ).astype(jnp.bfloat16)
    weight_grad = lax.psum_scatter(
        lax.dot_general(
            grad_pre, aggregated, (((0,), (0,)), ((), ())), preferred_element_type=jnp.float32
        ),
        ("rows", "blk"),
        scatter_dimension=0,
        tiled=True,
    )
    return (output, weight_grad)


def solution(mesh):
    in_specs = (
        P(("rows", "blk"), None),
        P(("rows", "blk"), None, None, None),
        P(("rows", "blk"), None),
        P(("rows", "blk")),
        P(("rows", "blk"), None),
        P(("rows", "blk"), None),
    )
    out_specs = (P(("rows", "blk"), None), P(("rows", "blk"), None))
    return jax.shard_map(local, mesh=mesh, in_specs=in_specs, out_specs=out_specs, check_vma=False)
```

profile of v0, /device:TPU:0, one launch (start us, length us, event | category | flops | bytes accessed | tf_op | source)
XLA Modules:
  0.0 222.9 jit_solution(13967145267294514328)
XLA Ops:
  7.2 0.0 all-gather.2.cloned.1.call-start
  7.2 0.7 all-gather.2.cloned.1.call-update
  7.9 0.0 reduce-scatter.2.cloned.1.call-start
  7.9 2.4 %collective-permute-start.1 = (bf16[256,1024]{1,0:T(8,128)(2,1)}, bf16[256,1024]{1,0:T(8,128)(2,1)S(1)}, u32[]{:S(2)}, u32[]{:S(2)}) collective-permute-start(bf16[256,1024]{1,0:T(8,128)(2,1)} %param.12), channel_id=1, source_target_pairs={{0,3},{1,0},{2,1},{3,2},{4,7},{5,4},{6,5},{7,6},{8,11},{9,8},{10,9... | collective-permute-start | bytes 1572872 | tf_op jit(solution)/shard_map/ppermute | solution.py:9
  10.4 0.0 collective-permute-start
  11.0 1.3 fusion.16
  12.3 0.7 fusion.17
  14.9 4.0 %conditional.3 = (f32[256,1024]{1,0:T(8,128)S(1)}) conditional(s32[]{:T(128)} %convert_element_type.21, () %tuple.32, (pred[3]{0:T(512)(128)(4,1)S(1)}, bf16[1,3,256,256]{3,2,1,0:T(8,128)(2,1)}, bf16[256,1024]{1,0:T(8,128)(2,1)}, s32[]{:T(128)}, s32[3]{0:T(128)S(1)}, /*index=5*/s32[]{:T(128)}) %tuple.33), branch_computations={%region_2.3_spmd, %region_3.4_spmd} | conditional | flops 134217728 | bytes 1704009 | solution.py:38
  14.9 0.6 select_reduce_fusion
  17.5 1.4 fusion
  18.9 4.2 %collective-permute-done.1 = bf16[256,1024]{1,0:T(8,128)(2,1)S(1)} collective-permute-done((bf16[256,1024]{1,0:T(8,128)(2,1)}, bf16[256,1024]{1,0:T(8,128)(2,1)S(1)}, u32[]{:S(2)}, u32[]{:S(2)}) %collective-permute-start.1) | collective-permute-done | bytes 524320 | tf_op jit(solution)/shard_map/ppermute | solution.py:9
  23.1 3.8 %conditional.5 = (f32[256,1024]{1,0:T(8,128)S(1)}) conditional(s32[]{:T(128)} %convert_element_type.23, () %tuple.36, (pred[3]{0:T(512)(128)(4,1)S(1)}, bf16[1,3,256,256]{3,2,1,0:T(8,128)(2,1)}, bf16[256,1024]{1,0:T(8,128)(2,1)S(1)}, s32[]{:T(128)}, s32[3]{0:T(128)S(1)}, /*index=5*/s32[]{:T(128)}) %tuple.37), branch_computations={%region_10.11_spmd, %region_11.12_spmd} | conditional | flops 134217728 | bytes 1704009 | solution.py:38
  23.1 0.6 select_reduce_fusion.2
  25.7 1.2 fusion.8
  26.9 0.0 collective-permute-done
  26.9 4.1 %conditional.4 = (f32[256,1024]{1,0:T(8,128)S(1)}) conditional(s32[]{:T(128)} %convert_element_type.22, () %tuple.34, (pred[3]{0:T(512)(128)(4,1)S(1)}, bf16[1,3,256,256]{3,2,1,0:T(8,128)(2,1)}, bf16[256,1024]{1,0:T(8,128)(2,1)S(1)}, s32[]{:T(128)}, s32[3]{0:T(128)S(1)}, /*index=5*/s32[]{:T(128)}) %tuple.35), branch_computations={%region_6.7_spmd, %region_7.8_spmd} | conditional | flops 134217728 | bytes 3801189 | solution.py:38
  27.0 0.0 copy-start.1
  27.0 0.7 select_reduce_fusion.1
  29.0 0.0 copy-done.1
  29.6 1.4 fusion.4
  31.0 1.1 add_convert_fusion
  32.1 0.0 copy-start
  32.1 0.0 copy-start.2
  32.1 37.9 %all-gather.2.cloned.1.call-done = bf16[1024,1024]{1,0:T(8,128)(2,1)} async-done(((bf16[32,1024]{1,0:T(8,128)(2,1)}), bf16[1024,1024]{1,0:T(8,128)(2,1)}) %all-gather.2.cloned.1.call-update) | async-done | bytes 2097168 | tf_op jit(solution)/shard_map/all_gather | solution.py:57
  70.0 3.4 %multiply_convert_fusion.1 = (bf16[256,1024]{1,0:T(8,128)(2,1)}, f32[256,1024]{1,0:T(8,128)S(1)}) fusion(bf16[256,1024]{1,0:T(8,128)(2,1)} %add_convert_fusion, bf16[1024,1024]{1,0:T(8,128)(2,1)} %all-gather.2.cloned.1.call-done), kind=kOutput, calls=%fused_computation.16 | convolution fusion | flops 538181632 | bytes 4194304 | tf_op jit(solution)/shard_map/dot_general | solution.py:55
  73.4 0.0 copy-done
  73.4 0.0 copy-done.2
  73.4 3.0 %fusion.12 = f32[1024,1024]{1,0:T(8,128)} fusion(bf16[256,1024]{1,0:T(8,128)(2,1)S(1)} %copy-done, f32[256,1024]{1,0:T(8,128)S(1)} %get-tuple-element.141, bf16[256,1024]{1,0:T(8,128)(2,1)S(1)} %copy-done.2), kind=kOutput, calls=%fused_computation.19 | convolution fusion | flops 539492352 | bytes 6291456 | tf_op jit(solution)/shard_map/dot_general | solution.py:67
  76.3 0.0 reduce-scatter.2.cloned.1.call-update
  76.4 139.7 %reduce-scatter.2.cloned.1.call-done = f32[32,1024]{1,0:T(8,128)} async-done(((f32[1024,1024]{1,0:T(8,128)}), f32[32,1024]{1,0:T(8,128)}) %reduce-scatter.2.cloned.1.call-update) | async-done | bytes 131088 | tf_op jit(solution)/shard_map/reduce_scatter | solution.py:66
  (3 shorter events, 0.0 us)
Async XLA Ops:
  7.2 62.8 %all-gather.2.cloned.1.call-start = ((), (), s32[]{:S(2)}) async-start(), calls=%async_computation.1 | async-start | bytes 2162688 | tf_op jit(solution)/shard_map/all_gather | solution.py:57
  7.9 208.2 %reduce-scatter.2.cloned.1.call-start = ((), (), s32[]{:S(2)}) async-start(), calls=%async_computation.2 | async-start | bytes 4325376 | tf_op jit(solution)/shard_map/reduce_scatter | solution.py:66
  7.9 15.2 %collective-permute-start.1 = (bf16[256,1024]{1,0:T(8,128)(2,1)}, bf16[256,1024]{1,0:T(8,128)(2,1)S(1)}, u32[]{:S(2)}, u32[]{:S(2)}) collective-permute-start(bf16[256,1024]{1,0:T(8,128)(2,1)} %param.12), channel_id=1, source_target_pairs={{0,3},{1,0},{2,1},{3,2},{4,7},{5,4},{6,5},{7,6},{8,11},{9,8},{10,9... | collective-permute-start | bytes 1572872 | tf_op jit(solution)/shard_map/ppermute | solution.py:9
  10.4 16.6 %collective-permute-start = (bf16[256,1024]{1,0:T(8,128)(2,1)}, bf16[256,1024]{1,0:T(8,128)(2,1)S(1)}, u32[]{:S(2)}, u32[]{:S(2)}) collective-permute-start(bf16[256,1024]{1,0:T(8,128)(2,1)} %param.12), channel_id=1, source_target_pairs={{0,1},{1,2},{2,3},{3,0},{4,5},{5,6},{6,7},{7,4},{8,9},{9,10},{10,1... | collective-permute-start | bytes 1572872 | tf_op jit(solution)/shard_map/ppermute | solution.py:9
  27.0 2.0 copy-start.1
  32.1 41.3 %copy-start = (bf16[256,1024]{1,0:T(8,128)(2,1)S(1)}, bf16[256,1024]{1,0:T(8,128)(2,1)}, u32[]{:S(2)}) copy-start(bf16[256,1024]{1,0:T(8,128)(2,1)} %add_convert_fusion) | copy-start | bytes 1572868
  32.1 41.3 %copy-start.2 = (bf16[256,1024]{1,0:T(8,128)(2,1)S(1)}, bf16[256,1024]{1,0:T(8,128)(2,1)}, u32[]{:S(2)}) copy-start(bf16[256,1024]{1,0:T(8,128)(2,1)} %param.17) | copy-start | bytes 1572868
Sparse Core Ops, SparseCore 0:
  10.9 59.0 all-gather.1
  76.5 139.5 reduce-scatter.1
where the time goes:
time: 223 us
  waiting for transfers between devices  182 us (82%)
  between operations  16.6 us (7%)
  matrix products  10.4 us (5%)
  loops' own time  5.9 us (3%)
  other arithmetic  4.97 us (2%)
  starting transfers between devices  2.51 us (1%)
    reduce_scatter x1, waiting for transfers between devices, local(): lax.psum_scatter(lax.dot_general(grad_pre, aggregated, (((0,), (0,)), (()...  140 us
    all_gather x1, waiting for transfers between devices, local(): lax.all_gather(weight, ('rows', 'blk'), axis=0, tiled=True)  37.9 us
    another operation x3, loops' own time, apply_panel(): running = running + lax.cond(present, multiply, nothing)  5.9 us
  transfers between devices with their start and end apart: 4, of which 3 were waited for; matrix products, arithmetic and copies ran while one was open for 4% of the time, Pallas kernels for 0%

commit v1 on v0

v1 whole, which is shorter than its diff:
```python
import jax
import jax.numpy as jnp
from jax import lax
from jax.experimental import pallas as pl
from jax.experimental.pallas import tpu as pltpu
from jax.sharding import PartitionSpec as P

AXES = ("rows", "blk")
CORE = 1
F32 = jnp.float32
BF16 = jnp.bfloat16


def swap(value, mask):
    total = lax.axis_size(AXES)
    return lax.ppermute(value, AXES, [(i, i ^ mask) for i in range(total)])


def shifted(value, by):
    length = lax.axis_size("blk")
    return lax.ppermute(value, "blk", [(i, (i + by) % length) for i in range(length)])


def neighbour_blocks(features, reach):
    length = lax.axis_size("blk")
    position = lax.axis_index("blk")
    if length == 4 and reach == 1:
        return [(position ^ 3, swap(features, 3)), (position ^ 1, swap(features, 1))]
    found = []
    for offset in range(1, reach + 1):
        found.append(((position - offset) % length, shifted(features, offset)))
        found.append(((position + offset) % length, shifted(features, -offset)))
    return found


def gather_weight(weight):
    total = lax.axis_size(AXES)
    if total == 32:
        x, y, z = 2, 4, (8, 16, 24)
        pair = jnp.concatenate([weight, swap(weight, x)])
        along = [pair] + [swap(pair, m) for m in z]
        near = swap(jnp.concatenate(along[:2]), y)
        far = swap(jnp.concatenate(along[2:]), y)
        masks = [b * x + c * y + a * 8 for c in range(2) for a in range(4) for b in range(2)]
        return along + [near, far], masks
    held = weight
    bit = 2
    while bit < total:
        held = jnp.concatenate([held, swap(held, bit)])
        bit *= 2
    return [held], [2 * s for s in range(total // 2)]


def one_hot_rows(me, masks, rows, width):
    owner = jnp.repeat(jnp.asarray(masks, jnp.int32) ^ me, rows)
    at = owner * rows + jnp.tile(jnp.arange(rows, dtype=jnp.int32), len(masks))
    return (at[:, None] == jnp.arange(width, dtype=jnp.int32)[None, :]).astype(BF16)


def layer_kernel(n_pieces, rows, split, *refs):
    agg_own, agg_other, cot_own, cot_other = refs[:4]
    pieces = refs[4 : 4 + n_pieces]
    out_own, out_other = refs[4 + n_pieces : 6 + n_pieces]
    grads = refs[6 + n_pieces : -2]
    w_all, a_all = refs[-2:]
    nodes = agg_own.shape[0]
    at = 0
    for piece in pieces:
        w_all[at : at + piece.shape[0], :] = piece[...]
        at += piece.shape[0]
    a_all[:nodes, :] = agg_own[...]
    a_all[nodes:, :] = agg_other[...]
    step = 128
    for first in range(0, w_all.shape[0], step):
        part = pl.ds(first, step)
        pre = lax.dot_general(
            w_all[part, :], a_all[...], (((1,), (1,)), ((), ())), preferred_element_type=F32
        )
        s = jax.nn.sigmoid(pre)
        out = (pre * s).astype(BF16)
        out_own[part, :] = out[:, :nodes]
        out_other[part, :] = out[:, nodes:]
        slope = s * (1.0 + pre * (1.0 - s))
        gp_own = (cot_own[part, :].astype(F32) * slope[:, :nodes]).astype(BF16)
        gp_other = (cot_other[part, :].astype(F32) * slope[:, nodes:]).astype(BF16)
        grad = jnp.dot(
            jnp.concatenate([gp_own, gp_other], axis=1), a_all[...], preferred_element_type=F32
        )
        if split is None:
            grads[0][part, :] = grad
            continue
        for k in range(step // rows):
            slot = first // rows + k
            p, z = slot // 8 * 2 + slot % 2, slot // 2 % 4
            value = grad[k * rows : (k + 1) * rows, :]
            to_a, to_c = pl.ds(z * rows, rows), pl.ds(p * rows, rows)
            grads[p][to_a, :] = value[:, :split].astype(grads[p].dtype)
            grads[4 + z][to_c, :] = value[:, split:].astype(grads[4 + z].dtype)


def layer(agg_own, agg_other, cot_own, cot_other, pieces, rows, split):
    nodes, width = agg_own.shape
    outs = cot_own.shape[0]
    shapes = [jax.ShapeDtypeStruct((outs, nodes), BF16)] * 2
    if split is None:
        shapes.append(jax.ShapeDtypeStruct((outs, width), F32))
    else:
        for columns in (split, width - split):
            for k in range(4):
                shapes.append(jax.ShapeDtypeStruct((4 * rows, columns), BF16 if k else F32))
    n_in = 4 + len(pieces)

    def body(*refs):
        layer_kernel(len(pieces), rows, split, *refs)

    in_vmem = pl.BlockSpec(memory_space=pltpu.VMEM)
    return pl.pallas_call(
        body,
        out_shape=shapes,
        in_specs=[in_vmem] * n_in,
        out_specs=[in_vmem] * len(shapes),
        scratch_shapes=[pltpu.VMEM((outs, width), BF16), pltpu.VMEM((2 * nodes, width), BF16)],
        compiler_params=pltpu.CompilerParams(vmem_limit_bytes=24 * 1024 * 1024),
        name="layer",
    )(agg_own, agg_other, cot_own, cot_other, *pieces)


def reduce_pieces(grads, rows):
    xy, z = (2, 4, 6), (8, 16, 24)
    a_in = [swap(grads[k], xy[k - 1]) for k in (1, 2, 3)]
    c_in = [swap(grads[4 + k], z[k - 1]) for k in (1, 2, 3)]
    a = grads[0] + sum(v.astype(F32) for v in a_in)
    c = grads[4] + sum(v.astype(F32) for v in c_in)
    a = a.reshape(4, rows, -1)
    c = c.reshape(4, rows, -1)
    a_in = [swap(a[k].astype(BF16), z[k - 1]) for k in (1, 2, 3)]
    c_in = [swap(c[k].astype(BF16), xy[k - 1]) for k in (1, 2, 3)]
    a = a[0] + sum(v.astype(F32) for v in a_in)
    c = c[0] + sum(v.astype(F32) for v in c_in)
    return jnp.concatenate([a, c], axis=1)


def reduce_halving(grad):
    bit = lax.axis_size(AXES) // 2
    while bit > 1:
        half = grad.shape[0] // 2
        grad = grad[:half] + swap(grad[half:].astype(BF16), bit).astype(F32)
        bit //= 2
    return grad


def local(features, tiles, tile_cols, tile_count, weight, cotangent):
    total = lax.axis_size(AXES)
    group_len = lax.axis_size("blk")
    position = lax.axis_index("blk")
    me = lax.axis_index(AXES)
    slot_total = tiles.shape[1]
    rows, width = weight.shape
    slot_ids = jnp.arange(slot_total, dtype=jnp.int32)
    in_use = slot_ids < tile_count[0]
    columns = tile_cols[0] % group_len

    def tile_of(source):
        match = jnp.logical_and(in_use, columns == source)
        return jnp.sum(jnp.where(match[:, None, None], tiles[0], 0), axis=0, dtype=BF16)

    pieces, masks = gather_weight(weight)
    blocks = neighbour_blocks(features, (slot_total - 1) // 2)

    mine = one_hot_rows(me, masks, rows, width)
    others = one_hot_rows(me ^ CORE, masks, rows, width)
    turn = (((1,), (1,)), ((), ()))
    cot_own = lax.dot_general(mine, cotangent, turn, preferred_element_type=F32).astype(BF16)
    cot_other = swap(
        lax.dot_general(others, cotangent, turn, preferred_element_type=F32).astype(BF16), CORE
    )

    summed = jnp.dot(tile_of(position), features, preferred_element_type=F32)
    for source, block in blocks[::-1]:
        summed = summed + jnp.dot(tile_of(source), block, preferred_element_type=F32)
    agg_own = summed.astype(BF16)
    agg_other = swap(agg_own, CORE)

    split = 640 if total == 32 and width == 1024 else None
    out_own, out_other, *grads = layer(
        agg_own, agg_other, cot_own, cot_other, pieces, rows, split
    )
    if split is None:
        weight_grad = reduce_halving(grads[0])
    else:
        weight_grad = reduce_pieces(grads, rows)

    out_t = jnp.concatenate([out_own, swap(out_other, CORE)])
    place = jnp.concatenate([mine, others])
    output = lax.dot_general(
        out_t, place, (((0,), (0,)), ((), ())), preferred_element_type=F32
    ).astype(BF16)
    return output, weight_grad


def solution(mesh):
    in_specs = (
        P(AXES, None),
        P(AXES, None, None, None),
        P(AXES, None),
        P(AXES),
        P(AXES, None),
        P(AXES, None),
    )
    out_specs = (P(AXES, None), P(AXES, None))
    return jax.shard_map(local, mesh=mesh, in_specs=in_specs, out_specs=out_specs, check_vma=False)
```

time: 223 us -> 76.7 us (0.34)
  waiting for transfers between devices: 182 us -> 34.5 us
  starting transfers between devices: 2.51 us -> 29.3 us
  between operations: 16.6 us -> 1.49 us
  matrix products: 10.4 us -> 4.18 us
  loops' own time: 5.9 us -> 0 us
  Pallas kernels: 0 us -> 2.69 us
    reduce_scatter x1 -> x0, waiting for transfers between devices: 140 us -> none  [local(): lax.psum_scatter(lax.dot_general(grad_pre, aggregated, (((0,), (0,)), (()...]
    all_gather x1 -> x0, waiting for transfers between devices: 37.9 us -> none  [local(): lax.all_gather(weight, ('rows', 'blk'), axis=0, tiled=True)]
    ppermute x2 -> x23, waiting for transfers between devices: 4.21 us -> 34.5 us  [swap(): return lax.ppermute(value, AXES, [(i, i ^ mask) for i in range(total)])]
    ppermute x2 -> x23, starting transfers between devices: 2.43 us -> 29.3 us  [swap(): return lax.ppermute(value, AXES, [(i, i ^ mask) for i in range(total)])]
    dot_general x5 -> x6, matrix products: 10.4 us -> 4.18 us  [the longest x1 1.54 us: local(): lax.dot_general(out_t, place, (((0,), (0,)), ((), ())), preferred_element...]
    another operation x3 -> x0, loops' own time: 5.9 us -> none  [apply_panel(): running = running + lax.cond(present, multiply, nothing)]
    pallas_call x0 -> x1, Pallas kernels: none -> 2.69 us  [layer(): pl.pallas_call(body, out_shape=shapes, in_specs=[in_vmem] * n_in, out_spe...]
  transfers between devices with their start and end apart: 4 -> 23, of which waited for: 3 -> 9; matrix products, arithmetic and copies ran while one was open for 4% -> 9% of each run, Pallas kernels for 0% -> 0%
where the time goes in v1:
time: 76.7 us; the launch traced here: 76.6 us
  waiting for transfers between devices  34.5 us (45%)
  starting transfers between devices  29.3 us (38%)
  matrix products  4.18 us (5%)
  other arithmetic  4.13 us (5%)
  Pallas kernels  2.69 us (4%)
  between operations  1.49 us (2%)
    ppermute x23, waiting for transfers between devices, swap(): return lax.ppermute(value, AXES, [(i, i ^ mask) for i in range(total)])  34.5 us
    ppermute x23, starting transfers between devices, swap(): return lax.ppermute(value, AXES, [(i, i ^ mask) for i in range(total)])  29.3 us
    pallas_call x1, Pallas kernels, layer(): pl.pallas_call(body, out_shape=shapes, in_specs=[in_vmem] * n_in, out_spe...  2.69 us
    dot_general x1, matrix products, local(): lax.dot_general(out_t, place, (((0,), (0,)), ((), ())), preferred_element...  1.54 us
  transfers between devices with their start and end apart: 23, of which 9 were waited for; matrix products, arithmetic and copies ran while one was open for 9% of the time, Pallas kernels for 0%

profile of v1, /device:TPU:0, one launch (start us, length us, event | category | flops | bytes accessed | tf_op | source)
XLA Modules:
  0.0 76.6 jit_solution(12476116108234137692)
XLA Ops:
  0.7 0.5 collective-permute-start
  1.2 2.6 %collective-permute-start.1 = (bf16[256,1024]{1,0:T(8,128)(2,1)}, bf16[256,1024]{1,0:T(8,128)(2,1)S(1)}, u32[]{:S(2)}, u32[]{:S(2)}) collective-permute-start(bf16[256,1024]{1,0:T(8,128)(2,1)} %param.8), channel_id=1, source_target_pairs={{0,3},{1,2},{2,1},{3,0},{4,7},{5,6},{6,5},{7,4},{8,11},{9,10},{10,... | collective-permute-start | bytes 1572872 | tf_op jit(solution)/shard_map/ppermute | solution.py:16
  3.8 0.7 xor_multiply_fusion.1
  4.5 0.1 iota_add_fusion
  4.5 0.1 add.88
  4.6 1.2 %convolution_convert_fusion = bf16[512,256]{1,0:T(8,128)(2,1)} fusion(bf16[256,1024]{1,0:T(8,128)(2,1)S(1)} %copy-done, s32[512]{0:T(512)S(1)} %add.88), kind=kOutput, calls=%fused_computation.10 | convolution fusion | flops 269090816 | bytes 788480 | tf_op jit(solution)/shard_map/dot_general | solution.py:175
  5.8 0.1 collective-permute-start.3
  5.9 0.3 collective-permute-start.4
  6.9 0.4 fusion.13
  7.3 10.5 %collective-permute-done.4 = bf16[32,1024]{1,0:T(8,128)(2,1)S(1)} collective-permute-done((bf16[32,1024]{1,0:T(8,128)(2,1)S(1)}, bf16[32,1024]{1,0:T(8,128)(2,1)S(1)}, u32[]{:S(2)}, u32[]{:S(2)}) %collective-permute-start.4) | collective-permute-done | bytes 65568 | tf_op jit(solution)/shard_map/ppermute | solution.py:16
  17.9 2.8 %collective-permute-start.6 = (bf16[64,1024]{1,0:T(8,128)(2,1)S(1)}, bf16[64,1024]{1,0:T(8,128)(2,1)S(1)}, u32[]{:S(2)}, u32[]{:S(2)}) collective-permute-start(bf16[64,1024]{1,0:T(8,128)(2,1)S(1)} %constant_dynamic-update-slice_fusion.refs_4_), channel_id=1, source_target_pairs={{0,16},{1,17},{2,18},{3,19},{4,20},{5,21},{6,22},{7,23},{8,24},{9,... | collective-permute-start | bytes 393224 | tf_op jit(solution)/shard_map/ppermute | solution.py:16
  20.7 1.3 %collective-permute-start.7 = (bf16[64,1024]{1,0:T(8,128)(2,1)S(1)}, bf16[64,1024]{1,0:T(8,128)(2,1)S(1)}, u32[]{:S(2)}, u32[]{:S(2)}) collective-permute-start(bf16[64,1024]{1,0:T(8,128)(2,1)S(1)} %constant_dynamic-update-slice_fusion.refs_4_), channel_id=1, source_target_pairs={{0,24},{1,25},{2,26},{3,27},{4,28},{5,29},{6,30},{7,31},{8,16},{9,... | collective-permute-start | bytes 393224 | tf_op jit(solution)/shard_map/ppermute | solution.py:16
  22.1 0.3 fusion.21
  22.4 8.3 %collective-permute-done.6.refs_6_ = bf16[64,1024]{1,0:T(8,128)(2,1)S(1)} collective-permute-done((bf16[64,1024]{1,0:T(8,128)(2,1)S(1)}, bf16[64,1024]{1,0:T(8,128)(2,1)S(1)}, u32[]{:S(2)}, u32[]{:S(2)}) %collective-permute-start.6) | collective-permute-done | bytes 131104 | tf_op jit(solution)/shard_map/ppermute | solution.py:16
  30.7 0.7 pad_maximum_fusion.1
  31.4 1.6 %collective-permute-start.9 = (bf16[128,1024]{1,0:T(8,128)(2,1)}, bf16[128,1024]{1,0:T(8,128)(2,1)S(1)}, u32[]{:S(2)}, u32[]{:S(2)}) collective-permute-start(bf16[128,1024]{1,0:T(8,128)(2,1)} %pad_maximum_fusion.1), channel_id=1, source_target_pairs={{0,4},{1,5},{2,6},{3,7},{4,0},{5,1},{6,2},{7,3},{8,12},{9,13},{10,... | collective-permute-start | bytes 786440 | tf_op jit(solution)/shard_map/ppermute | solution.py:16
  33.0 0.3 convolution_add_fusion.1
  33.3 0.3 fusion.7.refs_0_
  33.6 0.1 collective-permute-start.2
  33.7 2.0 %collective-permute-done.5.refs_5_ = bf16[64,1024]{1,0:T(8,128)(2,1)S(1)} collective-permute-done((bf16[64,1024]{1,0:T(8,128)(2,1)S(1)}, bf16[64,1024]{1,0:T(8,128)(2,1)S(1)}, u32[]{:S(2)}, u32[]{:S(2)}) %collective-permute-start.5) | collective-permute-done | bytes 131104 | tf_op jit(solution)/shard_map/ppermute | solution.py:16
  35.7 0.7 pad_maximum_fusion
  36.4 1.6 %collective-permute-start.8 = (bf16[128,1024]{1,0:T(8,128)(2,1)}, bf16[128,1024]{1,0:T(8,128)(2,1)S(1)}, u32[]{:S(2)}, u32[]{:S(2)}) collective-permute-start(bf16[128,1024]{1,0:T(8,128)(2,1)} %pad_maximum_fusion), channel_id=1, source_target_pairs={{0,4},{1,5},{2,6},{3,7},{4,0},{5,1},{6,2},{7,3},{8,12},{9,13},{10,... | collective-permute-start | bytes 786440 | tf_op jit(solution)/shard_map/ppermute | solution.py:16
  37.9 0.4 iota_compare_fusion
  38.3 0.1 add.86
  38.4 0.5 convolution_convert_fusion.1.refs_2_
  38.9 1.5 %collective-permute-done.9.refs_9_ = bf16[128,1024]{1,0:T(8,128)(2,1)S(1)} collective-permute-done((bf16[128,1024]{1,0:T(8,128)(2,1)}, bf16[128,1024]{1,0:T(8,128)(2,1)S(1)}, u32[]{:S(2)}, u32[]{:S(2)}) %collective-permute-start.9) | collective-permute-done | bytes 262176 | tf_op jit(solution)/shard_map/ppermute | solution.py:16
  40.5 4.3 %collective-permute-done.8.refs_8_ = bf16[128,1024]{1,0:T(8,128)(2,1)S(1)} collective-permute-done((bf16[128,1024]{1,0:T(8,128)(2,1)}, bf16[128,1024]{1,0:T(8,128)(2,1)S(1)}, u32[]{:S(2)}, u32[]{:S(2)}) %collective-permute-start.8) | collective-permute-done | bytes 262176 | tf_op jit(solution)/shard_map/ppermute | solution.py:16
  44.8 2.7 %layer.1 = (bf16[512,256]{1,0:T(8,128)(2,1)S(1)}, bf16[512,256]{1,0:T(8,128)(2,1)S(1)}, f32[128,640]{1,0:T(8,128)S(1)}, bf16[128,640]{1,0:T(8,128)(2,1)S(1)}, bf...) custom-call(bf16[256,1024]{1,0:T(8,128)(2,1)S(1)} %fusion.7.refs_0_,, ...), custom_call_target="tpu_custom_call" | custom-call | tf_op jit(solution)/shard_map/layer/pallas_call | solution.py:117
  47.5 3.1 %collective-permute-start.17 = (bf16[128,384]{1,0:T(8,128)(2,1)S(1)}, bf16[128,384]{1,0:T(8,128)(2,1)S(1)}, u32[]{:S(2)}, u32[]{:S(2)}) collective-permute-start(bf16[128,384]{1,0:T(8,128)(2,1)S(1)} %get-tuple-element.19), channel_id=1, source_target_pairs={{0,8},{1,9},{2,10},{3,11},{4,12},{5,13},{6,14},{7,15},{8,0},{9,1},... | collective-permute-start | bytes 294920 | tf_op jit(solution)/shard_map/ppermute | solution.py:16
  50.6 2.0 %collective-permute-start.18 = (bf16[128,384]{1,0:T(8,128)(2,1)S(1)}, bf16[128,384]{1,0:T(8,128)(2,1)S(1)}, u32[]{:S(2)}, u32[]{:S(2)}) collective-permute-start(bf16[128,384]{1,0:T(8,128)(2,1)S(1)} %get-tuple-element.20), channel_id=1, source_target_pairs={{0,16},{1,17},{2,18},{3,19},{4,20},{5,21},{6,22},{7,23},{8,24},{9,... | collective-permute-start | bytes 294920 | tf_op jit(solution)/shard_map/ppermute | solution.py:16
  52.6 1.4 %collective-permute-start.19 = (bf16[128,384]{1,0:T(8,128)(2,1)S(1)}, bf16[128,384]{1,0:T(8,128)(2,1)S(1)}, u32[]{:S(2)}, u32[]{:S(2)}) collective-permute-start(bf16[128,384]{1,0:T(8,128)(2,1)S(1)} %get-tuple-element.21), channel_id=1, source_target_pairs={{0,24},{1,25},{2,26},{3,27},{4,28},{5,29},{6,30},{7,31},{8,16},{9,... | collective-permute-start | bytes 294920 | tf_op jit(solution)/shard_map/ppermute | solution.py:16
  54.0 0.4 iota_compare_fusion.1
  54.4 1.6 %collective-permute-start.11 = (bf16[128,640]{1,0:T(8,128)(2,1)S(1)}, bf16[128,640]{1,0:T(8,128)(2,1)S(1)}, u32[]{:S(2)}, u32[]{:S(2)}) collective-permute-start(bf16[128,640]{1,0:T(8,128)(2,1)S(1)} %get-tuple-element.15), channel_id=1, source_target_pairs={{0,2},{1,3},{2,0},{3,1},{4,6},{5,7},{6,4},{7,5},{8,10},{9,11},{10,... | collective-permute-start | bytes 491528 | tf_op jit(solution)/shard_map/ppermute | solution.py:16
  55.9 1.5 %collective-permute-start.12 = (bf16[128,640]{1,0:T(8,128)(2,1)S(1)}, bf16[128,640]{1,0:T(8,128)(2,1)S(1)}, u32[]{:S(2)}, u32[]{:S(2)}) collective-permute-start(bf16[128,640]{1,0:T(8,128)(2,1)S(1)} %get-tuple-element.16), channel_id=1, source_target_pairs={{0,4},{1,5},{2,6},{3,7},{4,0},{5,1},{6,2},{7,3},{8,12},{9,13},{10,... | collective-permute-start | bytes 491528 | tf_op jit(solution)/shard_map/ppermute | solution.py:16
  57.4 0.5 collective-permute-start.13
  57.9 3.2 %collective-permute-done.18 = bf16[128,384]{1,0:T(8,128)(2,1)S(1)} collective-permute-done((bf16[128,384]{1,0:T(8,128)(2,1)S(1)}, bf16[128,384]{1,0:T(8,128)(2,1)S(1)}, u32[]{:S(2)}, u32[]{:S(2)}) %collective-permute-start.18) | collective-permute-done | bytes 98336 | tf_op jit(solution)/shard_map/ppermute | solution.py:16
  61.2 1.6 %collective-permute-start.20 = (bf16[32,384]{1,0:T(8,128)(2,1)S(1)}, bf16[32,384]{1,0:T(8,128)(2,1)S(1)}, u32[]{:S(2)}, u32[]{:S(2)}) collective-permute-start(bf16[32,384]{1,0:T(8,128)(2,1)S(1)} %get-tuple-element.34), channel_id=1, source_target_pairs={{0,2},{1,3},{2,0},{3,1},{4,6},{5,7},{6,4},{7,5},{8,10},{9,11},{10,... | collective-permute-start | bytes 73736 | tf_op jit(solution)/shard_map/ppermute | solution.py:16
  62.7 1.5 %collective-permute-start.21 = (bf16[32,384]{1,0:T(8,128)(2,1)S(1)}, bf16[32,384]{1,0:T(8,128)(2,1)S(1)}, u32[]{:S(2)}, u32[]{:S(2)}) collective-permute-start(bf16[32,384]{1,0:T(8,128)(2,1)S(1)} %get-tuple-element.36), channel_id=1, source_target_pairs={{0,4},{1,5},{2,6},{3,7},{4,0},{5,1},{6,2},{7,3},{8,12},{9,13},{10,... | collective-permute-start | bytes 73736 | tf_op jit(solution)/shard_map/ppermute | solution.py:16
  64.3 0.2 collective-permute-done.12
  64.5 0.9 %collective-permute-start.22 = (bf16[32,384]{1,0:T(8,128)(2,1)S(1)}, bf16[32,384]{1,0:T(8,128)(2,1)S(1)}, u32[]{:S(2)}, u32[]{:S(2)}) collective-permute-start(bf16[32,384]{1,0:T(8,128)(2,1)S(1)} %get-tuple-element.35), channel_id=1, source_target_pairs={{0,6},{1,7},{2,4},{3,5},{4,2},{5,3},{6,0},{7,1},{8,14},{9,15},{10,... | collective-permute-start | bytes 73736 | tf_op jit(solution)/shard_map/ppermute | solution.py:16
  65.4 0.1 fusion.17
  65.5 1.1 %collective-permute-start.14 = (bf16[32,640]{1,0:T(8,128)(2,1)S(1)}, bf16[32,640]{1,0:T(8,128)(2,1)S(1)}, u32[]{:S(2)}, u32[]{:S(2)}) collective-permute-start(bf16[32,640]{1,0:T(8,128)(2,1)S(1)} %get-tuple-element.31), channel_id=1, source_target_pairs={{0,8},{1,9},{2,10},{3,11},{4,12},{5,13},{6,14},{7,15},{8,0},{9,1},... | collective-permute-start | bytes 122888 | tf_op jit(solution)/shard_map/ppermute | solution.py:16
  66.5 2.0 %collective-permute-start.15 = (bf16[32,640]{1,0:T(8,128)(2,1)S(1)}, bf16[32,640]{1,0:T(8,128)(2,1)S(1)}, u32[]{:S(2)}, u32[]{:S(2)}) collective-permute-start(bf16[32,640]{1,0:T(8,128)(2,1)S(1)} %get-tuple-element.33), channel_id=1, source_target_pairs={{0,16},{1,17},{2,18},{3,19},{4,20},{5,21},{6,22},{7,23},{8,24},{9,... | collective-permute-start | bytes 122888 | tf_op jit(solution)/shard_map/ppermute | solution.py:16
  68.5 1.4 %collective-permute-start.16 = (bf16[32,640]{1,0:T(8,128)(2,1)S(1)}, bf16[32,640]{1,0:T(8,128)(2,1)S(1)}, u32[]{:S(2)}, u32[]{:S(2)}) collective-permute-start(bf16[32,640]{1,0:T(8,128)(2,1)S(1)} %get-tuple-element.32), channel_id=1, source_target_pairs={{0,24},{1,25},{2,26},{3,27},{4,28},{5,29},{6,30},{7,31},{8,16},{9,... | collective-permute-start | bytes 122888 | tf_op jit(solution)/shard_map/ppermute | solution.py:16
  70.0 1.5 %collective-permute-done.15 = bf16[32,640]{1,0:T(8,128)(2,1)S(1)} collective-permute-done((bf16[32,640]{1,0:T(8,128)(2,1)S(1)}, bf16[32,640]{1,0:T(8,128)(2,1)S(1)}, u32[]{:S(2)}, u32[]{:S(2)}) %collective-permute-start.15) | collective-permute-done | bytes 40992 | tf_op jit(solution)/shard_map/ppermute | solution.py:16
  71.4 2.9 %collective-permute-done.16 = bf16[32,640]{1,0:T(8,128)(2,1)S(1)} collective-permute-done((bf16[32,640]{1,0:T(8,128)(2,1)S(1)}, bf16[32,640]{1,0:T(8,128)(2,1)S(1)}, u32[]{:S(2)}, u32[]{:S(2)}) %collective-permute-start.16) | collective-permute-done | bytes 40992 | tf_op jit(solution)/shard_map/ppermute | solution.py:16
  74.4 0.7 pad_maximum_fusion.2
  75.0 1.5 %fusion.4 = bf16[256,1024]{1,0:T(8,128)(2,1)} fusion(pred[512,1024]{1,0:T(32,128)(4,1)S(1)} %iota_compare_fusion, pred[512,1024]{1,0:T(32,128)(4,1)S(1)} %iota_compare_fusion.1, bf16[512,256]{1,0:T(8,128)(2,1)S(1)} %collective-permute-done.10, bf16[512,256]{1,0:T(8,128)(2,1)S(1)} %get-tuple-element.12), kind=kOutput, calls=%fused_computation.8 | convolution fusion | flops 539230208 | bytes 2097152 | tf_op jit(solution)/shard_map/dot_general | solution.py:195
  (35 shorter events, 0.2 us)
Async XLA Ops:
  0.6 4.0 %copy-start = (bf16[256,1024]{1,0:T(8,128)(2,1)S(1)}, bf16[256,1024]{1,0:T(8,128)(2,1)}, u32[]{:S(2)}) copy-start(bf16[256,1024]{1,0:T(8,128)(2,1)} %param.13) | copy-start | bytes 1572868
  0.6 5.3 %copy-start.3 = (bf16[32,1024]{1,0:T(8,128)(2,1)S(1)}, bf16[32,1024]{1,0:T(8,128)(2,1)}, u32[]{:S(2)}) copy-start(bf16[32,1024]{1,0:T(8,128)(2,1)} %param.12) | copy-start | bytes 196612
  0.7 6.2 %copy-start.4 = (s32[1,3]{1,0:T(1,128)S(1)}, s32[1,3]{1,0:T(1,128)}, u32[]{:S(2)}) copy-start(s32[1,3]{1,0:T(1,128)} %param.10) | copy-start | bytes 40
  0.7 6.3 %copy-start.2 = (bf16[1,3,256,256]{3,2,1,0:T(8,128)(2,1)S(1)}, bf16[1,3,256,256]{3,2,1,0:T(8,128)(2,1)}, u32[]{:S(2)}) copy-start(bf16[1,3,256,256]{3,2,1,0:T(8,128)(2,1)} %param.9) | copy-start | bytes 1179652
  0.7 32.3 %collective-permute-start = (bf16[256,1024]{1,0:T(8,128)(2,1)}, bf16[256,1024]{1,0:T(8,128)(2,1)S(1)}, u32[]{:S(2)}, u32[]{:S(2)}) collective-permute-start(bf16[256,1024]{1,0:T(8,128)(2,1)} %param.8), channel_id=1, source_target_pairs={{0,1},{1,0},{2,3},{3,2},{4,5},{5,4},{6,7},{7,6},{8,9},{9,8},{10,11... | collective-permute-start | bytes 1572872 | tf_op jit(solution)/shard_map/ppermute | solution.py:16
  1.2 32.1 %collective-permute-start.1 = (bf16[256,1024]{1,0:T(8,128)(2,1)}, bf16[256,1024]{1,0:T(8,128)(2,1)S(1)}, u32[]{:S(2)}, u32[]{:S(2)}) collective-permute-start(bf16[256,1024]{1,0:T(8,128)(2,1)} %param.8), channel_id=1, source_target_pairs={{0,3},{1,2},{2,1},{3,0},{4,7},{5,6},{6,5},{7,4},{8,11},{9,10},{10,... | collective-permute-start | bytes 1572872 | tf_op jit(solution)/shard_map/ppermute | solution.py:16
  4.6 17.4 %copy-start.1 = (bf16[256,1024]{1,0:T(8,128)(2,1)S(1)}, bf16[256,1024]{1,0:T(8,128)(2,1)}, u32[]{:S(2)}) copy-start(bf16[256,1024]{1,0:T(8,128)(2,1)} %param.8) | copy-start | bytes 1572868
  5.8 33.1 %collective-permute-start.3 = (bf16[512,256]{1,0:T(8,128)(2,1)}, bf16[512,256]{1,0:T(8,128)(2,1)S(1)}, u32[]{:S(2)}, u32[]{:S(2)}) collective-permute-start(bf16[512,256]{1,0:T(8,128)(2,1)} %convolution_convert_fusion), channel_id=1, source_target_pairs={{0,1},{1,0},{2,3},{3,2},{4,5},{5,4},{6,7},{7,6},{8,9},{9,8},{10,11... | collective-permute-start | bytes 786440 | tf_op jit(solution)/shard_map/ppermute | solution.py:16
  5.9 12.0 %collective-permute-start.4 = (bf16[32,1024]{1,0:T(8,128)(2,1)S(1)}, bf16[32,1024]{1,0:T(8,128)(2,1)S(1)}, u32[]{:S(2)}, u32[]{:S(2)}) collective-permute-start(bf16[32,1024]{1,0:T(8,128)(2,1)S(1)} %copy-done.3), channel_id=1, source_target_pairs={{0,2},{1,3},{2,0},{3,1},{4,6},{5,7},{6,4},{7,5},{8,10},{9,11},{10,... | collective-permute-start | bytes 196616 | tf_op jit(solution)/shard_map/ppermute | solution.py:16
  17.9 12.8 %collective-permute-start.6 = (bf16[64,1024]{1,0:T(8,128)(2,1)S(1)}, bf16[64,1024]{1,0:T(8,128)(2,1)S(1)}, u32[]{:S(2)}, u32[]{:S(2)}) collective-permute-start(bf16[64,1024]{1,0:T(8,128)(2,1)S(1)} %constant_dynamic-update-slice_fusion.refs_4_), channel_id=1, source_target_pairs={{0,16},{1,17},{2,18},{3,19},{4,20},{5,21},{6,22},{7,23},{8,24},{9,... | collective-permute-start | bytes 393224 | tf_op jit(solution)/shard_map/ppermute | solution.py:16
  20.7 10.0 %collective-permute-start.7 = (bf16[64,1024]{1,0:T(8,128)(2,1)S(1)}, bf16[64,1024]{1,0:T(8,128)(2,1)S(1)}, u32[]{:S(2)}, u32[]{:S(2)}) collective-permute-start(bf16[64,1024]{1,0:T(8,128)(2,1)S(1)} %constant_dynamic-update-slice_fusion.refs_4_), channel_id=1, source_target_pairs={{0,24},{1,25},{2,26},{3,27},{4,28},{5,29},{6,30},{7,31},{8,16},{9,... | collective-permute-start | bytes 393224 | tf_op jit(solution)/shard_map/ppermute | solution.py:16
  30.7 5.0 %collective-permute-start.5 = (bf16[64,1024]{1,0:T(8,128)(2,1)S(1)}, bf16[64,1024]{1,0:T(8,128)(2,1)S(1)}, u32[]{:S(2)}, u32[]{:S(2)}) collective-permute-start(bf16[64,1024]{1,0:T(8,128)(2,1)S(1)} %constant_dynamic-update-slice_fusion.refs_4_), channel_id=1, source_target_pairs={{0,8},{1,9},{2,10},{3,11},{4,12},{5,13},{6,14},{7,15},{8,0},{9,1},... | collective-permute-start | bytes 393224 | tf_op jit(solution)/shard_map/ppermute | solution.py:16
  31.4 9.0 %collective-permute-start.9 = (bf16[128,1024]{1,0:T(8,128)(2,1)}, bf16[128,1024]{1,0:T(8,128)(2,1)S(1)}, u32[]{:S(2)}, u32[]{:S(2)}) collective-permute-start(bf16[128,1024]{1,0:T(8,128)(2,1)} %pad_maximum_fusion.1), channel_id=1, source_target_pairs={{0,4},{1,5},{2,6},{3,7},{4,0},{5,1},{6,2},{7,3},{8,12},{9,13},{10,... | collective-permute-start | bytes 786440 | tf_op jit(solution)/shard_map/ppermute | solution.py:16
  33.6 11.1 %collective-permute-start.2 = (bf16[256,1024]{1,0:T(8,128)(2,1)S(1)}, bf16[256,1024]{1,0:T(8,128)(2,1)S(1)}, u32[]{:S(2)}, u32[]{:S(2)}) collective-permute-start(bf16[256,1024]{1,0:T(8,128)(2,1)S(1)} %fusion.7.refs_0_), channel_id=1, source_target_pairs={{0,1},{1,0},{2,3},{3,2},{4,5},{5,4},{6,7},{7,6},{8,9},{9,8},{10,11... | collective-permute-start | bytes 1572872 | tf_op jit(solution)/shard_map/ppermute | solution.py:16
  36.4 8.4 %collective-permute-start.8 = (bf16[128,1024]{1,0:T(8,128)(2,1)}, bf16[128,1024]{1,0:T(8,128)(2,1)S(1)}, u32[]{:S(2)}, u32[]{:S(2)}) collective-permute-start(bf16[128,1024]{1,0:T(8,128)(2,1)} %pad_maximum_fusion), channel_id=1, source_target_pairs={{0,4},{1,5},{2,6},{3,7},{4,0},{5,1},{6,2},{7,3},{8,12},{9,13},{10,... | collective-permute-start | bytes 786440 | tf_op jit(solution)/shard_map/ppermute | solution.py:16
  47.5 10.0 %collective-permute-start.17 = (bf16[128,384]{1,0:T(8,128)(2,1)S(1)}, bf16[128,384]{1,0:T(8,128)(2,1)S(1)}, u32[]{:S(2)}, u32[]{:S(2)}) collective-permute-start(bf16[128,384]{1,0:T(8,128)(2,1)S(1)} %get-tuple-element.19), channel_id=1, source_target_pairs={{0,8},{1,9},{2,10},{3,11},{4,12},{5,13},{6,14},{7,15},{8,0},{9,1},... | collective-permute-start | bytes 294920 | tf_op jit(solution)/shard_map/ppermute | solution.py:16
  50.6 10.5 %collective-permute-start.18 = (bf16[128,384]{1,0:T(8,128)(2,1)S(1)}, bf16[128,384]{1,0:T(8,128)(2,1)S(1)}, u32[]{:S(2)}, u32[]{:S(2)}) collective-permute-start(bf16[128,384]{1,0:T(8,128)(2,1)S(1)} %get-tuple-element.20), channel_id=1, source_target_pairs={{0,16},{1,17},{2,18},{3,19},{4,20},{5,21},{6,22},{7,23},{8,24},{9,... | collective-permute-start | bytes 294920 | tf_op jit(solution)/shard_map/ppermute | solution.py:16
  52.6 8.5 %collective-permute-start.19 = (bf16[128,384]{1,0:T(8,128)(2,1)S(1)}, bf16[128,384]{1,0:T(8,128)(2,1)S(1)}, u32[]{:S(2)}, u32[]{:S(2)}) collective-permute-start(bf16[128,384]{1,0:T(8,128)(2,1)S(1)} %get-tuple-element.21), channel_id=1, source_target_pairs={{0,24},{1,25},{2,26},{3,27},{4,28},{5,29},{6,30},{7,31},{8,16},{9,... | collective-permute-start | bytes 294920 | tf_op jit(solution)/shard_map/ppermute | solution.py:16
  54.4 8.4 %collective-permute-start.11 = (bf16[128,640]{1,0:T(8,128)(2,1)S(1)}, bf16[128,640]{1,0:T(8,128)(2,1)S(1)}, u32[]{:S(2)}, u32[]{:S(2)}) collective-permute-start(bf16[128,640]{1,0:T(8,128)(2,1)S(1)} %get-tuple-element.15), channel_id=1, source_target_pairs={{0,2},{1,3},{2,0},{3,1},{4,6},{5,7},{6,4},{7,5},{8,10},{9,11},{10,... | collective-permute-start | bytes 491528 | tf_op jit(solution)/shard_map/ppermute | solution.py:16
  55.9 8.6 %collective-permute-start.12 = (bf16[128,640]{1,0:T(8,128)(2,1)S(1)}, bf16[128,640]{1,0:T(8,128)(2,1)S(1)}, u32[]{:S(2)}, u32[]{:S(2)}) collective-permute-start(bf16[128,640]{1,0:T(8,128)(2,1)S(1)} %get-tuple-element.16), channel_id=1, source_target_pairs={{0,4},{1,5},{2,6},{3,7},{4,0},{5,1},{6,2},{7,3},{8,12},{9,13},{10,... | collective-permute-start | bytes 491528 | tf_op jit(solution)/shard_map/ppermute | solution.py:16
  57.4 7.9 %collective-permute-start.13 = (bf16[128,640]{1,0:T(8,128)(2,1)S(1)}, bf16[128,640]{1,0:T(8,128)(2,1)S(1)}, u32[]{:S(2)}, u32[]{:S(2)}) collective-permute-start(bf16[128,640]{1,0:T(8,128)(2,1)S(1)} %get-tuple-element.17), channel_id=1, source_target_pairs={{0,6},{1,7},{2,4},{3,5},{4,2},{5,3},{6,0},{7,1},{8,14},{9,15},{10,... | collective-permute-start | bytes 491528 | tf_op jit(solution)/shard_map/ppermute | solution.py:16
  61.1 13.9 %collective-permute-start.10 = (bf16[512,256]{1,0:T(8,128)(2,1)S(1)}, bf16[512,256]{1,0:T(8,128)(2,1)S(1)}, u32[]{:S(2)}, u32[]{:S(2)}) collective-permute-start(bf16[512,256]{1,0:T(8,128)(2,1)S(1)} %get-tuple-element.13), channel_id=1, source_target_pairs={{0,1},{1,0},{2,3},{3,2},{4,5},{5,4},{6,7},{7,6},{8,9},{9,8},{10,11... | collective-permute-start | bytes 786440 | tf_op jit(solution)/shard_map/ppermute | solution.py:16
  61.2 5.4 %collective-permute-start.20 = (bf16[32,384]{1,0:T(8,128)(2,1)S(1)}, bf16[32,384]{1,0:T(8,128)(2,1)S(1)}, u32[]{:S(2)}, u32[]{:S(2)}) collective-permute-start(bf16[32,384]{1,0:T(8,128)(2,1)S(1)} %get-tuple-element.34), channel_id=1, source_target_pairs={{0,2},{1,3},{2,0},{3,1},{4,6},{5,7},{6,4},{7,5},{8,10},{9,11},{10,... | collective-permute-start | bytes 73736 | tf_op jit(solution)/shard_map/ppermute | solution.py:16
  62.7 5.8 %collective-permute-start.21 = (bf16[32,384]{1,0:T(8,128)(2,1)S(1)}, bf16[32,384]{1,0:T(8,128)(2,1)S(1)}, u32[]{:S(2)}, u32[]{:S(2)}) collective-permute-start(bf16[32,384]{1,0:T(8,128)(2,1)S(1)} %get-tuple-element.36), channel_id=1, source_target_pairs={{0,4},{1,5},{2,6},{3,7},{4,0},{5,1},{6,2},{7,3},{8,12},{9,13},{10,... | collective-permute-start | bytes 73736 | tf_op jit(solution)/shard_map/ppermute | solution.py:16
  64.5 5.4 %collective-permute-start.22 = (bf16[32,384]{1,0:T(8,128)(2,1)S(1)}, bf16[32,384]{1,0:T(8,128)(2,1)S(1)}, u32[]{:S(2)}, u32[]{:S(2)}) collective-permute-start(bf16[32,384]{1,0:T(8,128)(2,1)S(1)} %get-tuple-element.35), channel_id=1, source_target_pairs={{0,6},{1,7},{2,4},{3,5},{4,2},{5,3},{6,0},{7,1},{8,14},{9,15},{10,... | collective-permute-start | bytes 73736 | tf_op jit(solution)/shard_map/ppermute | solution.py:16
  65.5 4.5 %collective-permute-start.14 = (bf16[32,640]{1,0:T(8,128)(2,1)S(1)}, bf16[32,640]{1,0:T(8,128)(2,1)S(1)}, u32[]{:S(2)}, u32[]{:S(2)}) collective-permute-start(bf16[32,640]{1,0:T(8,128)(2,1)S(1)} %get-tuple-element.31), channel_id=1, source_target_pairs={{0,8},{1,9},{2,10},{3,11},{4,12},{5,13},{6,14},{7,15},{8,0},{9,1},... | collective-permute-start | bytes 122888 | tf_op jit(solution)/shard_map/ppermute | solution.py:16
  66.5 4.9 %collective-permute-start.15 = (bf16[32,640]{1,0:T(8,128)(2,1)S(1)}, bf16[32,640]{1,0:T(8,128)(2,1)S(1)}, u32[]{:S(2)}, u32[]{:S(2)}) collective-permute-start(bf16[32,640]{1,0:T(8,128)(2,1)S(1)} %get-tuple-element.33), channel_id=1, source_target_pairs={{0,16},{1,17},{2,18},{3,19},{4,20},{5,21},{6,22},{7,23},{8,24},{9,... | collective-permute-start | bytes 122888 | tf_op jit(solution)/shard_map/ppermute | solution.py:16
  68.5 5.8 %collective-permute-start.16 = (bf16[32,640]{1,0:T(8,128)(2,1)S(1)}, bf16[32,640]{1,0:T(8,128)(2,1)S(1)}, u32[]{:S(2)}, u32[]{:S(2)}) collective-permute-start(bf16[32,640]{1,0:T(8,128)(2,1)S(1)} %get-tuple-element.32), channel_id=1, source_target_pairs={{0,24},{1,25},{2,26},{3,27},{4,28},{5,29},{6,30},{7,31},{8,16},{9,... | collective-permute-start | bytes 122888 | tf_op jit(solution)/shard_map/ppermute | solution.py:16

commit v2 on v0

v2 whole, which is shorter than its diff:
```python
import jax
import jax.numpy as jnp
from jax import lax
from jax.experimental import pallas as pl
from jax.experimental.pallas import tpu as pltpu
from jax.sharding import PartitionSpec as P

AXES = ("rows", "blk")
CORE, X, Y, NEAR, FAR = 1, 2, 4, 8, 16
ALONG_Z = (0, NEAR, NEAR ^ FAR, FAR)
F32 = jnp.float32
BF16 = jnp.bfloat16
TURN = (((1,), (1,)), ((), ()))
IN_VMEM = pl.BlockSpec(memory_space=pltpu.VMEM)
IN_SMEM = pl.BlockSpec(memory_space=pltpu.SMEM)
LIMIT = pltpu.CompilerParams(vmem_limit_bytes=24 * 1024 * 1024)
BRIEF = pl.CostEstimate(flops=0, bytes_accessed=0, transcendentals=0)
LONG = pl.CostEstimate(flops=20_000_000_000, bytes_accessed=0, transcendentals=0)


def swap(value, mask, odd_mask=None):
    total = lax.axis_size(AXES)
    masks = (mask, mask if odd_mask is None else odd_mask)
    return lax.ppermute(value, AXES, [(i, i ^ masks[i % 2]) for i in range(total)])


def after(value, *earlier):
    return lax.optimization_barrier((value, *earlier))[0]


def shifted(value, by):
    length = lax.axis_size("blk")
    return lax.ppermute(value, "blk", [(i, (i + by) % length) for i in range(length)])


def layer_body(first, step, agg_own, agg_other, cot_own, cot_other, w, out_own, out_other, grad):
    for at in range(0, grad.shape[0], step):
        src, dst = pl.ds(first + at, step), pl.ds(at, step)
        rows = w[src, :]
        total = None
        for agg, cot, out in ((agg_own, cot_own, out_own), (agg_other, cot_other, out_other)):
            pre = lax.dot_general(rows, agg[...], TURN, preferred_element_type=F32)
            s = jax.nn.sigmoid(pre)
            out[dst, :] = (pre * s).astype(BF16)
            slope = s * (1.0 + pre * (1.0 - s))
            grad_pre = (cot[src, :].astype(F32) * slope).astype(BF16)
            term = jnp.dot(grad_pre, agg[...], preferred_element_type=F32)
            total = term if total is None else total + term
        grad[dst, :] = total.astype(grad.dtype)


def layer(operands, first, count, kind):
    nodes, width = operands[0].shape

    def body(*refs):
        layer_body(first, 128, *refs)

    return pl.pallas_call(
        body,
        out_shape=[
            jax.ShapeDtypeStruct((count, nodes), BF16),
            jax.ShapeDtypeStruct((count, nodes), BF16),
            jax.ShapeDtypeStruct((count, width), kind),
        ],
        in_specs=[IN_VMEM] * 5,
        out_specs=[IN_VMEM] * 3,
        compiler_params=LIMIT,
        cost_estimate=LONG,
        name="layer",
    )(*operands)


def one_hot_rows(me, rows, width):
    slots = width // rows // 2
    owner = jnp.repeat((2 * jnp.arange(slots, dtype=jnp.int32)) ^ me, rows)
    at = owner * rows + jnp.tile(jnp.arange(rows, dtype=jnp.int32), slots)
    return (at[:, None] == jnp.arange(width, dtype=jnp.int32)[None, :]).astype(BF16)


def local_any(features, tiles, tile_cols, tile_count, weight, cotangent):
    total = lax.axis_size(AXES)
    group_len = lax.axis_size("blk")
    position = lax.axis_index("blk")
    me = lax.axis_index(AXES)
    slot_total = tiles.shape[1]
    rows, width = weight.shape
    in_use = jnp.arange(slot_total, dtype=jnp.int32) < tile_count[0]
    columns = tile_cols[0] % group_len

    held = weight
    bit = 2
    while bit < total:
        held = jnp.concatenate([held, swap(held, bit)])
        bit *= 2

    blocks = [(position, features)]
    for offset in range(1, (slot_total - 1) // 2 + 1):
        blocks.append(((position - offset) % group_len, shifted(features, offset)))
        blocks.append(((position + offset) % group_len, shifted(features, -offset)))
    summed = 0.0
    for source, block in blocks:
        match = jnp.logical_and(in_use, columns == source)
        tile = jnp.sum(jnp.where(match[:, None, None], tiles[0], 0), axis=0, dtype=BF16)
        summed = summed + jnp.dot(tile, block, preferred_element_type=F32)
    agg_own = summed.astype(BF16)
    agg_other = swap(agg_own, CORE)

    mine = one_hot_rows(me, rows, width)
    others = one_hot_rows(me ^ CORE, rows, width)
    cot_own = lax.dot_general(mine, cotangent, TURN, preferred_element_type=F32).astype(BF16)
    cot_other = lax.dot_general(others, cotangent, TURN, preferred_element_type=F32).astype(BF16)
    operands = (agg_own, agg_other, cot_own, swap(cot_other, CORE), held)
    out_own, out_other, grad = layer(operands, 0, width // 2, F32)
    bit = total // 2
    while bit > 1:
        n = grad.shape[0] // 2
        grad = grad[:n] + swap(grad[n:].astype(BF16), bit).astype(F32)
        bit //= 2
    out_t = jnp.concatenate([out_own, swap(out_other, CORE)])
    place = jnp.concatenate([mine, others])
    output = lax.dot_general(out_t, place, (((0,), (0,)), ((), ())), preferred_element_type=F32)
    return output.astype(BF16), grad


def hold_body(weight, near_block, out):
    out[...] = weight[...]


def hold(weight, near_block):
    return pl.pallas_call(
        hold_body,
        out_shape=jax.ShapeDtypeStruct(weight.shape, BF16),
        in_specs=[IN_VMEM, pl.BlockSpec(memory_space=pl.ANY)],
        out_specs=IN_VMEM,
        compiler_params=LIMIT,
        cost_estimate=LONG,
        name="hold",
    )(weight, near_block)


def prepare_body(
    me_ref, cols, count, tiles_in, features_in, cotangent_in, near_block,
    partial, tile_x, cot_own, cot_other, place, tiles, features, cotangent, sems,
):
    copies = [
        pltpu.make_async_copy(src, dst, sems.at[k])
        for k, (src, dst) in enumerate(
            ((tiles_in, tiles), (features_in, features), (cotangent_in, cotangent))
        )
    ]
    for copy in copies:
        copy.start()
    me = me_ref[0]
    core = me % 2
    position = me % 4
    width = features.shape[1]
    half = width // 2
    rows = half // 16

    def tile_of(source):
        chosen = jnp.zeros(tiles.shape[2:], BF16)
        for k in range(tiles.shape[1]):
            match = jnp.logical_and(k < count[0], cols[0, k] % 4 == source)
            chosen = jnp.where(match, tiles[0, k], chosen)
        return chosen

    row_at = lax.broadcasted_iota(jnp.int32, (rows, width), 0)
    column_at = lax.broadcasted_iota(jnp.int32, (rows, width), 1)
    for whose in range(2):
        even = core == whose
        first, second = jnp.where(even, X, Y), jnp.where(even, Y, X)
        for slot in range(16):
            mask = (slot // 8) * first + (slot // 4 % 2) * second + ALONG_Z[slot % 4]
            start = (me ^ whose ^ mask) * rows
            at = whose * half + slot * rows
            place[at : at + rows, :] = (column_at == row_at + start).astype(BF16)
    copies[0].wait()
    copies[1].wait()
    tile_x[...] = tile_of(position ^ (X ^ CORE))
    partial[...] = jnp.dot(
        tile_of(position), features[...], preferred_element_type=F32
    ) + jnp.dot(tile_of(position ^ CORE), near_block[...], preferred_element_type=F32)
    copies[2].wait()
    for whose, cot in ((0, cot_own), (1, cot_other)):
        cot[...] = lax.dot_general(
            place[whose * half : (whose + 1) * half, :], cotangent[...], TURN,
            preferred_element_type=F32,
        ).astype(BF16)


def prepare(me, cols, count, tiles, features, cotangent, near_block):
    nodes, width = features.shape
    half = width // 2
    side = tiles.shape[2]
    return pl.pallas_call(
        prepare_body,
        out_shape=[
            jax.ShapeDtypeStruct((nodes, width), F32),
            jax.ShapeDtypeStruct((side, side), BF16),
            jax.ShapeDtypeStruct((half, nodes), BF16),
            jax.ShapeDtypeStruct((half, nodes), BF16),
            jax.ShapeDtypeStruct((width, width), BF16),
        ],
        in_specs=[IN_SMEM] * 3 + [pl.BlockSpec(memory_space=pltpu.HBM)] * 3 + [IN_VMEM],
        out_specs=[IN_VMEM] * 5,
        scratch_shapes=[
            pltpu.VMEM(tiles.shape, BF16),
            pltpu.VMEM(features.shape, BF16),
            pltpu.VMEM(cotangent.shape, BF16),
            pltpu.SemaphoreType.DMA((3,)),
        ],
        compiler_params=LIMIT,
        cost_estimate=BRIEF,
        name="prepare",
    )(me, cols, count, tiles, features, cotangent, near_block)


def aggregate_body(partial, tile, block, out):
    out[...] = (
        partial[...] + jnp.dot(tile[...], block[...], preferred_element_type=F32)
    ).astype(BF16)


def aggreafter(partial, tile, block):
    return pl.pallas_call(
        aggregate_body,
        out_shape=jax.ShapeDtypeStruct(partial.shape, BF16),
        in_specs=[IN_VMEM] * 3,
        out_specs=IN_VMEM,
        compiler_params=LIMIT,
        cost_estimate=LONG,
        name="aggregate",
    )(partial, tile, block)


def order_body(me_ref, *refs):
    pieces, w = refs[:8], refs[8]
    rows = pieces[0].shape[0] // 2
    even = me_ref[0] % 2 == 0
    for first in range(2):
        for second in range(2):
            for z in range(4):
                by_x = pieces[second * 4 + z][first * rows : (first + 1) * rows, :]
                by_y = pieces[first * 4 + z][second * rows : (second + 1) * rows, :]
                at = ((first * 2 + second) * 4 + z) * rows
                w[at : at + rows, :] = jnp.where(even, by_x, by_y)


def into_place_body(*refs):
    parts, place, out = refs[:-2], refs[-2], refs[-1]
    at, total = 0, 0.0
    for part in parts:
        count = part.shape[0]
        total += lax.dot_general(
            part[...], place[at : at + count, :], (((0,), (0,)), ((), ())),
            preferred_element_type=F32,
        )
        at += count
    out[...] = total.astype(out.dtype)


def into_place(parts, place):
    return pl.pallas_call(
        into_place_body,
        out_shape=jax.ShapeDtypeStruct((parts[0].shape[1], place.shape[1]), BF16),
        in_specs=[IN_VMEM] * (len(parts) + 1),
        out_specs=IN_VMEM,
        compiler_params=LIMIT,
        cost_estimate=BRIEF,
        name="into_place",
    )(*parts, place)


def add(kept, first, count, got, kind, cost=BRIEF):
    def body(kept_ref, got_ref, out):
        out[...] = (kept_ref[pl.ds(first, count), :] + got_ref[...].astype(F32)).astype(kind)

    return pl.pallas_call(
        body,
        out_shape=jax.ShapeDtypeStruct((count, kept.shape[1]), kind),
        in_specs=[IN_VMEM] * 2,
        out_specs=IN_VMEM,
        compiler_params=LIMIT,
        cost_estimate=cost,
        name="add",
    )(kept, got)


def in_order(me, pieces):
    rows, width = pieces[0].shape
    return pl.pallas_call(
        order_body,
        out_shape=jax.ShapeDtypeStruct((8 * rows, width), BF16),
        in_specs=[IN_SMEM] + [IN_VMEM] * 8,
        out_specs=IN_VMEM,
        compiler_params=LIMIT,
        cost_estimate=LONG,
        name="in_order",
    )(me, *pieces)


def local_cube(features, tiles, tile_cols, tile_count, weight, cotangent):
    me = lax.axis_index(AXES).astype(jnp.int32).reshape(1)
    rows, width = weight.shape

    near_block = swap(features, CORE)
    weight_x = swap(weight, X)
    x_block = swap(after(features, near_block), X ^ CORE)
    pair = jnp.concatenate([hold(weight, near_block), weight_x])
    far = swap(pair, FAR)
    near = swap(pair, NEAR)
    pieces = {(0, 0): pair, (0, NEAR): near}
    pieces[1, 0] = swap(pair, Y)
    pieces[1, NEAR] = swap(pair, Y ^ NEAR)
    partial, tile_x, cot_own, cot_other, place = prepare(
        after(me, pair), tile_cols, tile_count, tiles, features, cotangent, near_block
    )
    cot_other = swap(cot_other, CORE)
    far = after(far, near, pieces[1, 0])
    pieces[0, FAR] = far
    pieces[1, FAR] = swap(far, Y)
    pieces[0, NEAR ^ FAR] = swap(far, NEAR)
    pieces[1, NEAR ^ FAR] = swap(far, Y ^ NEAR)

    agg_own = aggreafter(partial, tile_x, x_block)
    agg_other = swap(agg_own, CORE)
    w = in_order(me, [pieces[y, z] for y in range(2) for z in ALONG_Z])
    operands = (agg_own, agg_other, cot_own, cot_other, w)

    quarter = width // 8
    own_3, other_3, grad_3 = layer(operands, 3 * quarter, quarter, BF16)
    got_3 = swap(grad_3, X, Y)
    own_2, other_2, grad_2 = layer(operands, 2 * quarter, quarter, BF16)
    got_2 = swap(grad_2, X, Y)
    own_1, other_1, keep = layer(operands, 0, 2 * quarter, F32)

    from_other = swap(jnp.concatenate([other_1, other_2, other_3]), CORE)
    output = into_place([own_1, own_2, own_3, from_other], place)

    send_hi = add(keep, quarter + 2 * rows, 2 * rows, got_3[2 * rows :], BF16)
    got_hi = swap(send_hi, Y, X)
    send_lo = add(keep, quarter, 2 * rows, got_3[: 2 * rows], BF16)
    got_lo = swap(send_lo, Y, X)
    got_hi = after(got_hi, output)
    keep = add(keep, 0, quarter, got_2, F32, LONG)
    high_16 = add(keep, 3 * rows, rows, got_hi[rows:], BF16)
    got_16 = swap(high_16, ALONG_Z[3])
    high_24 = add(keep, 2 * rows, rows, got_hi[:rows], BF16)
    got_24 = swap(high_24, ALONG_Z[2])
    got_lo = after(got_lo, high_24, high_16)
    got_8 = swap(add(keep, rows, rows, got_lo[rows:], BF16, LONG), ALONG_Z[1])
    mine = keep[:rows] + got_lo[:rows].astype(F32)
    return output, mine + sum(v.astype(F32) for v in (got_24, got_16, got_8))


def solution(mesh):
    cube = mesh.shape["rows"] == 8 and mesh.shape["blk"] == 4
    in_specs = (
        P(AXES, None),
        P(AXES, None, None, None),
        P(AXES, None),
        P(AXES),
        P(AXES, None),
        P(AXES, None),
    )
    out_specs = (P(AXES, None), P(AXES, None))
    return jax.shard_map(
        local_cube if cube else local_any,
        mesh=mesh,
        in_specs=in_specs,
        out_specs=out_specs,
        check_vma=False,
    )
```

time: 223 us -> 51.5 us (0.23)
  waiting for transfers between devices: 182 us -> 17.1 us
  starting transfers between devices: 2.51 us -> 23.4 us
  between operations: 16.6 us -> 1.52 us
  matrix products: 10.4 us -> 0 us
  Pallas kernels: 0 us -> 7.66 us
  loops' own time: 5.9 us -> 0 us
  other arithmetic: 4.97 us -> 0.72 us
    reduce_scatter x1 -> x0, waiting for transfers between devices: 140 us -> none  [local(): lax.psum_scatter(lax.dot_general(grad_pre, aggregated, (((0,), (0,)), (()...]
    all_gather x1 -> x0, waiting for transfers between devices: 37.9 us -> none  [local(): lax.all_gather(weight, ('rows', 'blk'), axis=0, tiled=True)]
    ppermute x2 -> x20, starting transfers between devices: 2.43 us -> 23.4 us  [swap(): lax.ppermute(value, AXES, [(i, i ^ masks[i % 2]) for i in range(total)])]
    ppermute x2 -> x20, waiting for transfers between devices: 4.21 us -> 17.1 us  [swap(): lax.ppermute(value, AXES, [(i, i ^ masks[i % 2]) for i in range(total)])]
    dot_general x5 -> x0, matrix products: 10.4 us -> none  [the longest x3 4.05 us: multiply(): return jnp.dot(chosen, rows_there, preferred_element_type=jnp.float32)]
    pallas_call x0 -> x14, Pallas kernels: none -> 7.66 us  [the longest x3 3.09 us: layer(): pl.pallas_call(body, out_shape=[jax.ShapeDtypeStruct((count, nodes), BF16...]
    another operation x3 -> x0, loops' own time: 5.9 us -> none  [apply_panel(): running = running + lax.cond(present, multiply, nothing)]
  transfers between devices with their start and end apart: 4 -> 20, of which waited for: 3 -> 11; matrix products, arithmetic and copies ran while one was open for 4% -> 0% of each run, Pallas kernels for 0% -> 13%
where the time goes in v2:
time: 51.5 us; the launch traced here: 51.3 us
  starting transfers between devices  23.4 us (45%)
  waiting for transfers between devices  17.1 us (33%)
  Pallas kernels  7.66 us (15%)
  between operations  1.52 us (3%)
  local copies, waits for them, and re-layouts  0.89 us (2%)
  other arithmetic  0.72 us (1%)
    ppermute x20, starting transfers between devices, swap(): lax.ppermute(value, AXES, [(i, i ^ masks[i % 2]) for i in range(total)])  23.4 us
    ppermute x20, waiting for transfers between devices, swap(): lax.ppermute(value, AXES, [(i, i ^ masks[i % 2]) for i in range(total)])  17.1 us
    pallas_call x3, Pallas kernels, layer(): pl.pallas_call(body, out_shape=[jax.ShapeDtypeStruct((count, nodes), BF16...  3.09 us
    pallas_call x1, Pallas kernels, prepare(): pl.pallas_call(prepare_body, out_shape=[jax.ShapeDtypeStruct((nodes, widt...  2.39 us
    pallas_call x1, Pallas kernels, into_place(): pl.pallas_call(into_place_body, out_shape=jax.ShapeDtypeStruct((parts[0]....  1.66 us
  transfers between devices with their start and end apart: 20, of which 11 were waited for; matrix products, arithmetic and copies ran while one was open for 0% of the time, Pallas kernels for 13%

profile of v2, /device:TPU:0, one launch (start us, length us, event | category | flops | bytes accessed | tf_op | source)
XLA Modules:
  0.0 51.3 jit_solution(15174553075527527565)
XLA Ops:
  0.7 0.5 %collective-permute-start = (bf16[256,1024]{1,0:T(8,128)(2,1)}, bf16[256,1024]{1,0:T(8,128)(2,1)S(1)}, u32[]{:S(2)}, u32[]{:S(2)}) collective-permute-start(bf16[256,1024]{1,0:T(8,128)(2,1)} %features_in.1), channel_id=1, source_target_pairs={{0,1},{1,0},{2,3},{3,2},{4,5},{5,4},{6,7},{7,6},{8,9},{9,8},{10,11... | collective-permute-start | bytes 1572872 | tf_op jit(solution)/shard_map/ppermute | solution.py:24
  1.2 2.6 %collective-permute-start.1 = (bf16[32,1024]{1,0:T(8,128)(2,1)}, bf16[32,1024]{1,0:T(8,128)(2,1)S(1)}, u32[]{:S(2)}, u32[]{:S(2)}) collective-permute-start(bf16[32,1024]{1,0:T(8,128)(2,1)} %weight.1), channel_id=1, source_target_pairs={{0,2},{1,3},{2,0},{3,1},{4,6},{5,7},{6,4},{7,5},{8,10},{9,11},{10,... | collective-permute-start | bytes 196616 | tf_op jit(solution)/shard_map/ppermute | solution.py:24
  3.8 0.0 collective-permute-done.near_block
  3.8 1.8 %collective-permute-start.2 = (bf16[256,1024]{1,0:T(8,128)(2,1)}, bf16[256,1024]{1,0:T(8,128)(2,1)S(1)}, u32[]{:S(2)}, u32[]{:S(2)}) collective-permute-start(bf16[256,1024]{1,0:T(8,128)(2,1)} %features_in.1), channel_id=1, source_target_pairs={{0,3},{1,2},{2,1},{3,0},{4,7},{5,6},{6,5},{7,4},{8,11},{9,10},{10,... | collective-permute-start | bytes 1572872 | tf_op jit(solution)/shard_map/ppermute | solution.py:24
  5.5 0.8 %copy-done.4 = bf16[32,1024]{1,0:T(8,128)(2,1)S(1)} copy-done((bf16[32,1024]{1,0:T(8,128)(2,1)S(1)}, bf16[32,1024]{1,0:T(8,128)(2,1)}, u32[]{:S(2)}) %copy-start.4) | copy-done | bytes 65560
  6.4 0.3 collective-permute-done.1
  6.7 1.9 %collective-permute-start.7 = (bf16[64,1024]{1,0:T(8,128)(2,1)S(1)}, bf16[64,1024]{1,0:T(8,128)(2,1)S(1)}, u32[]{:S(2)}, u32[]{:S(2)}) collective-permute-start(bf16[64,1024]{1,0:T(8,128)(2,1)S(1)} %pad_maximum_fusion.1.refs_0_), channel_id=1, source_target_pairs={{0,4},{1,5},{2,6},{3,7},{4,0},{5,1},{6,2},{7,3},{8,12},{9,13},{10,... | collective-permute-start | bytes 393224 | tf_op jit(solution)/shard_map/ppermute | solution.py:24
  8.5 2.6 %collective-permute-start.6 = (bf16[64,1024]{1,0:T(8,128)(2,1)S(1)}, bf16[64,1024]{1,0:T(8,128)(2,1)S(1)}, u32[]{:S(2)}, u32[]{:S(2)}) collective-permute-start(bf16[64,1024]{1,0:T(8,128)(2,1)S(1)} %pad_maximum_fusion.1.refs_0_), channel_id=1, source_target_pairs={{0,16},{1,17},{2,18},{3,19},{4,20},{5,21},{6,22},{7,23},{8,24},{9,... | collective-permute-start | bytes 393224 | tf_op jit(solution)/shard_map/ppermute | solution.py:24
  11.1 1.6 %collective-permute-start.5 = (bf16[64,1024]{1,0:T(8,128)(2,1)S(1)}, bf16[64,1024]{1,0:T(8,128)(2,1)S(1)}, u32[]{:S(2)}, u32[]{:S(2)}) collective-permute-start(bf16[64,1024]{1,0:T(8,128)(2,1)S(1)} %pad_maximum_fusion.1.refs_0_), channel_id=1, source_target_pairs={{0,8},{1,9},{2,10},{3,11},{4,12},{5,13},{6,14},{7,15},{8,0},{9,1},... | collective-permute-start | bytes 393224 | tf_op jit(solution)/shard_map/ppermute | solution.py:24
  13.3 0.5 collective-permute-start.9
  13.8 2.4 %prepare.1 = (f32[256,1024]{1,0:T(8,128)S(1)}, bf16[256,256]{1,0:T(8,128)(2,1)S(1)}, bf16[512,256]{1,0:T(8,128)(2,1)S(1)}, bf16[512,256]{1,0:T(8,128)(2,1)S(1)}, bf16[1024,1024]{1,0:T(8,128)(2,1)S(1)}) custom-call(s32[1]{0:T(128)} %bitcast.me_ref, s32[1,3]{1,0:T(1,128)S(1)} %copy-done.3, s32[1]{0:T(128)S(6)} %copy.8.count, ...), custom_call_target="tpu_custom_call" | custom-call | tf_op jit(solution)/shard_map/prepare/pallas_call | solution.py:195
  16.2 0.0 collective-permute-done.7.refs_4_
  16.2 0.1 collective-permute-start.4
  16.3 1.0 %collective-permute-done.6.refs_3_ = bf16[64,1024]{1,0:T(8,128)(2,1)S(1)} collective-permute-done((bf16[64,1024]{1,0:T(8,128)(2,1)S(1)}, bf16[64,1024]{1,0:T(8,128)(2,1)S(1)}, u32[]{:S(2)}, u32[]{:S(2)}) %collective-permute-start.6) | collective-permute-done | bytes 131104 | tf_op jit(solution)/shard_map/ppermute | solution.py:24
  17.3 1.5 %collective-permute-done.5.refs_1_ = bf16[64,1024]{1,0:T(8,128)(2,1)S(1)} collective-permute-done((bf16[64,1024]{1,0:T(8,128)(2,1)S(1)}, bf16[64,1024]{1,0:T(8,128)(2,1)S(1)}, u32[]{:S(2)}, u32[]{:S(2)}) %collective-permute-start.5) | collective-permute-done | bytes 131104 | tf_op jit(solution)/shard_map/ppermute | solution.py:24
  18.8 0.0 collective-permute-start.11
  18.8 3.0 %collective-permute-start.10 = (bf16[64,1024]{1,0:T(8,128)(2,1)S(1)}, bf16[64,1024]{1,0:T(8,128)(2,1)S(1)}, u32[]{:S(2)}, u32[]{:S(2)}) collective-permute-start(bf16[64,1024]{1,0:T(8,128)(2,1)S(1)} %collective-permute-done.6.refs_3_), channel_id=1, source_target_pairs={{0,12},{1,13},{2,14},{3,15},{4,8},{5,9},{6,10},{7,11},{8,4},{9,5},... | collective-permute-start | bytes 393224 | tf_op jit(solution)/shard_map/ppermute | solution.py:24
  21.8 0.0 collective-permute-done.2.block
  21.8 0.5 collective-permute-start.8
  22.3 0.3 aggregate.1.refs_0_
  22.6 0.0 collective-permute-done.9.refs_5_
  22.6 0.1 collective-permute-start.3
  22.7 3.2 %collective-permute-done.11.refs_7_ = bf16[64,1024]{1,0:T(8,128)(2,1)S(1)} collective-permute-done((bf16[64,1024]{1,0:T(8,128)(2,1)S(1)}, bf16[64,1024]{1,0:T(8,128)(2,1)S(1)}, u32[]{:S(2)}, u32[]{:S(2)}) %collective-permute-start.11) | collective-permute-done | bytes 131104 | tf_op jit(solution)/shard_map/ppermute | solution.py:24
  25.9 0.0 collective-permute-done.10.refs_6_
  25.9 0.8 %collective-permute-done.8.refs_2_ = bf16[64,1024]{1,0:T(8,128)(2,1)S(1)} collective-permute-done((bf16[64,1024]{1,0:T(8,128)(2,1)S(1)}, bf16[64,1024]{1,0:T(8,128)(2,1)S(1)}, u32[]{:S(2)}, u32[]{:S(2)}) %collective-permute-start.8) | collective-permute-done | bytes 131104 | tf_op jit(solution)/shard_map/ppermute | solution.py:24
  26.7 0.1 in_order.1.refs_4_
  26.8 0.0 collective-permute-done.4.refs_3_
  26.8 0.0 collective-permute-done.3.refs_1_
  26.8 0.8 %layer.5 = (bf16[128,256]{1,0:T(8,128)(2,1)S(1)}, bf16[128,256]{1,0:T(8,128)(2,1)S(1)}, bf16[128,1024]{1,0:T(8,128)(2,1)S(1)}) custom-call(bf16[256,1024]{1,0:T(8,128)(2,1)S(1)} %aggregate.1.refs_0_, bf16[256,1024]{1,0:T(8,128)(2,1)S(1)} %collective-permute-done.3.refs_1_, bf16[512,256]{1,0:T(8,128)(2,1)S(1)} %get-tuple-element.25.refs_2_, ...), custom_call_target="tpu_custom_call" | custom-call | flops 20000000000 | tf_op jit(solution)/shard_map/layer/pallas_call | solution.py:58
  27.6 1.4 %collective-permute-start.14 = (bf16[128,1024]{1,0:T(8,128)(2,1)S(1)}, bf16[128,1024]{1,0:T(8,128)(2,1)S(1)}, u32[]{:S(2)}, u32[]{:S(2)}) collective-permute-start(bf16[128,1024]{1,0:T(8,128)(2,1)S(1)} %get-tuple-element.37), channel_id=1, source_target_pairs={{0,2},{1,5},{2,0},{3,7},{4,6},{5,1},{6,4},{7,3},{8,10},{9,13},{10,... | collective-permute-start | bytes 786440 | tf_op jit(solution)/shard_map/ppermute | solution.py:24
  29.0 0.8 %layer.4 = (bf16[128,256]{1,0:T(8,128)(2,1)S(1)}, bf16[128,256]{1,0:T(8,128)(2,1)S(1)}, bf16[128,1024]{1,0:T(8,128)(2,1)S(1)}) custom-call(bf16[256,1024]{1,0:T(8,128)(2,1)S(1)} %aggregate.1.refs_0_, bf16[256,1024]{1,0:T(8,128)(2,1)S(1)} %collective-permute-done.3.refs_1_, bf16[512,256]{1,0:T(8,128)(2,1)S(1)} %get-tuple-element.25.refs_2_, ...), custom_call_target="tpu_custom_call" | custom-call | flops 20000000000 | tf_op jit(solution)/shard_map/layer/pallas_call | solution.py:58
  29.8 0.8 %collective-permute-start.13 = (bf16[128,1024]{1,0:T(8,128)(2,1)S(1)}, bf16[128,1024]{1,0:T(8,128)(2,1)S(1)}, u32[]{:S(2)}, u32[]{:S(2)}) collective-permute-start(bf16[128,1024]{1,0:T(8,128)(2,1)S(1)} %get-tuple-element.36), channel_id=1, source_target_pairs={{0,2},{1,5},{2,0},{3,7},{4,6},{5,1},{6,4},{7,3},{8,10},{9,13},{10,... | collective-permute-start | bytes 786440 | tf_op jit(solution)/shard_map/ppermute | solution.py:24
  30.6 1.5 %layer.3 = (bf16[256,256]{1,0:T(8,128)(2,1)S(1)}, bf16[256,256]{1,0:T(8,128)(2,1)S(1)}, f32[256,1024]{1,0:T(8,128)S(1)}) custom-call(bf16[256,1024]{1,0:T(8,128)(2,1)S(1)} %aggregate.1.refs_0_, bf16[256,1024]{1,0:T(8,128)(2,1)S(1)} %collective-permute-done.3.refs_1_, bf16[512,256]{1,0:T(8,128)(2,1)S(1)} %get-tuple-element.25.refs_2_, ...), custom_call_target="tpu_custom_call" | custom-call | flops 20000000000 | tf_op jit(solution)/shard_map/layer/pallas_call | solution.py:58
  32.1 0.1 collective-permute-start.12
  32.2 1.9 %collective-permute-done.14 = bf16[128,1024]{1,0:T(8,128)(2,1)S(1)} collective-permute-done((bf16[128,1024]{1,0:T(8,128)(2,1)S(1)}, bf16[128,1024]{1,0:T(8,128)(2,1)S(1)}, u32[]{:S(2)}, u32[]{:S(2)}) %collective-permute-start.14) | collective-permute-done | bytes 262176 | tf_op jit(solution)/shard_map/ppermute | solution.py:24
  34.2 1.1 %collective-permute-start.15 = (bf16[64,1024]{1,0:T(8,128)(2,1)S(1)}, bf16[64,1024]{1,0:T(8,128)(2,1)S(1)}, u32[]{:S(2)}, u32[]{:S(2)}) collective-permute-start(bf16[64,1024]{1,0:T(8,128)(2,1)S(1)} %add.33), channel_id=1, source_target_pairs={{0,4},{1,3},{2,6},{3,1},{4,0},{5,7},{6,2},{7,5},{8,12},{9,11},{10,... | collective-permute-start | bytes 393224 | tf_op jit(solution)/shard_map/ppermute | solution.py:24
  35.3 1.0 %collective-permute-start.16 = (bf16[64,1024]{1,0:T(8,128)(2,1)S(1)}, bf16[64,1024]{1,0:T(8,128)(2,1)S(1)}, u32[]{:S(2)}, u32[]{:S(2)}) collective-permute-start(bf16[64,1024]{1,0:T(8,128)(2,1)S(1)} %add.34), channel_id=1, source_target_pairs={{0,4},{1,3},{2,6},{3,1},{4,0},{5,7},{6,2},{7,5},{8,12},{9,11},{10,... | collective-permute-start | bytes 393224 | tf_op jit(solution)/shard_map/ppermute | solution.py:24
  36.3 2.0 %collective-permute-done.13.got_ref = bf16[128,1024]{1,0:T(8,128)(2,1)S(1)} collective-permute-done((bf16[128,1024]{1,0:T(8,128)(2,1)S(1)}, bf16[128,1024]{1,0:T(8,128)(2,1)S(1)}, u32[]{:S(2)}, u32[]{:S(2)}) %collective-permute-start.13) | collective-permute-done | bytes 262176 | tf_op jit(solution)/shard_map/ppermute | solution.py:24
  38.3 0.0 collective-permute-done.12.refs_3_
  38.3 1.7 %into_place.1 = bf16[256,1024]{1,0:T(8,128)(2,1)} custom-call(bf16[256,256]{1,0:T(8,128)(2,1)S(1)} %get-tuple-element.28.refs_0_, bf16[128,256]{1,0:T(8,128)(2,1)S(1)} %get-tuple-element.29.refs_1_, bf16[128,256]{1,0:T(8,128)(2,1)S(1)} %get-tuple-element.30.refs_2_, bf16[512,256]{1,0:T(8,128)(2,1)S(1)} %collective-permute-done.12.refs_3_, ...), custom_call_target="tpu_custom_call" | custom-call | tf_op jit(solution)/shard_map/into_place/pallas_call | solution.py:263
  40.0 0.6 %collective-permute-done.16 = bf16[64,1024]{1,0:T(8,128)(2,1)S(1)} collective-permute-done((bf16[64,1024]{1,0:T(8,128)(2,1)S(1)}, bf16[64,1024]{1,0:T(8,128)(2,1)S(1)}, u32[]{:S(2)}, u32[]{:S(2)}) %collective-permute-start.16) | collective-permute-done | bytes 131104 | tf_op jit(solution)/shard_map/ppermute | solution.py:24
  40.7 1.5 %collective-permute-start.19 = (bf16[32,1024]{1,0:T(8,128)(2,1)S(1)}, bf16[32,1024]{1,0:T(8,128)(2,1)S(1)}, u32[]{:S(2)}, u32[]{:S(2)}) collective-permute-start(bf16[32,1024]{1,0:T(8,128)(2,1)S(1)} %add.37), channel_id=1, source_target_pairs={{0,8},{1,9},{2,10},{3,11},{4,12},{5,13},{6,14},{7,15},{8,0},{9,1},... | collective-permute-start | bytes 196616 | tf_op jit(solution)/shard_map/ppermute | solution.py:24
  42.2 2.3 %collective-permute-start.17 = (bf16[32,1024]{1,0:T(8,128)(2,1)S(1)}, bf16[32,1024]{1,0:T(8,128)(2,1)S(1)}, u32[]{:S(2)}, u32[]{:S(2)}) collective-permute-start(bf16[32,1024]{1,0:T(8,128)(2,1)S(1)} %add.35), channel_id=1, source_target_pairs={{0,24},{1,25},{2,26},{3,27},{4,28},{5,29},{6,30},{7,31},{8,16},{9,... | collective-permute-start | bytes 196616 | tf_op jit(solution)/shard_map/ppermute | solution.py:24
  44.5 0.3 collective-permute-start.18
  44.8 0.2 collective-permute-done.19
  45.0 3.4 %collective-permute-done.17 = bf16[32,1024]{1,0:T(8,128)(2,1)S(1)} collective-permute-done((bf16[32,1024]{1,0:T(8,128)(2,1)S(1)}, bf16[32,1024]{1,0:T(8,128)(2,1)S(1)}, u32[]{:S(2)}, u32[]{:S(2)}) %collective-permute-start.17) | collective-permute-done | bytes 65568 | tf_op jit(solution)/shard_map/ppermute | solution.py:24
  48.5 2.2 %collective-permute-done.18 = bf16[32,1024]{1,0:T(8,128)(2,1)S(1)} collective-permute-done((bf16[32,1024]{1,0:T(8,128)(2,1)S(1)}, bf16[32,1024]{1,0:T(8,128)(2,1)S(1)}, u32[]{:S(2)}, u32[]{:S(2)}) %collective-permute-start.18) | collective-permute-done | bytes 65568 | tf_op jit(solution)/shard_map/ppermute | solution.py:24
  50.6 0.7 %fusion = f32[32,1024]{1,0:T(8,128)} fusion(f32[128,1024]{1,0:T(8,128)S(1)} %add.32.kept_ref, bf16[32,1024]{1,0:T(8,128)(2,1)S(1)} %collective-permute-done.19, bf16[32,1024]{1,0:T(8,128)(2,1)S(1)} %collective-permute-done.18, bf16[32,1024]{1,0:T(8,128)(2,1)S(1)} %collective-permute-done.17, bf16[64,1024]{1,0:T(8,128)(2,1)S(1)} %collective-permute-done.15), kind=kLoop, calls=%fused_computation.2 | loop fusion | flops 262144 | bytes 524288 | tf_op jit(solution)/shard_map/add | solution.py:353
  (22 shorter events, 0.2 us)
Async XLA Ops:
  0.6 13.2 %copy-start.1 = (bf16[256,1024]{1,0:T(8,128)(2,1)S(1)}, bf16[256,1024]{1,0:T(8,128)(2,1)}, u32[]{:S(2)}) copy-start(bf16[256,1024]{1,0:T(8,128)(2,1)} %features_in.1) | copy-start | bytes 1572868
  0.6 13.2 %copy-start = (bf16[256,1024]{1,0:T(8,128)(2,1)S(1)}, bf16[256,1024]{1,0:T(8,128)(2,1)}, u32[]{:S(2)}) copy-start(bf16[256,1024]{1,0:T(8,128)(2,1)} %cotangent_in.1) | copy-start | bytes 1572868
  0.7 13.1 %copy-start.3 = (s32[1,3]{1,0:T(1,128)S(1)}, s32[1,3]{1,0:T(1,128)}, u32[]{:S(2)}) copy-start(s32[1,3]{1,0:T(1,128)} %cols.1) | copy-start | bytes 40
  0.7 13.1 %copy-start.2 = (bf16[1,3,256,256]{3,2,1,0:T(8,128)(2,1)S(1)}, bf16[1,3,256,256]{3,2,1,0:T(8,128)(2,1)}, u32[]{:S(2)}) copy-start(bf16[1,3,256,256]{3,2,1,0:T(8,128)(2,1)} %tiles_in.1) | copy-start | bytes 1179652
  0.7 3.1 %collective-permute-start = (bf16[256,1024]{1,0:T(8,128)(2,1)}, bf16[256,1024]{1,0:T(8,128)(2,1)S(1)}, u32[]{:S(2)}, u32[]{:S(2)}) collective-permute-start(bf16[256,1024]{1,0:T(8,128)(2,1)} %features_in.1), channel_id=1, source_target_pairs={{0,1},{1,0},{2,3},{3,2},{4,5},{5,4},{6,7},{7,6},{8,9},{9,8},{10,11... | collective-permute-start | bytes 1572872 | tf_op jit(solution)/shard_map/ppermute | solution.py:24
  1.2 5.5 %collective-permute-start.1 = (bf16[32,1024]{1,0:T(8,128)(2,1)}, bf16[32,1024]{1,0:T(8,128)(2,1)S(1)}, u32[]{:S(2)}, u32[]{:S(2)}) collective-permute-start(bf16[32,1024]{1,0:T(8,128)(2,1)} %weight.1), channel_id=1, source_target_pairs={{0,2},{1,3},{2,0},{3,1},{4,6},{5,7},{6,4},{7,5},{8,10},{9,11},{10,... | collective-permute-start | bytes 196616 | tf_op jit(solution)/shard_map/ppermute | solution.py:24
  3.8 18.0 %collective-permute-start.2 = (bf16[256,1024]{1,0:T(8,128)(2,1)}, bf16[256,1024]{1,0:T(8,128)(2,1)S(1)}, u32[]{:S(2)}, u32[]{:S(2)}) collective-permute-start(bf16[256,1024]{1,0:T(8,128)(2,1)} %features_in.1), channel_id=1, source_target_pairs={{0,3},{1,2},{2,1},{3,0},{4,7},{5,6},{6,5},{7,4},{8,11},{9,10},{10,... | collective-permute-start | bytes 1572872 | tf_op jit(solution)/shard_map/ppermute | solution.py:24
  5.5 0.8 %copy-start.4 = (bf16[32,1024]{1,0:T(8,128)(2,1)S(1)}, bf16[32,1024]{1,0:T(8,128)(2,1)}, u32[]{:S(2)}) copy-start(bf16[32,1024]{1,0:T(8,128)(2,1)} %weight.1) | copy-start | bytes 196612
  6.7 9.5 %collective-permute-start.7 = (bf16[64,1024]{1,0:T(8,128)(2,1)S(1)}, bf16[64,1024]{1,0:T(8,128)(2,1)S(1)}, u32[]{:S(2)}, u32[]{:S(2)}) collective-permute-start(bf16[64,1024]{1,0:T(8,128)(2,1)S(1)} %pad_maximum_fusion.1.refs_0_), channel_id=1, source_target_pairs={{0,4},{1,5},{2,6},{3,7},{4,0},{5,1},{6,2},{7,3},{8,12},{9,13},{10,... | collective-permute-start | bytes 393224 | tf_op jit(solution)/shard_map/ppermute | solution.py:24
  8.5 8.8 %collective-permute-start.6 = (bf16[64,1024]{1,0:T(8,128)(2,1)S(1)}, bf16[64,1024]{1,0:T(8,128)(2,1)S(1)}, u32[]{:S(2)}, u32[]{:S(2)}) collective-permute-start(bf16[64,1024]{1,0:T(8,128)(2,1)S(1)} %pad_maximum_fusion.1.refs_0_), channel_id=1, source_target_pairs={{0,16},{1,17},{2,18},{3,19},{4,20},{5,21},{6,22},{7,23},{8,24},{9,... | collective-permute-start | bytes 393224 | tf_op jit(solution)/shard_map/ppermute | solution.py:24
  11.1 7.7 %collective-permute-start.5 = (bf16[64,1024]{1,0:T(8,128)(2,1)S(1)}, bf16[64,1024]{1,0:T(8,128)(2,1)S(1)}, u32[]{:S(2)}, u32[]{:S(2)}) collective-permute-start(bf16[64,1024]{1,0:T(8,128)(2,1)S(1)} %pad_maximum_fusion.1.refs_0_), channel_id=1, source_target_pairs={{0,8},{1,9},{2,10},{3,11},{4,12},{5,13},{6,14},{7,15},{8,0},{9,1},... | collective-permute-start | bytes 393224 | tf_op jit(solution)/shard_map/ppermute | solution.py:24
  13.3 9.2 %collective-permute-start.9 = (bf16[64,1024]{1,0:T(8,128)(2,1)S(1)}, bf16[64,1024]{1,0:T(8,128)(2,1)S(1)}, u32[]{:S(2)}, u32[]{:S(2)}) collective-permute-start(bf16[64,1024]{1,0:T(8,128)(2,1)S(1)} %pad_maximum_fusion.1.refs_0_), channel_id=1, source_target_pairs={{0,12},{1,13},{2,14},{3,15},{4,8},{5,9},{6,10},{7,11},{8,4},{9,5},... | collective-permute-start | bytes 393224 | tf_op jit(solution)/shard_map/ppermute | solution.py:24
  16.2 10.6 %collective-permute-start.4 = (bf16[512,256]{1,0:T(8,128)(2,1)S(1)}, bf16[512,256]{1,0:T(8,128)(2,1)S(1)}, u32[]{:S(2)}, u32[]{:S(2)}) collective-permute-start(bf16[512,256]{1,0:T(8,128)(2,1)S(1)} %get-tuple-element.26), channel_id=1, source_target_pairs={{0,1},{1,0},{2,3},{3,2},{4,5},{5,4},{6,7},{7,6},{8,9},{9,8},{10,11... | collective-permute-start | bytes 786440 | tf_op jit(solution)/shard_map/ppermute | solution.py:24
  18.8 7.1 %collective-permute-start.11 = (bf16[64,1024]{1,0:T(8,128)(2,1)S(1)}, bf16[64,1024]{1,0:T(8,128)(2,1)S(1)}, u32[]{:S(2)}, u32[]{:S(2)}) collective-permute-start(bf16[64,1024]{1,0:T(8,128)(2,1)S(1)} %collective-permute-done.6.refs_3_), channel_id=1, source_target_pairs={{0,4},{1,5},{2,6},{3,7},{4,0},{5,1},{6,2},{7,3},{8,12},{9,13},{10,... | collective-permute-start | bytes 393224 | tf_op jit(solution)/shard_map/ppermute | solution.py:24
  18.8 7.1 %collective-permute-start.10 = (bf16[64,1024]{1,0:T(8,128)(2,1)S(1)}, bf16[64,1024]{1,0:T(8,128)(2,1)S(1)}, u32[]{:S(2)}, u32[]{:S(2)}) collective-permute-start(bf16[64,1024]{1,0:T(8,128)(2,1)S(1)} %collective-permute-done.6.refs_3_), channel_id=1, source_target_pairs={{0,12},{1,13},{2,14},{3,15},{4,8},{5,9},{6,10},{7,11},{8,4},{9,5},... | collective-permute-start | bytes 393224 | tf_op jit(solution)/shard_map/ppermute | solution.py:24
  21.8 5.0 %collective-permute-start.8 = (bf16[64,1024]{1,0:T(8,128)(2,1)S(1)}, bf16[64,1024]{1,0:T(8,128)(2,1)S(1)}, u32[]{:S(2)}, u32[]{:S(2)}) collective-permute-start(bf16[64,1024]{1,0:T(8,128)(2,1)S(1)} %collective-permute-done.6.refs_3_), channel_id=1, source_target_pairs={{0,8},{1,9},{2,10},{3,11},{4,12},{5,13},{6,14},{7,15},{8,0},{9,1},... | collective-permute-start | bytes 393224 | tf_op jit(solution)/shard_map/ppermute | solution.py:24
  22.6 4.2 %collective-permute-start.3 = (bf16[256,1024]{1,0:T(8,128)(2,1)S(1)}, bf16[256,1024]{1,0:T(8,128)(2,1)S(1)}, u32[]{:S(2)}, u32[]{:S(2)}) collective-permute-start(bf16[256,1024]{1,0:T(8,128)(2,1)S(1)} %aggregate.1.refs_0_), channel_id=1, source_target_pairs={{0,1},{1,0},{2,3},{3,2},{4,5},{5,4},{6,7},{7,6},{8,9},{9,8},{10,11... | collective-permute-start | bytes 1572872 | tf_op jit(solution)/shard_map/ppermute | solution.py:24
  27.6 6.4 %collective-permute-start.14 = (bf16[128,1024]{1,0:T(8,128)(2,1)S(1)}, bf16[128,1024]{1,0:T(8,128)(2,1)S(1)}, u32[]{:S(2)}, u32[]{:S(2)}) collective-permute-start(bf16[128,1024]{1,0:T(8,128)(2,1)S(1)} %get-tuple-element.37), channel_id=1, source_target_pairs={{0,2},{1,5},{2,0},{3,7},{4,6},{5,1},{6,4},{7,3},{8,10},{9,13},{10,... | collective-permute-start | bytes 786440 | tf_op jit(solution)/shard_map/ppermute | solution.py:24
  29.8 8.4 %collective-permute-start.13 = (bf16[128,1024]{1,0:T(8,128)(2,1)S(1)}, bf16[128,1024]{1,0:T(8,128)(2,1)S(1)}, u32[]{:S(2)}, u32[]{:S(2)}) collective-permute-start(bf16[128,1024]{1,0:T(8,128)(2,1)S(1)} %get-tuple-element.36), channel_id=1, source_target_pairs={{0,2},{1,5},{2,0},{3,7},{4,6},{5,1},{6,4},{7,3},{8,10},{9,13},{10,... | collective-permute-start | bytes 786440 | tf_op jit(solution)/shard_map/ppermute | solution.py:24
  32.1 6.2 %collective-permute-start.12 = (bf16[512,256]{1,0:T(8,128)(2,1)S(1)}, bf16[512,256]{1,0:T(8,128)(2,1)S(1)}, u32[]{:S(2)}, u32[]{:S(2)}) collective-permute-start(bf16[512,256]{1,0:T(8,128)(2,1)S(1)} %pad_maximum_fusion), channel_id=1, source_target_pairs={{0,1},{1,0},{2,3},{3,2},{4,5},{5,4},{6,7},{7,6},{8,9},{9,8},{10,11... | collective-permute-start | bytes 786440 | tf_op jit(solution)/shard_map/ppermute | solution.py:24
  34.2 6.5 %collective-permute-start.15 = (bf16[64,1024]{1,0:T(8,128)(2,1)S(1)}, bf16[64,1024]{1,0:T(8,128)(2,1)S(1)}, u32[]{:S(2)}, u32[]{:S(2)}) collective-permute-start(bf16[64,1024]{1,0:T(8,128)(2,1)S(1)} %add.33), channel_id=1, source_target_pairs={{0,4},{1,3},{2,6},{3,1},{4,0},{5,7},{6,2},{7,5},{8,12},{9,11},{10,... | collective-permute-start | bytes 393224 | tf_op jit(solution)/shard_map/ppermute | solution.py:24
  35.3 5.3 %collective-permute-start.16 = (bf16[64,1024]{1,0:T(8,128)(2,1)S(1)}, bf16[64,1024]{1,0:T(8,128)(2,1)S(1)}, u32[]{:S(2)}, u32[]{:S(2)}) collective-permute-start(bf16[64,1024]{1,0:T(8,128)(2,1)S(1)} %add.34), channel_id=1, source_target_pairs={{0,4},{1,3},{2,6},{3,1},{4,0},{5,7},{6,2},{7,5},{8,12},{9,11},{10,... | collective-permute-start | bytes 393224 | tf_op jit(solution)/shard_map/ppermute | solution.py:24
  40.7 4.3 %collective-permute-start.19 = (bf16[32,1024]{1,0:T(8,128)(2,1)S(1)}, bf16[32,1024]{1,0:T(8,128)(2,1)S(1)}, u32[]{:S(2)}, u32[]{:S(2)}) collective-permute-start(bf16[32,1024]{1,0:T(8,128)(2,1)S(1)} %add.37), channel_id=1, source_target_pairs={{0,8},{1,9},{2,10},{3,11},{4,12},{5,13},{6,14},{7,15},{8,0},{9,1},... | collective-permute-start | bytes 196616 | tf_op jit(solution)/shard_map/ppermute | solution.py:24
  42.2 6.2 %collective-permute-start.17 = (bf16[32,1024]{1,0:T(8,128)(2,1)S(1)}, bf16[32,1024]{1,0:T(8,128)(2,1)S(1)}, u32[]{:S(2)}, u32[]{:S(2)}) collective-permute-start(bf16[32,1024]{1,0:T(8,128)(2,1)S(1)} %add.35), channel_id=1, source_target_pairs={{0,24},{1,25},{2,26},{3,27},{4,28},{5,29},{6,30},{7,31},{8,16},{9,... | collective-permute-start | bytes 196616 | tf_op jit(solution)/shard_map/ppermute | solution.py:24
  44.5 6.1 %collective-permute-start.18 = (bf16[32,1024]{1,0:T(8,128)(2,1)S(1)}, bf16[32,1024]{1,0:T(8,128)(2,1)S(1)}, u32[]{:S(2)}, u32[]{:S(2)}) collective-permute-start(bf16[32,1024]{1,0:T(8,128)(2,1)S(1)} %add.36), channel_id=1, source_target_pairs={{0,16},{1,17},{2,18},{3,19},{4,20},{5,21},{6,22},{7,23},{8,24},{9,... | collective-permute-start | bytes 196616 | tf_op jit(solution)/shard_map/ppermute | solution.py:24

commit v3 on v2

--- a/solution.py
+++ b/solution.py
@@ -33,27 +33,27 @@
     return lax.ppermute(value, "blk", [(i, (i + by) % length) for i in range(length)])
 
 
-def layer_body(first, step, agg_own, agg_other, cot_own, cot_other, w, out_own, out_other, grad):
+def layer_body(first, cot_first, step, agg_own, agg_other, cot_own, cot_other, w, out_own, out_other, grad):
     for at in range(0, grad.shape[0], step):
-        src, dst = pl.ds(first + at, step), pl.ds(at, step)
-        rows = w[src, :]
+        dst = pl.ds(at, step)
+        rows = w[pl.ds(first + at, step), :]
         total = None
         for agg, cot, out in ((agg_own, cot_own, out_own), (agg_other, cot_other, out_other)):
             pre = lax.dot_general(rows, agg[...], TURN, preferred_element_type=F32)
             s = jax.nn.sigmoid(pre)
             out[dst, :] = (pre * s).astype(BF16)
             slope = s * (1.0 + pre * (1.0 - s))
-            grad_pre = (cot[src, :].astype(F32) * slope).astype(BF16)
+            grad_pre = (cot[pl.ds(cot_first + at, step), :].astype(F32) * slope).astype(BF16)
             term = jnp.dot(grad_pre, agg[...], preferred_element_type=F32)
             total = term if total is None else total + term
         grad[dst, :] = total.astype(grad.dtype)
 
 
-def layer(operands, first, count, kind):
+def layer(operands, first, cot_first, count, kind):
     nodes, width = operands[0].shape
 
     def body(*refs):
-        layer_body(first, 128, *refs)
+        layer_body(first, cot_first, 128, *refs)
 
     return pl.pallas_call(
         body,
@@ -110,7 +110,7 @@
     cot_own = lax.dot_general(mine, cotangent, TURN, preferred_element_type=F32).astype(BF16)
     cot_other = lax.dot_general(others, cotangent, TURN, preferred_element_type=F32).astype(BF16)
     operands = (agg_own, agg_other, cot_own, swap(cot_other, CORE), held)
-    out_own, out_other, grad = layer(operands, 0, width // 2, F32)
+    out_own, out_other, grad = layer(operands, 0, 0, width // 2, F32)
     bit = total // 2
     while bit > 1:
         n = grad.shape[0] // 2
@@ -170,7 +170,8 @@
         even = core == whose
         first, second = jnp.where(even, X, Y), jnp.where(even, Y, X)
         for slot in range(16):
-            mask = (slot // 8) * first + (slot // 4 % 2) * second + ALONG_Z[slot % 4]
+            z = ALONG_Z[slot // 8 * 2 + slot % 2]
+            mask = (slot // 4 % 2) * first + (slot // 2 % 2) * second + z
             start = (me ^ whose ^ mask) * rows
             at = whose * half + slot * rows
             place[at : at + rows, :] = (column_at == row_at + start).astype(BF16)
@@ -221,29 +222,42 @@
     ).astype(BF16)
 
 
-def aggreafter(partial, tile, block):
+def aggregate(partial, tile, block):
     return pl.pallas_call(
         aggregate_body,
         out_shape=jax.ShapeDtypeStruct(partial.shape, BF16),
         in_specs=[IN_VMEM] * 3,
         out_specs=IN_VMEM,
         compiler_params=LIMIT,
-        cost_estimate=LONG,
+        cost_estimate=BRIEF,
         name="aggregate",
     )(partial, tile, block)
 
 
 def order_body(me_ref, *refs):
-    pieces, w = refs[:8], refs[8]
+    pieces, w = refs[:4], refs[4]
     rows = pieces[0].shape[0] // 2
     even = me_ref[0] % 2 == 0
     for first in range(2):
         for second in range(2):
-            for z in range(4):
-                by_x = pieces[second * 4 + z][first * rows : (first + 1) * rows, :]
-                by_y = pieces[first * 4 + z][second * rows : (second + 1) * rows, :]
-                at = ((first * 2 + second) * 4 + z) * rows
+            for z in range(2):
+                by_x = pieces[second * 2 + z][first * rows : (first + 1) * rows, :]
+                by_y = pieces[first * 2 + z][second * rows : (second + 1) * rows, :]
+                at = ((first * 2 + second) * 2 + z) * rows
                 w[at : at + rows, :] = jnp.where(even, by_x, by_y)
+
+
+def in_order(me, pieces):
+    rows, width = pieces[0].shape
+    return pl.pallas_call(
+        order_body,
+        out_shape=jax.ShapeDtypeStruct((4 * rows, width), BF16),
+        in_specs=[IN_SMEM] + [IN_VMEM] * 4,
+        out_specs=IN_VMEM,
+        compiler_params=LIMIT,
+        cost_estimate=LONG,
+        name="in_order",
+    )(me, *pieces)
 
 
 def into_place_body(*refs):
@@ -284,19 +298,6 @@
         cost_estimate=cost,
         name="add",
     )(kept, got)
-
-
-def in_order(me, pieces):
-    rows, width = pieces[0].shape
-    return pl.pallas_call(
-        order_body,
-        out_shape=jax.ShapeDtypeStruct((8 * rows, width), BF16),
-        in_specs=[IN_SMEM] + [IN_VMEM] * 8,
-        out_specs=IN_VMEM,
-        compiler_params=LIMIT,
-        cost_estimate=LONG,
-        name="in_order",
-    )(me, *pieces)
 
 
 def local_cube(features, tiles, tile_cols, tile_count, weight, cotangent):
@@ -315,41 +316,45 @@
     partial, tile_x, cot_own, cot_other, place = prepare(
         after(me, pair), tile_cols, tile_count, tiles, features, cotangent, near_block
     )
-    cot_other = swap(cot_other, CORE)
+    cot_other = swap(after(cot_other, x_block), CORE)
     far = after(far, near, pieces[1, 0])
     pieces[0, FAR] = far
     pieces[1, FAR] = swap(far, Y)
     pieces[0, NEAR ^ FAR] = swap(far, NEAR)
     pieces[1, NEAR ^ FAR] = swap(far, Y ^ NEAR)
 
-    agg_own = aggreafter(partial, tile_x, x_block)
+    agg_own = aggregate(partial, tile_x, x_block)
     agg_other = swap(agg_own, CORE)
-    w = in_order(me, [pieces[y, z] for y in range(2) for z in ALONG_Z])
-    operands = (agg_own, agg_other, cot_own, cot_other, w)
-
-    quarter = width // 8
-    own_3, other_3, grad_3 = layer(operands, 3 * quarter, quarter, BF16)
-    got_3 = swap(grad_3, X, Y)
-    own_2, other_2, grad_2 = layer(operands, 2 * quarter, quarter, BF16)
-    got_2 = swap(grad_2, X, Y)
-    own_1, other_1, keep = layer(operands, 0, 2 * quarter, F32)
-
-    from_other = swap(jnp.concatenate([other_1, other_2, other_3]), CORE)
-    output = into_place([own_1, own_2, own_3, from_other], place)
-
-    send_hi = add(keep, quarter + 2 * rows, 2 * rows, got_3[2 * rows :], BF16)
-    got_hi = swap(send_hi, Y, X)
-    send_lo = add(keep, quarter, 2 * rows, got_3[: 2 * rows], BF16)
-    got_lo = swap(send_lo, Y, X)
-    got_hi = after(got_hi, output)
-    keep = add(keep, 0, quarter, got_2, F32, LONG)
-    high_16 = add(keep, 3 * rows, rows, got_hi[rows:], BF16)
-    got_16 = swap(high_16, ALONG_Z[3])
-    high_24 = add(keep, 2 * rows, rows, got_hi[:rows], BF16)
-    got_24 = swap(high_24, ALONG_Z[2])
-    got_lo = after(got_lo, high_24, high_16)
-    got_8 = swap(add(keep, rows, rows, got_lo[rows:], BF16, LONG), ALONG_Z[1])
-    mine = keep[:rows] + got_lo[:rows].astype(F32)
+    order_e = [pieces[y, z] for y in range(2) for z in ALONG_Z[:2]]
+    order_e[0] = after(order_e[0], agg_own)
+    w_e = in_order(me, order_e)
+    operands = [agg_own, agg_other, cot_own, cot_other]
+    own_e1, other_e1, send_e = layer(operands + [w_e], 4 * rows, 4 * rows, 4 * rows, BF16)
+    got_e = swap(send_e, X, Y)
+    order_l = [pieces[y, z] for y in range(2) for z in ALONG_Z[2:]]
+    order_l[0] = after(order_l[0], send_e)
+    w_l = in_order(me, order_l)
+    own_l1, other_l1, send_l = layer(operands + [w_l], 4 * rows, 12 * rows, 4 * rows, BF16)
+    got_l = swap(send_l, X, Y)
+    w_e = after(w_e, send_l)
+    own_e0, other_e0, keep_e = layer(operands + [w_e], 0, 0, 4 * rows, F32)
+    own_l0, other_l0, keep_l = layer(operands + [w_l], 0, 8 * rows, 4 * rows, F32)
+
+    sums = []
+    for got, keep in ((got_e, keep_e), (got_l, keep_l)):
+        send = add(keep, 2 * rows, 2 * rows, got[2 * rows :], BF16)
+        sums.append((swap(send, Y, X), add(keep, 0, 2 * rows, got[: 2 * rows], F32)))
+
+    others = jnp.concatenate([other_e0, other_e1, other_l0, other_l1])
+    from_other = swap(others, CORE)
+    output = into_place([own_e0, own_e1, own_l0, own_l1, from_other], place)
+
+    (got_e, keep_e), (got_l, keep_l) = sums
+    got_8 = swap(add(keep_e, rows, rows, got_e[rows:], BF16), ALONG_Z[1])
+    got_l = after(got_l, output)
+    got_16 = swap(add(keep_l, rows, rows, got_l[rows:], BF16), ALONG_Z[3])
+    got_24 = swap(add(keep_l, 0, rows, got_l[:rows], BF16), ALONG_Z[2])
+    mine = keep_e[:rows] + got_e[:rows].astype(F32)
     return output, mine + sum(v.astype(F32) for v in (got_24, got_16, got_8))
 
 

time: 51.5 us -> 48.9 us (0.950)
  waiting for transfers between devices: 17.1 us -> 14.2 us
    ppermute x20, waiting for transfers between devices: 17.1 us -> 14.2 us  [swap(): lax.ppermute(value, AXES, [(i, i ^ masks[i % 2]) for i in range(total)])]
    pallas_call x3 -> x4, Pallas kernels: 3.09 us -> 3.33 us  [layer(): pl.pallas_call(body, out_shape=[jax.ShapeDtypeStruct((count, nodes), BF16...]
  transfers between devices with their start and end apart: 20 -> 20, of which waited for: 11 -> 8; matrix products, arithmetic and copies ran while one was open for 0% -> 0% of each run, Pallas kernels for 13% -> 17%
where the time goes in v3:
time: 48.9 us; the launch traced here: 48.7 us
  starting transfers between devices  23.3 us (48%)
  waiting for transfers between devices  14.2 us (29%)
  Pallas kernels  8.07 us (17%)
  between operations  1.54 us (3%)
  local copies, waits for them, and re-layouts  0.91 us (2%)
  other arithmetic  0.72 us (1%)
    ppermute x20, starting transfers between devices, swap(): lax.ppermute(value, AXES, [(i, i ^ masks[i % 2]) for i in range(total)])  23.3 us
    ppermute x20, waiting for transfers between devices, swap(): lax.ppermute(value, AXES, [(i, i ^ masks[i % 2]) for i in range(total)])  14.2 us
    pallas_call x4, Pallas kernels, layer(): pl.pallas_call(body, out_shape=[jax.ShapeDtypeStruct((count, nodes), BF16...  3.33 us
    pallas_call x1, Pallas kernels, prepare(): pl.pallas_call(prepare_body, out_shape=[jax.ShapeDtypeStruct((nodes, widt...  2.4 us
    pallas_call x1, Pallas kernels, into_place(): pl.pallas_call(into_place_body, out_shape=jax.ShapeDtypeStruct((parts[0]....  1.79 us
  transfers between devices with their start and end apart: 20, of which 8 were waited for; matrix products, arithmetic and copies ran while one was open for 0% of the time, Pallas kernels for 17%

profile of v3, /device:TPU:0, one launch (start us, length us, event | category | flops | bytes accessed | tf_op | source)
XLA Modules:
  0.0 48.7 jit_solution(7412036218447270930)
XLA Ops:
  0.7 0.5 %collective-permute-start = (bf16[256,1024]{1,0:T(8,128)(2,1)}, bf16[256,1024]{1,0:T(8,128)(2,1)S(1)}, u32[]{:S(2)}, u32[]{:S(2)}) collective-permute-start(bf16[256,1024]{1,0:T(8,128)(2,1)} %features_in.1), channel_id=1, source_target_pairs={{0,1},{1,0},{2,3},{3,2},{4,5},{5,4},{6,7},{7,6},{8,9},{9,8},{10,11... | collective-permute-start | bytes 1572872 | tf_op jit(solution)/shard_map/ppermute | solution.py:24
  1.2 2.6 %collective-permute-start.1 = (bf16[32,1024]{1,0:T(8,128)(2,1)}, bf16[32,1024]{1,0:T(8,128)(2,1)S(1)}, u32[]{:S(2)}, u32[]{:S(2)}) collective-permute-start(bf16[32,1024]{1,0:T(8,128)(2,1)} %weight.1), channel_id=1, source_target_pairs={{0,2},{1,3},{2,0},{3,1},{4,6},{5,7},{6,4},{7,5},{8,10},{9,11},{10,... | collective-permute-start | bytes 196616 | tf_op jit(solution)/shard_map/ppermute | solution.py:24
  3.8 0.0 collective-permute-done.near_block
  3.8 1.8 %collective-permute-start.2 = (bf16[256,1024]{1,0:T(8,128)(2,1)}, bf16[256,1024]{1,0:T(8,128)(2,1)S(1)}, u32[]{:S(2)}, u32[]{:S(2)}) collective-permute-start(bf16[256,1024]{1,0:T(8,128)(2,1)} %features_in.1), channel_id=1, source_target_pairs={{0,3},{1,2},{2,1},{3,0},{4,7},{5,6},{6,5},{7,4},{8,11},{9,10},{10,... | collective-permute-start | bytes 1572872 | tf_op jit(solution)/shard_map/ppermute | solution.py:24
  5.5 0.8 %copy-done.4 = bf16[32,1024]{1,0:T(8,128)(2,1)S(1)} copy-done((bf16[32,1024]{1,0:T(8,128)(2,1)S(1)}, bf16[32,1024]{1,0:T(8,128)(2,1)}, u32[]{:S(2)}) %copy-start.4) | copy-done | bytes 65560
  6.4 0.3 collective-permute-done.1
  6.7 2.9 %collective-permute-start.8 = (bf16[64,1024]{1,0:T(8,128)(2,1)S(1)}, bf16[64,1024]{1,0:T(8,128)(2,1)S(1)}, u32[]{:S(2)}, u32[]{:S(2)}) collective-permute-start(bf16[64,1024]{1,0:T(8,128)(2,1)S(1)} %pad_maximum_fusion.1.refs_0_), channel_id=1, source_target_pairs={{0,16},{1,17},{2,18},{3,19},{4,20},{5,21},{6,22},{7,23},{8,24},{9,... | collective-permute-start | bytes 393224 | tf_op jit(solution)/shard_map/ppermute | solution.py:24
  9.6 1.5 %collective-permute-start.6 = (bf16[64,1024]{1,0:T(8,128)(2,1)S(1)}, bf16[64,1024]{1,0:T(8,128)(2,1)S(1)}, u32[]{:S(2)}, u32[]{:S(2)}) collective-permute-start(bf16[64,1024]{1,0:T(8,128)(2,1)S(1)} %pad_maximum_fusion.1.refs_0_), channel_id=1, source_target_pairs={{0,4},{1,5},{2,6},{3,7},{4,0},{5,1},{6,2},{7,3},{8,12},{9,13},{10,... | collective-permute-start | bytes 393224 | tf_op jit(solution)/shard_map/ppermute | solution.py:24
  11.1 1.6 %collective-permute-start.5 = (bf16[64,1024]{1,0:T(8,128)(2,1)S(1)}, bf16[64,1024]{1,0:T(8,128)(2,1)S(1)}, u32[]{:S(2)}, u32[]{:S(2)}) collective-permute-start(bf16[64,1024]{1,0:T(8,128)(2,1)S(1)} %pad_maximum_fusion.1.refs_0_), channel_id=1, source_target_pairs={{0,8},{1,9},{2,10},{3,11},{4,12},{5,13},{6,14},{7,15},{8,0},{9,1},... | collective-permute-start | bytes 393224 | tf_op jit(solution)/shard_map/ppermute | solution.py:24
  12.7 0.4 collective-permute-start.7
  13.8 2.4 %prepare.1 = (f32[256,1024]{1,0:T(8,128)S(1)}, bf16[256,256]{1,0:T(8,128)(2,1)S(1)}, bf16[512,256]{1,0:T(8,128)(2,1)S(1)}, bf16[512,256]{1,0:T(8,128)(2,1)S(1)}, bf16[1024,1024]{1,0:T(8,128)(2,1)S(1)}) custom-call(s32[1]{0:T(128)} %bitcast.me_ref, s32[1,3]{1,0:T(1,128)S(1)} %copy-done.3, s32[1]{0:T(128)S(6)} %copy.8.count, ...), custom_call_target="tpu_custom_call" | custom-call | tf_op jit(solution)/shard_map/prepare/pallas_call | solution.py:196
  16.2 0.0 collective-permute-done.8.refs_1_
  16.2 0.0 collective-permute-done.6.refs_2_
  16.2 2.3 %collective-permute-done.5.refs_1_ = bf16[64,1024]{1,0:T(8,128)(2,1)S(1)} collective-permute-done((bf16[64,1024]{1,0:T(8,128)(2,1)S(1)}, bf16[64,1024]{1,0:T(8,128)(2,1)S(1)}, u32[]{:S(2)}, u32[]{:S(2)}) %collective-permute-start.5) | collective-permute-done | bytes 131104 | tf_op jit(solution)/shard_map/ppermute | solution.py:24
  18.5 0.7 %collective-permute-start.11 = (bf16[64,1024]{1,0:T(8,128)(2,1)S(1)}, bf16[64,1024]{1,0:T(8,128)(2,1)S(1)}, u32[]{:S(2)}, u32[]{:S(2)}) collective-permute-start(bf16[64,1024]{1,0:T(8,128)(2,1)S(1)} %collective-permute-done.8.refs_1_), channel_id=1, source_target_pairs={{0,4},{1,5},{2,6},{3,7},{4,0},{5,1},{6,2},{7,3},{8,12},{9,13},{10,... | collective-permute-start | bytes 393224 | tf_op jit(solution)/shard_map/ppermute | solution.py:24
  19.2 1.4 %collective-permute-start.10 = (bf16[64,1024]{1,0:T(8,128)(2,1)S(1)}, bf16[64,1024]{1,0:T(8,128)(2,1)S(1)}, u32[]{:S(2)}, u32[]{:S(2)}) collective-permute-start(bf16[64,1024]{1,0:T(8,128)(2,1)S(1)} %collective-permute-done.8.refs_1_), channel_id=1, source_target_pairs={{0,12},{1,13},{2,14},{3,15},{4,8},{5,9},{6,10},{7,11},{8,4},{9,5},... | collective-permute-start | bytes 393224 | tf_op jit(solution)/shard_map/ppermute | solution.py:24
  20.6 1.4 %collective-permute-start.9 = (bf16[64,1024]{1,0:T(8,128)(2,1)S(1)}, bf16[64,1024]{1,0:T(8,128)(2,1)S(1)}, u32[]{:S(2)}, u32[]{:S(2)}) collective-permute-start(bf16[64,1024]{1,0:T(8,128)(2,1)S(1)} %collective-permute-done.8.refs_1_), channel_id=1, source_target_pairs={{0,8},{1,9},{2,10},{3,11},{4,12},{5,13},{6,14},{7,15},{8,0},{9,1},... | collective-permute-start | bytes 393224 | tf_op jit(solution)/shard_map/ppermute | solution.py:24
  22.0 0.0 collective-permute-done.2.block
  22.0 0.3 aggregate.1.refs_0_
  22.3 0.1 collective-permute-start.3
  22.4 0.0 collective-permute-done.7.refs_3_
  22.4 0.5 %collective-permute-start.4 = (bf16[512,256]{1,0:T(8,128)(2,1)S(1)}, bf16[512,256]{1,0:T(8,128)(2,1)S(1)}, u32[]{:S(2)}, u32[]{:S(2)}) collective-permute-start(bf16[512,256]{1,0:T(8,128)(2,1)S(1)} %get-tuple-element.33), channel_id=1, source_target_pairs={{0,1},{1,0},{2,3},{3,2},{4,5},{5,4},{6,7},{7,6},{8,9},{9,8},{10,11... | collective-permute-start | bytes 786440 | tf_op jit(solution)/shard_map/ppermute | solution.py:24
  22.9 1.7 %collective-permute-done.4.refs_3_ = bf16[512,256]{1,0:T(8,128)(2,1)S(1)} collective-permute-done((bf16[512,256]{1,0:T(8,128)(2,1)S(1)}, bf16[512,256]{1,0:T(8,128)(2,1)S(1)}, u32[]{:S(2)}, u32[]{:S(2)}) %collective-permute-start.4) | collective-permute-done | bytes 262176 | tf_op jit(solution)/shard_map/ppermute | solution.py:24
  24.7 0.0 collective-permute-done.3.refs_1_
  24.7 0.8 %layer.4 = (bf16[128,256]{1,0:T(8,128)(2,1)S(1)}, bf16[128,256]{1,0:T(8,128)(2,1)S(1)}, bf16[128,1024]{1,0:T(8,128)(2,1)S(1)}) custom-call(bf16[256,1024]{1,0:T(8,128)(2,1)S(1)} %aggregate.1.refs_0_, bf16[256,1024]{1,0:T(8,128)(2,1)S(1)} %collective-permute-done.3.refs_1_, bf16[512,256]{1,0:T(8,128)(2,1)S(1)} %get-tuple-element.31.refs_2_, ...), custom_call_target="tpu_custom_call" | custom-call | flops 20000000000 | tf_op jit(solution)/shard_map/layer/pallas_call | solution.py:58
  25.5 1.4 %collective-permute-start.13 = (bf16[128,1024]{1,0:T(8,128)(2,1)S(1)}, bf16[128,1024]{1,0:T(8,128)(2,1)S(1)}, u32[]{:S(2)}, u32[]{:S(2)}) collective-permute-start(bf16[128,1024]{1,0:T(8,128)(2,1)S(1)} %get-tuple-element.36), channel_id=1, source_target_pairs={{0,2},{1,5},{2,0},{3,7},{4,6},{5,1},{6,4},{7,3},{8,10},{9,13},{10,... | collective-permute-start | bytes 786440 | tf_op jit(solution)/shard_map/ppermute | solution.py:24
  26.9 0.0 collective-permute-done.9.refs_0_
  26.9 0.0 collective-permute-done.11.refs_3_
  26.9 0.0 collective-permute-done.10.refs_2_
  26.9 0.8 %layer.5 = (bf16[128,256]{1,0:T(8,128)(2,1)S(1)}, bf16[128,256]{1,0:T(8,128)(2,1)S(1)}, bf16[128,1024]{1,0:T(8,128)(2,1)S(1)}) custom-call(bf16[256,1024]{1,0:T(8,128)(2,1)S(1)} %aggregate.1.refs_0_, bf16[256,1024]{1,0:T(8,128)(2,1)S(1)} %collective-permute-done.3.refs_1_, bf16[512,256]{1,0:T(8,128)(2,1)S(1)} %get-tuple-element.31.refs_2_, ...), custom_call_target="tpu_custom_call" | custom-call | flops 20000000000 | tf_op jit(solution)/shard_map/layer/pallas_call | solution.py:58
  27.8 0.9 %collective-permute-start.15 = (bf16[128,1024]{1,0:T(8,128)(2,1)S(1)}, bf16[128,1024]{1,0:T(8,128)(2,1)S(1)}, u32[]{:S(2)}, u32[]{:S(2)}) collective-permute-start(bf16[128,1024]{1,0:T(8,128)(2,1)S(1)} %get-tuple-element.38), channel_id=1, source_target_pairs={{0,2},{1,5},{2,0},{3,7},{4,6},{5,1},{6,4},{7,3},{8,10},{9,13},{10,... | collective-permute-start | bytes 786440 | tf_op jit(solution)/shard_map/ppermute | solution.py:24
  28.6 0.8 %layer.7 = (bf16[128,256]{1,0:T(8,128)(2,1)S(1)}, bf16[128,256]{1,0:T(8,128)(2,1)S(1)}, f32[128,1024]{1,0:T(8,128)S(1)}) custom-call(bf16[256,1024]{1,0:T(8,128)(2,1)S(1)} %aggregate.1.refs_0_, bf16[256,1024]{1,0:T(8,128)(2,1)S(1)} %collective-permute-done.3.refs_1_, bf16[512,256]{1,0:T(8,128)(2,1)S(1)} %get-tuple-element.31.refs_2_, ...), custom_call_target="tpu_custom_call" | custom-call | flops 20000000000 | tf_op jit(solution)/shard_map/layer/pallas_call | solution.py:58
  29.5 0.8 %layer.6 = (bf16[128,256]{1,0:T(8,128)(2,1)S(1)}, bf16[128,256]{1,0:T(8,128)(2,1)S(1)}, f32[128,1024]{1,0:T(8,128)S(1)}) custom-call(bf16[256,1024]{1,0:T(8,128)(2,1)S(1)} %aggregate.1.refs_0_, bf16[256,1024]{1,0:T(8,128)(2,1)S(1)} %collective-permute-done.3.refs_1_, bf16[512,256]{1,0:T(8,128)(2,1)S(1)} %get-tuple-element.31.refs_2_, ...), custom_call_target="tpu_custom_call" | custom-call | flops 20000000000 | tf_op jit(solution)/shard_map/layer/pallas_call | solution.py:58
  30.3 0.1 collective-permute-start.12
  30.4 1.5 %collective-permute-done.13 = bf16[128,1024]{1,0:T(8,128)(2,1)S(1)} collective-permute-done((bf16[128,1024]{1,0:T(8,128)(2,1)S(1)}, bf16[128,1024]{1,0:T(8,128)(2,1)S(1)}, u32[]{:S(2)}, u32[]{:S(2)}) %collective-permute-start.13) | collective-permute-done | bytes 262176 | tf_op jit(solution)/shard_map/ppermute | solution.py:24
  32.0 0.7 %collective-permute-start.14 = (bf16[64,1024]{1,0:T(8,128)(2,1)S(1)}, bf16[64,1024]{1,0:T(8,128)(2,1)S(1)}, u32[]{:S(2)}, u32[]{:S(2)}) collective-permute-start(bf16[64,1024]{1,0:T(8,128)(2,1)S(1)} %add.34), channel_id=1, source_target_pairs={{0,4},{1,3},{2,6},{3,1},{4,0},{5,7},{6,2},{7,5},{8,12},{9,11},{10,... | collective-permute-start | bytes 393224 | tf_op jit(solution)/shard_map/ppermute | solution.py:24
  32.7 2.8 %collective-permute-done.15 = bf16[128,1024]{1,0:T(8,128)(2,1)S(1)} collective-permute-done((bf16[128,1024]{1,0:T(8,128)(2,1)S(1)}, bf16[128,1024]{1,0:T(8,128)(2,1)S(1)}, u32[]{:S(2)}, u32[]{:S(2)}) %collective-permute-start.15) | collective-permute-done | bytes 262176 | tf_op jit(solution)/shard_map/ppermute | solution.py:24
  35.6 0.7 %collective-permute-start.16 = (bf16[64,1024]{1,0:T(8,128)(2,1)S(1)}, bf16[64,1024]{1,0:T(8,128)(2,1)S(1)}, u32[]{:S(2)}, u32[]{:S(2)}) collective-permute-start(bf16[64,1024]{1,0:T(8,128)(2,1)S(1)} %add.36), channel_id=1, source_target_pairs={{0,4},{1,3},{2,6},{3,1},{4,0},{5,7},{6,2},{7,5},{8,12},{9,11},{10,... | collective-permute-start | bytes 393224 | tf_op jit(solution)/shard_map/ppermute | solution.py:24
  36.4 0.0 collective-permute-done.12.refs_4_
  36.4 1.8 %into_place.1 = bf16[256,1024]{1,0:T(8,128)(2,1)} custom-call(bf16[128,256]{1,0:T(8,128)(2,1)S(1)} %get-tuple-element.40.refs_0_, bf16[128,256]{1,0:T(8,128)(2,1)S(1)} %get-tuple-element.41.refs_1_, bf16[128,256]{1,0:T(8,128)(2,1)S(1)} %get-tuple-element.42.refs_2_, bf16[128,256]{1,0:T(8,128)(2,1)S(1)} %get-tuple-element.43.refs_3_, ...), custom_call_target="tpu_custom_call" | custom-call | tf_op jit(solution)/shard_map/into_place/pallas_call | solution.py:277
  38.2 0.0 collective-permute-done.14
  38.2 1.2 %collective-permute-start.19 = (bf16[32,1024]{1,0:T(8,128)(2,1)S(1)}, bf16[32,1024]{1,0:T(8,128)(2,1)S(1)}, u32[]{:S(2)}, u32[]{:S(2)}) collective-permute-start(bf16[32,1024]{1,0:T(8,128)(2,1)S(1)} %add.39), channel_id=1, source_target_pairs={{0,8},{1,9},{2,10},{3,11},{4,12},{5,13},{6,14},{7,15},{8,0},{9,1},... | collective-permute-start | bytes 196616 | tf_op jit(solution)/shard_map/ppermute | solution.py:24
  39.4 1.2 %collective-permute-done.16 = bf16[64,1024]{1,0:T(8,128)(2,1)S(1)} collective-permute-done((bf16[64,1024]{1,0:T(8,128)(2,1)S(1)}, bf16[64,1024]{1,0:T(8,128)(2,1)S(1)}, u32[]{:S(2)}, u32[]{:S(2)}) %collective-permute-start.16) | collective-permute-done | bytes 131104 | tf_op jit(solution)/shard_map/ppermute | solution.py:24
  40.7 1.2 %collective-permute-start.18 = (bf16[32,1024]{1,0:T(8,128)(2,1)S(1)}, bf16[32,1024]{1,0:T(8,128)(2,1)S(1)}, u32[]{:S(2)}, u32[]{:S(2)}) collective-permute-start(bf16[32,1024]{1,0:T(8,128)(2,1)S(1)} %add.38), channel_id=1, source_target_pairs={{0,16},{1,17},{2,18},{3,19},{4,20},{5,21},{6,22},{7,23},{8,24},{9,... | collective-permute-start | bytes 196616 | tf_op jit(solution)/shard_map/ppermute | solution.py:24
  41.8 1.8 %collective-permute-start.17 = (bf16[32,1024]{1,0:T(8,128)(2,1)S(1)}, bf16[32,1024]{1,0:T(8,128)(2,1)S(1)}, u32[]{:S(2)}, u32[]{:S(2)}) collective-permute-start(bf16[32,1024]{1,0:T(8,128)(2,1)S(1)} %add.37), channel_id=1, source_target_pairs={{0,24},{1,25},{2,26},{3,27},{4,28},{5,29},{6,30},{7,31},{8,16},{9,... | collective-permute-start | bytes 196616 | tf_op jit(solution)/shard_map/ppermute | solution.py:24
  43.7 3.0 %collective-permute-done.18 = bf16[32,1024]{1,0:T(8,128)(2,1)S(1)} collective-permute-done((bf16[32,1024]{1,0:T(8,128)(2,1)S(1)}, bf16[32,1024]{1,0:T(8,128)(2,1)S(1)}, u32[]{:S(2)}, u32[]{:S(2)}) %collective-permute-start.18) | collective-permute-done | bytes 65568 | tf_op jit(solution)/shard_map/ppermute | solution.py:24
  46.6 1.4 %collective-permute-done.17 = bf16[32,1024]{1,0:T(8,128)(2,1)S(1)} collective-permute-done((bf16[32,1024]{1,0:T(8,128)(2,1)S(1)}, bf16[32,1024]{1,0:T(8,128)(2,1)S(1)}, u32[]{:S(2)}, u32[]{:S(2)}) %collective-permute-start.17) | collective-permute-done | bytes 65568 | tf_op jit(solution)/shard_map/ppermute | solution.py:24
  48.0 0.7 %fusion = f32[32,1024]{1,0:T(8,128)} fusion(f32[64,1024]{1,0:T(8,128)S(1)} %add.33.kept_ref, bf16[32,1024]{1,0:T(8,128)(2,1)S(1)} %collective-permute-done.19, bf16[32,1024]{1,0:T(8,128)(2,1)S(1)} %collective-permute-done.18, bf16[32,1024]{1,0:T(8,128)(2,1)S(1)} %collective-permute-done.17, bf16[64,1024]{1,0:T(8,128)(2,1)S(1)} %collective-permute-done.14), kind=kLoop, calls=%fused_computation.2 | loop fusion | flops 262144 | bytes 524288 | tf_op jit(solution)/shard_map/add | solution.py:358
  (26 shorter events, 0.3 us)
Async XLA Ops:
  0.6 13.1 %copy-start.1 = (bf16[256,1024]{1,0:T(8,128)(2,1)S(1)}, bf16[256,1024]{1,0:T(8,128)(2,1)}, u32[]{:S(2)}) copy-start(bf16[256,1024]{1,0:T(8,128)(2,1)} %features_in.1) | copy-start | bytes 1572868
  0.6 13.1 %copy-start = (bf16[256,1024]{1,0:T(8,128)(2,1)S(1)}, bf16[256,1024]{1,0:T(8,128)(2,1)}, u32[]{:S(2)}) copy-start(bf16[256,1024]{1,0:T(8,128)(2,1)} %cotangent_in.1) | copy-start | bytes 1572868
  0.7 13.1 %copy-start.3 = (s32[1,3]{1,0:T(1,128)S(1)}, s32[1,3]{1,0:T(1,128)}, u32[]{:S(2)}) copy-start(s32[1,3]{1,0:T(1,128)} %cols.1) | copy-start | bytes 40
  0.7 13.1 %copy-start.2 = (bf16[1,3,256,256]{3,2,1,0:T(8,128)(2,1)S(1)}, bf16[1,3,256,256]{3,2,1,0:T(8,128)(2,1)}, u32[]{:S(2)}) copy-start(bf16[1,3,256,256]{3,2,1,0:T(8,128)(2,1)} %tiles_in.1) | copy-start | bytes 1179652
  0.7 3.1 %collective-permute-start = (bf16[256,1024]{1,0:T(8,128)(2,1)}, bf16[256,1024]{1,0:T(8,128)(2,1)S(1)}, u32[]{:S(2)}, u32[]{:S(2)}) collective-permute-start(bf16[256,1024]{1,0:T(8,128)(2,1)} %features_in.1), channel_id=1, source_target_pairs={{0,1},{1,0},{2,3},{3,2},{4,5},{5,4},{6,7},{7,6},{8,9},{9,8},{10,11... | collective-permute-start | bytes 1572872 | tf_op jit(solution)/shard_map/ppermute | solution.py:24
  1.2 5.5 %collective-permute-start.1 = (bf16[32,1024]{1,0:T(8,128)(2,1)}, bf16[32,1024]{1,0:T(8,128)(2,1)S(1)}, u32[]{:S(2)}, u32[]{:S(2)}) collective-permute-start(bf16[32,1024]{1,0:T(8,128)(2,1)} %weight.1), channel_id=1, source_target_pairs={{0,2},{1,3},{2,0},{3,1},{4,6},{5,7},{6,4},{7,5},{8,10},{9,11},{10,... | collective-permute-start | bytes 196616 | tf_op jit(solution)/shard_map/ppermute | solution.py:24
  3.8 18.3 %collective-permute-start.2 = (bf16[256,1024]{1,0:T(8,128)(2,1)}, bf16[256,1024]{1,0:T(8,128)(2,1)S(1)}, u32[]{:S(2)}, u32[]{:S(2)}) collective-permute-start(bf16[256,1024]{1,0:T(8,128)(2,1)} %features_in.1), channel_id=1, source_target_pairs={{0,3},{1,2},{2,1},{3,0},{4,7},{5,6},{6,5},{7,4},{8,11},{9,10},{10,... | collective-permute-start | bytes 1572872 | tf_op jit(solution)/shard_map/ppermute | solution.py:24
  5.5 0.8 %copy-start.4 = (bf16[32,1024]{1,0:T(8,128)(2,1)S(1)}, bf16[32,1024]{1,0:T(8,128)(2,1)}, u32[]{:S(2)}) copy-start(bf16[32,1024]{1,0:T(8,128)(2,1)} %weight.1) | copy-start | bytes 196612
  6.7 9.5 %collective-permute-start.8 = (bf16[64,1024]{1,0:T(8,128)(2,1)S(1)}, bf16[64,1024]{1,0:T(8,128)(2,1)S(1)}, u32[]{:S(2)}, u32[]{:S(2)}) collective-permute-start(bf16[64,1024]{1,0:T(8,128)(2,1)S(1)} %pad_maximum_fusion.1.refs_0_), channel_id=1, source_target_pairs={{0,16},{1,17},{2,18},{3,19},{4,20},{5,21},{6,22},{7,23},{8,24},{9,... | collective-permute-start | bytes 393224 | tf_op jit(solution)/shard_map/ppermute | solution.py:24
  9.6 6.6 %collective-permute-start.6 = (bf16[64,1024]{1,0:T(8,128)(2,1)S(1)}, bf16[64,1024]{1,0:T(8,128)(2,1)S(1)}, u32[]{:S(2)}, u32[]{:S(2)}) collective-permute-start(bf16[64,1024]{1,0:T(8,128)(2,1)S(1)} %pad_maximum_fusion.1.refs_0_), channel_id=1, source_target_pairs={{0,4},{1,5},{2,6},{3,7},{4,0},{5,1},{6,2},{7,3},{8,12},{9,13},{10,... | collective-permute-start | bytes 393224 | tf_op jit(solution)/shard_map/ppermute | solution.py:24
  11.1 7.4 %collective-permute-start.5 = (bf16[64,1024]{1,0:T(8,128)(2,1)S(1)}, bf16[64,1024]{1,0:T(8,128)(2,1)S(1)}, u32[]{:S(2)}, u32[]{:S(2)}) collective-permute-start(bf16[64,1024]{1,0:T(8,128)(2,1)S(1)} %pad_maximum_fusion.1.refs_0_), channel_id=1, source_target_pairs={{0,8},{1,9},{2,10},{3,11},{4,12},{5,13},{6,14},{7,15},{8,0},{9,1},... | collective-permute-start | bytes 393224 | tf_op jit(solution)/shard_map/ppermute | solution.py:24
  12.7 9.7 %collective-permute-start.7 = (bf16[64,1024]{1,0:T(8,128)(2,1)S(1)}, bf16[64,1024]{1,0:T(8,128)(2,1)S(1)}, u32[]{:S(2)}, u32[]{:S(2)}) collective-permute-start(bf16[64,1024]{1,0:T(8,128)(2,1)S(1)} %pad_maximum_fusion.1.refs_0_), channel_id=1, source_target_pairs={{0,12},{1,13},{2,14},{3,15},{4,8},{5,9},{6,10},{7,11},{8,4},{9,5},... | collective-permute-start | bytes 393224 | tf_op jit(solution)/shard_map/ppermute | solution.py:24
  18.5 8.4 %collective-permute-start.11 = (bf16[64,1024]{1,0:T(8,128)(2,1)S(1)}, bf16[64,1024]{1,0:T(8,128)(2,1)S(1)}, u32[]{:S(2)}, u32[]{:S(2)}) collective-permute-start(bf16[64,1024]{1,0:T(8,128)(2,1)S(1)} %collective-permute-done.8.refs_1_), channel_id=1, source_target_pairs={{0,4},{1,5},{2,6},{3,7},{4,0},{5,1},{6,2},{7,3},{8,12},{9,13},{10,... | collective-permute-start | bytes 393224 | tf_op jit(solution)/shard_map/ppermute | solution.py:24
  19.2 7.7 %collective-permute-start.10 = (bf16[64,1024]{1,0:T(8,128)(2,1)S(1)}, bf16[64,1024]{1,0:T(8,128)(2,1)S(1)}, u32[]{:S(2)}, u32[]{:S(2)}) collective-permute-start(bf16[64,1024]{1,0:T(8,128)(2,1)S(1)} %collective-permute-done.8.refs_1_), channel_id=1, source_target_pairs={{0,12},{1,13},{2,14},{3,15},{4,8},{5,9},{6,10},{7,11},{8,4},{9,5},... | collective-permute-start | bytes 393224 | tf_op jit(solution)/shard_map/ppermute | solution.py:24
  20.6 6.3 %collective-permute-start.9 = (bf16[64,1024]{1,0:T(8,128)(2,1)S(1)}, bf16[64,1024]{1,0:T(8,128)(2,1)S(1)}, u32[]{:S(2)}, u32[]{:S(2)}) collective-permute-start(bf16[64,1024]{1,0:T(8,128)(2,1)S(1)} %collective-permute-done.8.refs_1_), channel_id=1, source_target_pairs={{0,8},{1,9},{2,10},{3,11},{4,12},{5,13},{6,14},{7,15},{8,0},{9,1},... | collective-permute-start | bytes 393224 | tf_op jit(solution)/shard_map/ppermute | solution.py:24
  22.3 2.4 %collective-permute-start.3 = (bf16[256,1024]{1,0:T(8,128)(2,1)S(1)}, bf16[256,1024]{1,0:T(8,128)(2,1)S(1)}, u32[]{:S(2)}, u32[]{:S(2)}) collective-permute-start(bf16[256,1024]{1,0:T(8,128)(2,1)S(1)} %aggregate.1.refs_0_), channel_id=1, source_target_pairs={{0,1},{1,0},{2,3},{3,2},{4,5},{5,4},{6,7},{7,6},{8,9},{9,8},{10,11... | collective-permute-start | bytes 1572872 | tf_op jit(solution)/shard_map/ppermute | solution.py:24
  22.4 2.3 %collective-permute-start.4 = (bf16[512,256]{1,0:T(8,128)(2,1)S(1)}, bf16[512,256]{1,0:T(8,128)(2,1)S(1)}, u32[]{:S(2)}, u32[]{:S(2)}) collective-permute-start(bf16[512,256]{1,0:T(8,128)(2,1)S(1)} %get-tuple-element.33), channel_id=1, source_target_pairs={{0,1},{1,0},{2,3},{3,2},{4,5},{5,4},{6,7},{7,6},{8,9},{9,8},{10,11... | collective-permute-start | bytes 786440 | tf_op jit(solution)/shard_map/ppermute | solution.py:24
  25.5 6.4 %collective-permute-start.13 = (bf16[128,1024]{1,0:T(8,128)(2,1)S(1)}, bf16[128,1024]{1,0:T(8,128)(2,1)S(1)}, u32[]{:S(2)}, u32[]{:S(2)}) collective-permute-start(bf16[128,1024]{1,0:T(8,128)(2,1)S(1)} %get-tuple-element.36), channel_id=1, source_target_pairs={{0,2},{1,5},{2,0},{3,7},{4,6},{5,1},{6,4},{7,3},{8,10},{9,13},{10,... | collective-permute-start | bytes 786440 | tf_op jit(solution)/shard_map/ppermute | solution.py:24
  27.8 7.7 %collective-permute-start.15 = (bf16[128,1024]{1,0:T(8,128)(2,1)S(1)}, bf16[128,1024]{1,0:T(8,128)(2,1)S(1)}, u32[]{:S(2)}, u32[]{:S(2)}) collective-permute-start(bf16[128,1024]{1,0:T(8,128)(2,1)S(1)} %get-tuple-element.38), channel_id=1, source_target_pairs={{0,2},{1,5},{2,0},{3,7},{4,6},{5,1},{6,4},{7,3},{8,10},{9,13},{10,... | collective-permute-start | bytes 786440 | tf_op jit(solution)/shard_map/ppermute | solution.py:24
  30.3 6.0 %collective-permute-start.12 = (bf16[512,256]{1,0:T(8,128)(2,1)S(1)}, bf16[512,256]{1,0:T(8,128)(2,1)S(1)}, u32[]{:S(2)}, u32[]{:S(2)}) collective-permute-start(bf16[512,256]{1,0:T(8,128)(2,1)S(1)} %pad_maximum_fusion), channel_id=1, source_target_pairs={{0,1},{1,0},{2,3},{3,2},{4,5},{5,4},{6,7},{7,6},{8,9},{9,8},{10,11... | collective-permute-start | bytes 786440 | tf_op jit(solution)/shard_map/ppermute | solution.py:24
  32.0 6.1 %collective-permute-start.14 = (bf16[64,1024]{1,0:T(8,128)(2,1)S(1)}, bf16[64,1024]{1,0:T(8,128)(2,1)S(1)}, u32[]{:S(2)}, u32[]{:S(2)}) collective-permute-start(bf16[64,1024]{1,0:T(8,128)(2,1)S(1)} %add.34), channel_id=1, source_target_pairs={{0,4},{1,3},{2,6},{3,1},{4,0},{5,7},{6,2},{7,5},{8,12},{9,11},{10,... | collective-permute-start | bytes 393224 | tf_op jit(solution)/shard_map/ppermute | solution.py:24
  35.6 5.0 %collective-permute-start.16 = (bf16[64,1024]{1,0:T(8,128)(2,1)S(1)}, bf16[64,1024]{1,0:T(8,128)(2,1)S(1)}, u32[]{:S(2)}, u32[]{:S(2)}) collective-permute-start(bf16[64,1024]{1,0:T(8,128)(2,1)S(1)} %add.36), channel_id=1, source_target_pairs={{0,4},{1,3},{2,6},{3,1},{4,0},{5,7},{6,2},{7,5},{8,12},{9,11},{10,... | collective-permute-start | bytes 393224 | tf_op jit(solution)/shard_map/ppermute | solution.py:24
  38.2 5.5 %collective-permute-start.19 = (bf16[32,1024]{1,0:T(8,128)(2,1)S(1)}, bf16[32,1024]{1,0:T(8,128)(2,1)S(1)}, u32[]{:S(2)}, u32[]{:S(2)}) collective-permute-start(bf16[32,1024]{1,0:T(8,128)(2,1)S(1)} %add.39), channel_id=1, source_target_pairs={{0,8},{1,9},{2,10},{3,11},{4,12},{5,13},{6,14},{7,15},{8,0},{9,1},... | collective-permute-start | bytes 196616 | tf_op jit(solution)/shard_map/ppermute | solution.py:24
  40.7 6.0 %collective-permute-start.18 = (bf16[32,1024]{1,0:T(8,128)(2,1)S(1)}, bf16[32,1024]{1,0:T(8,128)(2,1)S(1)}, u32[]{:S(2)}, u32[]{:S(2)}) collective-permute-start(bf16[32,1024]{1,0:T(8,128)(2,1)S(1)} %add.38), channel_id=1, source_target_pairs={{0,16},{1,17},{2,18},{3,19},{4,20},{5,21},{6,22},{7,23},{8,24},{9,... | collective-permute-start | bytes 196616 | tf_op jit(solution)/shard_map/ppermute | solution.py:24
  41.8 6.2 %collective-permute-start.17 = (bf16[32,1024]{1,0:T(8,128)(2,1)S(1)}, bf16[32,1024]{1,0:T(8,128)(2,1)S(1)}, u32[]{:S(2)}, u32[]{:S(2)}) collective-permute-start(bf16[32,1024]{1,0:T(8,128)(2,1)S(1)} %add.37), channel_id=1, source_target_pairs={{0,24},{1,25},{2,26},{3,27},{4,28},{5,29},{6,30},{7,31},{8,16},{9,... | collective-permute-start | bytes 196616 | tf_op jit(solution)/shard_map/ppermute | solution.py:24

commit v4 on v3

--- a/solution.py
+++ b/solution.py
@@ -33,39 +33,45 @@
     return lax.ppermute(value, "blk", [(i, (i + by) % length) for i in range(length)])
 
 
-def layer_body(first, cot_first, step, agg_own, agg_other, cot_own, cot_other, w, out_own, out_other, grad):
-    for at in range(0, grad.shape[0], step):
-        dst = pl.ds(at, step)
-        rows = w[pl.ds(first + at, step), :]
-        total = None
-        for agg, cot, out in ((agg_own, cot_own, out_own), (agg_other, cot_other, out_other)):
-            pre = lax.dot_general(rows, agg[...], TURN, preferred_element_type=F32)
-            s = jax.nn.sigmoid(pre)
-            out[dst, :] = (pre * s).astype(BF16)
-            slope = s * (1.0 + pre * (1.0 - s))
-            grad_pre = (cot[pl.ds(cot_first + at, step), :].astype(F32) * slope).astype(BF16)
-            term = jnp.dot(grad_pre, agg[...], preferred_element_type=F32)
-            total = term if total is None else total + term
-        grad[dst, :] = total.astype(grad.dtype)
-
-
-def layer(operands, first, cot_first, count, kind):
+def layer_rows(operands, first, cot_first, step, outs, at):
+    w = operands[4]
+    rows, dst = w[pl.ds(first, step), :], pl.ds(at, step)
+    total = None
+    for agg, cot, out in zip(operands[:2], operands[2:4], outs):
+        pre = lax.dot_general(rows, agg[...], TURN, preferred_element_type=F32)
+        s = jax.nn.sigmoid(pre)
+        out[dst, :] = (pre * s).astype(BF16)
+        slope = s * (1.0 + pre * (1.0 - s))
+        grad_pre = (cot[pl.ds(cot_first, step), :].astype(F32) * slope).astype(BF16)
+        term = jnp.dot(grad_pre, agg[...], preferred_element_type=F32)
+        total = term if total is None else total + term
+    return total
+
+
+def layer(operands, first, cot_first, count, kinds, cost=LONG):
     nodes, width = operands[0].shape
+    part = count // len(kinds)
+    step = min(128, count)
 
     def body(*refs):
-        layer_body(first, cot_first, 128, *refs)
-
+        operands, outs, grads = refs[:5], refs[5:7], refs[7:]
+        for at in range(0, count, step):
+            total = layer_rows(operands, first + at, cot_first + at, step, outs, at)
+            for k, grad in enumerate(grads):
+                if len(grads) == 1:
+                    grad[pl.ds(at, step), :] = total.astype(grad.dtype)
+                else:
+                    grad[...] = total[k * part : (k + 1) * part, :].astype(grad.dtype)
+
+    assert len(kinds) == 1 or count == step
     return pl.pallas_call(
         body,
-        out_shape=[
-            jax.ShapeDtypeStruct((count, nodes), BF16),
-            jax.ShapeDtypeStruct((count, nodes), BF16),
-            jax.ShapeDtypeStruct((count, width), kind),
-        ],
+        out_shape=[jax.ShapeDtypeStruct((count, nodes), BF16)] * 2
+        + [jax.ShapeDtypeStruct((part, width), kind) for kind in kinds],
         in_specs=[IN_VMEM] * 5,
-        out_specs=[IN_VMEM] * 3,
-        compiler_params=LIMIT,
-        cost_estimate=LONG,
+        out_specs=[IN_VMEM] * (2 + len(kinds)),
+        compiler_params=LIMIT,
+        cost_estimate=cost,
         name="layer",
     )(*operands)
 
@@ -110,7 +116,7 @@
     cot_own = lax.dot_general(mine, cotangent, TURN, preferred_element_type=F32).astype(BF16)
     cot_other = lax.dot_general(others, cotangent, TURN, preferred_element_type=F32).astype(BF16)
     operands = (agg_own, agg_other, cot_own, swap(cot_other, CORE), held)
-    out_own, out_other, grad = layer(operands, 0, 0, width // 2, F32)
+    out_own, out_other, grad = layer(operands, 0, 0, width // 2, [F32])
     bit = total // 2
     while bit > 1:
         n = grad.shape[0] // 2
@@ -304,10 +310,11 @@
     me = lax.axis_index(AXES).astype(jnp.int32).reshape(1)
     rows, width = weight.shape
 
-    near_block = swap(features, CORE)
     weight_x = swap(weight, X)
-    x_block = swap(after(features, near_block), X ^ CORE)
-    pair = jnp.concatenate([hold(weight, near_block), weight_x])
+    tick = swap(tile_count, CORE)
+    x_block = swap(after(features, tick), X ^ CORE)
+    pair = jnp.concatenate([hold(weight, tick), weight_x])
+    near_block = swap(after(features, tick), CORE)
     far = swap(pair, FAR)
     near = swap(pair, NEAR)
     pieces = {(0, 0): pair, (0, NEAR): near}
@@ -317,43 +324,49 @@
         after(me, pair), tile_cols, tile_count, tiles, features, cotangent, near_block
     )
     cot_other = swap(after(cot_other, x_block), CORE)
-    far = after(far, near, pieces[1, 0])
+    far = after(far, pieces[1, 0], partial)
     pieces[0, FAR] = far
     pieces[1, FAR] = swap(far, Y)
-    pieces[0, NEAR ^ FAR] = swap(far, NEAR)
     pieces[1, NEAR ^ FAR] = swap(far, Y ^ NEAR)
 
     agg_own = aggregate(partial, tile_x, x_block)
     agg_other = swap(agg_own, CORE)
+    pieces[0, NEAR ^ FAR] = swap(after(far, agg_own), NEAR)
     order_e = [pieces[y, z] for y in range(2) for z in ALONG_Z[:2]]
     order_e[0] = after(order_e[0], agg_own)
     w_e = in_order(me, order_e)
     operands = [agg_own, agg_other, cot_own, cot_other]
-    own_e1, other_e1, send_e = layer(operands + [w_e], 4 * rows, 4 * rows, 4 * rows, BF16)
+    half = 2 * rows
+    own_e1, other_e1, send_e = layer(operands + [w_e], 2 * half, 2 * half, 2 * half, [BF16])
     got_e = swap(send_e, X, Y)
     order_l = [pieces[y, z] for y in range(2) for z in ALONG_Z[2:]]
     order_l[0] = after(order_l[0], send_e)
     w_l = in_order(me, order_l)
-    own_l1, other_l1, send_l = layer(operands + [w_l], 4 * rows, 12 * rows, 4 * rows, BF16)
-    got_l = swap(send_l, X, Y)
-    w_e = after(w_e, send_l)
-    own_e0, other_e0, keep_e = layer(operands + [w_e], 0, 0, 4 * rows, F32)
-    own_l0, other_l0, keep_l = layer(operands + [w_l], 0, 8 * rows, 4 * rows, F32)
-
-    sums = []
-    for got, keep in ((got_e, keep_e), (got_l, keep_l)):
-        send = add(keep, 2 * rows, 2 * rows, got[2 * rows :], BF16)
-        sums.append((swap(send, Y, X), add(keep, 0, 2 * rows, got[: 2 * rows], F32)))
+    own_l1, other_l1, send_0, send_1 = layer(
+        operands + [w_l], 2 * half, 6 * half, 2 * half, [BF16] * 2
+    )
+    got_1 = swap(send_1, X, Y)
+    got_0 = swap(send_0, X, Y)
+    w_e = after(w_e, send_1)
+    own_e0, other_e0, keep_e = layer(operands + [w_e], 0, 0, 2 * half, [F32])
+    own_l0, other_l0, keep_l = layer(operands + [w_l], 0, 4 * half, 2 * half, [F32])
+
+    send = add(keep_e, half, half, got_e[half:], BF16)
+    keep_e = add(keep_e, 0, half, got_e[:half], F32)
+    got_e = swap(send, Y, X)
+
+    got_24 = swap(add(keep_l, half, rows, got_1[:rows], BF16), Y, X)
+    got_16 = swap(add(keep_l, half + rows, rows, got_1[rows:], BF16), Y, X)
+    keep_l = add(keep_l, 0, half, got_0, F32)
 
     others = jnp.concatenate([other_e0, other_e1, other_l0, other_l1])
     from_other = swap(others, CORE)
     output = into_place([own_e0, own_e1, own_l0, own_l1, from_other], place)
 
-    (got_e, keep_e), (got_l, keep_l) = sums
     got_8 = swap(add(keep_e, rows, rows, got_e[rows:], BF16), ALONG_Z[1])
-    got_l = after(got_l, output)
-    got_16 = swap(add(keep_l, rows, rows, got_l[rows:], BF16), ALONG_Z[3])
-    got_24 = swap(add(keep_l, 0, rows, got_l[:rows], BF16), ALONG_Z[2])
+    got_24, got_16 = after(got_24, output), after(got_16, output)
+    got_24 = swap(add(keep_l, 0, rows, got_24, BF16), ALONG_Z[2])
+    got_16 = swap(add(keep_l, rows, rows, got_16, BF16), ALONG_Z[3])
     mine = keep_e[:rows] + got_e[:rows].astype(F32)
     return output, mine + sum(v.astype(F32) for v in (got_24, got_16, got_8))
 

time: 48.9 us -> 47.5 us (0.971)
  waiting for transfers between devices: 14.2 us -> 8.29 us
  starting transfers between devices: 23.3 us -> 27.2 us
  Pallas kernels: 8.07 us -> 8.67 us
    ppermute x20 -> x23, waiting for transfers between devices: 14.2 us -> 8.29 us  [swap(): lax.ppermute(value, AXES, [(i, i ^ masks[i % 2]) for i in range(total)])]
    ppermute x20 -> x23, starting transfers between devices: 23.3 us -> 27.2 us  [swap(): lax.ppermute(value, AXES, [(i, i ^ masks[i % 2]) for i in range(total)])]
    pallas_call x1, Pallas kernels: 0.01 us -> 0.61 us  [hold(): pl.pallas_call(hold_body, out_shape=jax.ShapeDtypeStruct(weight.shape, BF...]
  transfers between devices with their start and end apart: 20 -> 23, of which waited for: 8 -> 8; matrix products, arithmetic and copies ran while one was open for 0% -> 0% of each run, Pallas kernels for 17% -> 18%
where the time goes in v4:
time: 47.5 us; the launch traced here: 47.3 us
  starting transfers between devices  27.2 us (57%)
  Pallas kernels  8.67 us (18%)
  waiting for transfers between devices  8.29 us (17%)
  between operations  1.56 us (3%)
  local copies, waits for them, and re-layouts  0.89 us (2%)
  other arithmetic  0.73 us (2%)
    ppermute x23, starting transfers between devices, swap(): lax.ppermute(value, AXES, [(i, i ^ masks[i % 2]) for i in range(total)])  27.2 us
    ppermute x23, waiting for transfers between devices, swap(): lax.ppermute(value, AXES, [(i, i ^ masks[i % 2]) for i in range(total)])  8.29 us
    pallas_call x4, Pallas kernels, layer(): pl.pallas_call(body, out_shape=[jax.ShapeDtypeStruct((count, nodes), BF16...  3.33 us
    pallas_call x1, Pallas kernels, prepare(): pl.pallas_call(prepare_body, out_shape=[jax.ShapeDtypeStruct((nodes, widt...  2.39 us
    pallas_call x1, Pallas kernels, into_place(): pl.pallas_call(into_place_body, out_shape=jax.ShapeDtypeStruct((parts[0]....  1.79 us
  transfers between devices with their start and end apart: 23, of which 8 were waited for; matrix products, arithmetic and copies ran while one was open for 0% of the time, Pallas kernels for 18%

profile of v4, /device:TPU:0, one launch (start us, length us, event | category | flops | bytes accessed | tf_op | source)
XLA Modules:
  0.0 47.3 jit_solution(7735389686527934262)
XLA Ops:
  0.7 0.5 %collective-permute-start = (s32[1]{0:T(128)}, s32[1]{0:T(128)}, u32[]{:S(2)}, u32[]{:S(2)}) collective-permute-start(s32[1]{0:T(128)} %param.9), channel_id=1, source_target_pairs={{0,1},{1,0},{2,3},{3,2},{4,5},{5,4},{6,7},{7,6},{8,9},{9,8},{10,11... | collective-permute-start | bytes 20 | tf_op jit(solution)/shard_map/ppermute | solution.py:24
  1.2 2.6 %collective-permute-start.1 = (bf16[32,1024]{1,0:T(8,128)(2,1)}, bf16[32,1024]{1,0:T(8,128)(2,1)S(1)}, u32[]{:S(2)}, u32[]{:S(2)}) collective-permute-start(bf16[32,1024]{1,0:T(8,128)(2,1)} %weight.1), channel_id=1, source_target_pairs={{0,2},{1,3},{2,0},{3,1},{4,6},{5,7},{6,4},{7,5},{8,10},{9,11},{10,... | collective-permute-start | bytes 196616 | tf_op jit(solution)/shard_map/ppermute | solution.py:24
  3.8 0.0 collective-permute-done.near_block
  3.8 1.0 %collective-permute-start.3 = (bf16[256,1024]{1,0:T(8,128)(2,1)}, bf16[256,1024]{1,0:T(8,128)(2,1)S(1)}, u32[]{:S(2)}, u32[]{:S(2)}) collective-permute-start(bf16[256,1024]{1,0:T(8,128)(2,1)} %features_in.1), channel_id=1, source_target_pairs={{0,3},{1,2},{2,1},{3,0},{4,7},{5,6},{6,5},{7,4},{8,11},{9,10},{10,... | collective-permute-start | bytes 1572872 | tf_op jit(solution)/shard_map/ppermute | solution.py:24
  4.7 0.3 collective-permute-start.2
  5.0 0.8 %copy-done.4 = bf16[32,1024]{1,0:T(8,128)(2,1)S(1)} copy-done((bf16[32,1024]{1,0:T(8,128)(2,1)S(1)}, bf16[32,1024]{1,0:T(8,128)(2,1)}, u32[]{:S(2)}) %copy-start.4) | copy-done | bytes 65560
  5.9 0.6 %hold.1 = bf16[32,1024]{1,0:T(8,128)(2,1)S(1)} custom-call(bf16[32,1024]{1,0:T(8,128)(2,1)S(1)} %copy-done.4, s32[1]{0:T(128)} %collective-permute-done.near_block), custom_call_target="tpu_custom_call" | custom-call | flops 20000000000 | tf_op jit(solution)/shard_map/hold/pallas_call | solution.py:136
  6.5 0.2 collective-permute-done.1
  6.7 2.9 %collective-permute-start.9 = (bf16[64,1024]{1,0:T(8,128)(2,1)S(1)}, bf16[64,1024]{1,0:T(8,128)(2,1)S(1)}, u32[]{:S(2)}, u32[]{:S(2)}) collective-permute-start(bf16[64,1024]{1,0:T(8,128)(2,1)S(1)} %pad_maximum_fusion.1.refs_0_), channel_id=1, source_target_pairs={{0,16},{1,17},{2,18},{3,19},{4,20},{5,21},{6,22},{7,23},{8,24},{9,... | collective-permute-start | bytes 393224 | tf_op jit(solution)/shard_map/ppermute | solution.py:24
  9.6 1.5 %collective-permute-start.7 = (bf16[64,1024]{1,0:T(8,128)(2,1)S(1)}, bf16[64,1024]{1,0:T(8,128)(2,1)S(1)}, u32[]{:S(2)}, u32[]{:S(2)}) collective-permute-start(bf16[64,1024]{1,0:T(8,128)(2,1)S(1)} %pad_maximum_fusion.1.refs_0_), channel_id=1, source_target_pairs={{0,4},{1,5},{2,6},{3,7},{4,0},{5,1},{6,2},{7,3},{8,12},{9,13},{10,... | collective-permute-start | bytes 393224 | tf_op jit(solution)/shard_map/ppermute | solution.py:24
  11.1 1.5 %collective-permute-start.8 = (bf16[64,1024]{1,0:T(8,128)(2,1)S(1)}, bf16[64,1024]{1,0:T(8,128)(2,1)S(1)}, u32[]{:S(2)}, u32[]{:S(2)}) collective-permute-start(bf16[64,1024]{1,0:T(8,128)(2,1)S(1)} %pad_maximum_fusion.1.refs_0_), channel_id=1, source_target_pairs={{0,12},{1,13},{2,14},{3,15},{4,8},{5,9},{6,10},{7,11},{8,4},{9,5},... | collective-permute-start | bytes 393224 | tf_op jit(solution)/shard_map/ppermute | solution.py:24
  12.6 0.0 collective-permute-done.2.near_block
  12.6 0.5 collective-permute-start.6
  13.8 2.4 %prepare.1 = (f32[256,1024]{1,0:T(8,128)S(1)}, bf16[256,256]{1,0:T(8,128)(2,1)S(1)}, bf16[512,256]{1,0:T(8,128)(2,1)S(1)}, bf16[512,256]{1,0:T(8,128)(2,1)S(1)}, bf16[1024,1024]{1,0:T(8,128)(2,1)S(1)}) custom-call(s32[1]{0:T(128)} %bitcast.me_ref, s32[1,3]{1,0:T(1,128)S(1)} %copy-done.3, s32[1]{0:T(128)S(6)} %copy.8.count, ...), custom_call_target="tpu_custom_call" | custom-call | tf_op jit(solution)/shard_map/prepare/pallas_call | solution.py:202
  16.2 0.0 collective-permute-done.9.refs_1_
  16.2 1.6 %collective-permute-start.12 = (bf16[64,1024]{1,0:T(8,128)(2,1)S(1)}, bf16[64,1024]{1,0:T(8,128)(2,1)S(1)}, u32[]{:S(2)}, u32[]{:S(2)}) collective-permute-start(bf16[64,1024]{1,0:T(8,128)(2,1)S(1)} %collective-permute-done.9.refs_1_), channel_id=1, source_target_pairs={{0,4},{1,5},{2,6},{3,7},{4,0},{5,1},{6,2},{7,3},{8,12},{9,13},{10,... | collective-permute-start | bytes 393224 | tf_op jit(solution)/shard_map/ppermute | solution.py:24
  17.8 2.0 %collective-permute-start.11 = (bf16[64,1024]{1,0:T(8,128)(2,1)S(1)}, bf16[64,1024]{1,0:T(8,128)(2,1)S(1)}, u32[]{:S(2)}, u32[]{:S(2)}) collective-permute-start(bf16[64,1024]{1,0:T(8,128)(2,1)S(1)} %collective-permute-done.9.refs_1_), channel_id=1, source_target_pairs={{0,12},{1,13},{2,14},{3,15},{4,8},{5,9},{6,10},{7,11},{8,4},{9,5},... | collective-permute-start | bytes 393224 | tf_op jit(solution)/shard_map/ppermute | solution.py:24
  19.8 0.0 collective-permute-done.3.block
  19.8 0.3 aggregate.1.refs_0_
  20.1 0.1 collective-permute-start.4
  20.2 0.5 %collective-permute-start.5 = (bf16[512,256]{1,0:T(8,128)(2,1)S(1)}, bf16[512,256]{1,0:T(8,128)(2,1)S(1)}, u32[]{:S(2)}, u32[]{:S(2)}) collective-permute-start(bf16[512,256]{1,0:T(8,128)(2,1)S(1)} %get-tuple-element.36), channel_id=1, source_target_pairs={{0,1},{1,0},{2,3},{3,2},{4,5},{5,4},{6,7},{7,6},{8,9},{9,8},{10,11... | collective-permute-start | bytes 786440 | tf_op jit(solution)/shard_map/ppermute | solution.py:24
  20.7 0.6 %collective-permute-done.6.refs_1_ = bf16[64,1024]{1,0:T(8,128)(2,1)S(1)} collective-permute-done((bf16[64,1024]{1,0:T(8,128)(2,1)S(1)}, bf16[64,1024]{1,0:T(8,128)(2,1)S(1)}, u32[]{:S(2)}, u32[]{:S(2)}) %collective-permute-start.6) | collective-permute-done | bytes 131104 | tf_op jit(solution)/shard_map/ppermute | solution.py:24
  21.3 0.0 collective-permute-start.10
  21.3 1.1 %collective-permute-done.5.refs_3_ = bf16[512,256]{1,0:T(8,128)(2,1)S(1)} collective-permute-done((bf16[512,256]{1,0:T(8,128)(2,1)S(1)}, bf16[512,256]{1,0:T(8,128)(2,1)S(1)}, u32[]{:S(2)}, u32[]{:S(2)}) %collective-permute-start.5) | collective-permute-done | bytes 262176 | tf_op jit(solution)/shard_map/ppermute | solution.py:24
  22.4 0.0 collective-permute-done.4.refs_1_
  22.4 0.8 %layer.4 = (bf16[128,256]{1,0:T(8,128)(2,1)S(1)}, bf16[128,256]{1,0:T(8,128)(2,1)S(1)}, bf16[128,1024]{1,0:T(8,128)(2,1)S(1)}) custom-call(bf16[256,1024]{1,0:T(8,128)(2,1)S(1)} %aggregate.1.refs_0_, bf16[256,1024]{1,0:T(8,128)(2,1)S(1)} %collective-permute-done.4.refs_1_, bf16[512,256]{1,0:T(8,128)(2,1)S(1)} %get-tuple-element.34.refs_2_, ...), custom_call_target="tpu_custom_call" | custom-call | flops 20000000000 | tf_op jit(solution)/shard_map/layer/pallas_call | solution.py:67
  23.3 1.5 %collective-permute-start.14 = (bf16[128,1024]{1,0:T(8,128)(2,1)S(1)}, bf16[128,1024]{1,0:T(8,128)(2,1)S(1)}, u32[]{:S(2)}, u32[]{:S(2)}) collective-permute-start(bf16[128,1024]{1,0:T(8,128)(2,1)S(1)} %get-tuple-element.40), channel_id=1, source_target_pairs={{0,2},{1,5},{2,0},{3,7},{4,6},{5,1},{6,4},{7,3},{8,10},{9,13},{10,... | collective-permute-start | bytes 786440 | tf_op jit(solution)/shard_map/ppermute | solution.py:24
  24.7 1.5 %collective-permute-done.10.refs_0_ = bf16[64,1024]{1,0:T(8,128)(2,1)S(1)} collective-permute-done((bf16[64,1024]{1,0:T(8,128)(2,1)S(1)}, bf16[64,1024]{1,0:T(8,128)(2,1)S(1)}, u32[]{:S(2)}, u32[]{:S(2)}) %collective-permute-start.10) | collective-permute-done | bytes 131104 | tf_op jit(solution)/shard_map/ppermute | solution.py:24
  26.2 0.0 collective-permute-done.12.refs_3_
  26.2 0.0 collective-permute-done.11.refs_2_
  26.3 0.8 %layer.5 = (bf16[128,256]{1,0:T(8,128)(2,1)S(1)}, bf16[128,256]{1,0:T(8,128)(2,1)S(1)}, bf16[64,1024]{1,0:T(8,128)(2,1)S(1)}, bf16[64,1024]{1,0:T(8,128)(2,1)S(1)}) custom-call(bf16[256,1024]{1,0:T(8,128)(2,1)S(1)} %aggregate.1.refs_0_, bf16[256,1024]{1,0:T(8,128)(2,1)S(1)} %collective-permute-done.4.refs_1_, ...), custom_call_target="tpu_custom_call" | custom-call | flops 20000000000 | tf_op jit(solution)/shard_map/layer/pallas_call | solution.py:67
  27.1 1.4 %collective-permute-start.17 = (bf16[64,1024]{1,0:T(8,128)(2,1)S(1)}, bf16[64,1024]{1,0:T(8,128)(2,1)S(1)}, u32[]{:S(2)}, u32[]{:S(2)}) collective-permute-start(bf16[64,1024]{1,0:T(8,128)(2,1)S(1)} %get-tuple-element.42), channel_id=1, source_target_pairs={{0,2},{1,5},{2,0},{3,7},{4,6},{5,1},{6,4},{7,3},{8,10},{9,13},{10,... | collective-permute-start | bytes 393224 | tf_op jit(solution)/shard_map/ppermute | solution.py:24
  28.5 0.7 %collective-permute-start.16 = (bf16[64,1024]{1,0:T(8,128)(2,1)S(1)}, bf16[64,1024]{1,0:T(8,128)(2,1)S(1)}, u32[]{:S(2)}, u32[]{:S(2)}) collective-permute-start(bf16[64,1024]{1,0:T(8,128)(2,1)S(1)} %get-tuple-element.55), channel_id=1, source_target_pairs={{0,2},{1,5},{2,0},{3,7},{4,6},{5,1},{6,4},{7,3},{8,10},{9,13},{10,... | collective-permute-start | bytes 393224 | tf_op jit(solution)/shard_map/ppermute | solution.py:24
  29.2 0.8 %layer.7 = (bf16[128,256]{1,0:T(8,128)(2,1)S(1)}, bf16[128,256]{1,0:T(8,128)(2,1)S(1)}, f32[128,1024]{1,0:T(8,128)S(1)}) custom-call(bf16[256,1024]{1,0:T(8,128)(2,1)S(1)} %aggregate.1.refs_0_, bf16[256,1024]{1,0:T(8,128)(2,1)S(1)} %collective-permute-done.4.refs_1_, bf16[512,256]{1,0:T(8,128)(2,1)S(1)} %get-tuple-element.34.refs_2_, ...), custom_call_target="tpu_custom_call" | custom-call | flops 20000000000 | tf_op jit(solution)/shard_map/layer/pallas_call | solution.py:67
  30.0 0.8 %layer.6 = (bf16[128,256]{1,0:T(8,128)(2,1)S(1)}, bf16[128,256]{1,0:T(8,128)(2,1)S(1)}, f32[128,1024]{1,0:T(8,128)S(1)}) custom-call(bf16[256,1024]{1,0:T(8,128)(2,1)S(1)} %aggregate.1.refs_0_, bf16[256,1024]{1,0:T(8,128)(2,1)S(1)} %collective-permute-done.4.refs_1_, bf16[512,256]{1,0:T(8,128)(2,1)S(1)} %get-tuple-element.34.refs_2_, ...), custom_call_target="tpu_custom_call" | custom-call | flops 20000000000 | tf_op jit(solution)/shard_map/layer/pallas_call | solution.py:67
  30.9 0.1 collective-permute-start.13
  31.1 2.0 %collective-permute-start.15 = (bf16[64,1024]{1,0:T(8,128)(2,1)S(1)}, bf16[64,1024]{1,0:T(8,128)(2,1)S(1)}, u32[]{:S(2)}, u32[]{:S(2)}) collective-permute-start(bf16[64,1024]{1,0:T(8,128)(2,1)S(1)} %add.35), channel_id=1, source_target_pairs={{0,4},{1,3},{2,6},{3,1},{4,0},{5,7},{6,2},{7,5},{8,12},{9,11},{10,... | collective-permute-start | bytes 393224 | tf_op jit(solution)/shard_map/ppermute | solution.py:24
  33.1 1.1 %collective-permute-start.20 = (bf16[32,1024]{1,0:T(8,128)(2,1)S(1)}, bf16[32,1024]{1,0:T(8,128)(2,1)S(1)}, u32[]{:S(2)}, u32[]{:S(2)}) collective-permute-start(bf16[32,1024]{1,0:T(8,128)(2,1)S(1)} %add.39), channel_id=1, source_target_pairs={{0,4},{1,3},{2,6},{3,1},{4,0},{5,7},{6,2},{7,5},{8,12},{9,11},{10,... | collective-permute-start | bytes 196616 | tf_op jit(solution)/shard_map/ppermute | solution.py:24
  34.2 1.1 %collective-permute-start.18 = (bf16[32,1024]{1,0:T(8,128)(2,1)S(1)}, bf16[32,1024]{1,0:T(8,128)(2,1)S(1)}, u32[]{:S(2)}, u32[]{:S(2)}) collective-permute-start(bf16[32,1024]{1,0:T(8,128)(2,1)S(1)} %add.37), channel_id=1, source_target_pairs={{0,4},{1,3},{2,6},{3,1},{4,0},{5,7},{6,2},{7,5},{8,12},{9,11},{10,... | collective-permute-start | bytes 196616 | tf_op jit(solution)/shard_map/ppermute | solution.py:24
  35.4 1.8 %into_place.1 = bf16[256,1024]{1,0:T(8,128)(2,1)} custom-call(bf16[128,256]{1,0:T(8,128)(2,1)S(1)} %get-tuple-element.44.refs_0_, bf16[128,256]{1,0:T(8,128)(2,1)S(1)} %get-tuple-element.45.refs_1_, bf16[128,256]{1,0:T(8,128)(2,1)S(1)} %get-tuple-element.46.refs_2_, bf16[128,256]{1,0:T(8,128)(2,1)S(1)} %get-tuple-element.47.refs_3_, ...), custom_call_target="tpu_custom_call" | custom-call | tf_op jit(solution)/shard_map/into_place/pallas_call | solution.py:283
  37.2 0.3 collective-permute-done.20.got_ref
  37.5 1.1 %collective-permute-done.18.got_ref = bf16[32,1024]{1,0:T(8,128)(2,1)S(1)} collective-permute-done((bf16[32,1024]{1,0:T(8,128)(2,1)S(1)}, bf16[32,1024]{1,0:T(8,128)(2,1)S(1)}, u32[]{:S(2)}, u32[]{:S(2)}) %collective-permute-start.18) | collective-permute-done | bytes 65568 | tf_op jit(solution)/shard_map/ppermute | solution.py:24
  38.6 2.3 %collective-permute-start.19 = (bf16[32,1024]{1,0:T(8,128)(2,1)S(1)}, bf16[32,1024]{1,0:T(8,128)(2,1)S(1)}, u32[]{:S(2)}, u32[]{:S(2)}) collective-permute-start(bf16[32,1024]{1,0:T(8,128)(2,1)S(1)} %add.38), channel_id=1, source_target_pairs={{0,24},{1,25},{2,26},{3,27},{4,28},{5,29},{6,30},{7,31},{8,16},{9,... | collective-permute-start | bytes 196616 | tf_op jit(solution)/shard_map/ppermute | solution.py:24
  40.9 0.6 %collective-permute-start.21 = (bf16[32,1024]{1,0:T(8,128)(2,1)S(1)}, bf16[32,1024]{1,0:T(8,128)(2,1)S(1)}, u32[]{:S(2)}, u32[]{:S(2)}) collective-permute-start(bf16[32,1024]{1,0:T(8,128)(2,1)S(1)} %add.40), channel_id=1, source_target_pairs={{0,16},{1,17},{2,18},{3,19},{4,20},{5,21},{6,22},{7,23},{8,24},{9,... | collective-permute-start | bytes 196616 | tf_op jit(solution)/shard_map/ppermute | solution.py:24
  41.6 1.6 %collective-permute-start.22 = (bf16[32,1024]{1,0:T(8,128)(2,1)S(1)}, bf16[32,1024]{1,0:T(8,128)(2,1)S(1)}, u32[]{:S(2)}, u32[]{:S(2)}) collective-permute-start(bf16[32,1024]{1,0:T(8,128)(2,1)S(1)} %add.41), channel_id=1, source_target_pairs={{0,8},{1,9},{2,10},{3,11},{4,12},{5,13},{6,14},{7,15},{8,0},{9,1},... | collective-permute-start | bytes 196616 | tf_op jit(solution)/shard_map/ppermute | solution.py:24
  43.1 1.9 %collective-permute-done.19 = bf16[32,1024]{1,0:T(8,128)(2,1)S(1)} collective-permute-done((bf16[32,1024]{1,0:T(8,128)(2,1)S(1)}, bf16[32,1024]{1,0:T(8,128)(2,1)S(1)}, u32[]{:S(2)}, u32[]{:S(2)}) %collective-permute-start.19) | collective-permute-done | bytes 65568 | tf_op jit(solution)/shard_map/ppermute | solution.py:24
  45.1 1.6 %collective-permute-done.21 = bf16[32,1024]{1,0:T(8,128)(2,1)S(1)} collective-permute-done((bf16[32,1024]{1,0:T(8,128)(2,1)S(1)}, bf16[32,1024]{1,0:T(8,128)(2,1)S(1)}, u32[]{:S(2)}, u32[]{:S(2)}) %collective-permute-start.21) | collective-permute-done | bytes 65568 | tf_op jit(solution)/shard_map/ppermute | solution.py:24
  46.6 0.7 %fusion = f32[32,1024]{1,0:T(8,128)} fusion(f32[64,1024]{1,0:T(8,128)S(1)} %add.34.kept_ref, bf16[32,1024]{1,0:T(8,128)(2,1)S(1)} %collective-permute-done.22, bf16[32,1024]{1,0:T(8,128)(2,1)S(1)} %collective-permute-done.21, bf16[32,1024]{1,0:T(8,128)(2,1)S(1)} %collective-permute-done.19, bf16[64,1024]{1,0:T(8,128)(2,1)S(1)} %collective-permute-done.15), kind=kLoop, calls=%fused_computation.2 | loop fusion | flops 262144 | bytes 524288 | tf_op jit(solution)/shard_map/add | solution.py:371
  (32 shorter events, 0.3 us)
Async XLA Ops:
  0.6 13.1 %copy-start.1 = (bf16[256,1024]{1,0:T(8,128)(2,1)S(1)}, bf16[256,1024]{1,0:T(8,128)(2,1)}, u32[]{:S(2)}) copy-start(bf16[256,1024]{1,0:T(8,128)(2,1)} %features_in.1) | copy-start | bytes 1572868
  0.6 13.1 %copy-start = (bf16[256,1024]{1,0:T(8,128)(2,1)S(1)}, bf16[256,1024]{1,0:T(8,128)(2,1)}, u32[]{:S(2)}) copy-start(bf16[256,1024]{1,0:T(8,128)(2,1)} %cotangent_in.1) | copy-start | bytes 1572868
  0.7 13.1 %copy-start.3 = (s32[1,3]{1,0:T(1,128)S(1)}, s32[1,3]{1,0:T(1,128)}, u32[]{:S(2)}) copy-start(s32[1,3]{1,0:T(1,128)} %cols.1) | copy-start | bytes 40
  0.7 13.1 %copy-start.2 = (bf16[1,3,256,256]{3,2,1,0:T(8,128)(2,1)S(1)}, bf16[1,3,256,256]{3,2,1,0:T(8,128)(2,1)}, u32[]{:S(2)}) copy-start(bf16[1,3,256,256]{3,2,1,0:T(8,128)(2,1)} %tiles_in.1) | copy-start | bytes 1179652
  0.7 3.1 %collective-permute-start = (s32[1]{0:T(128)}, s32[1]{0:T(128)}, u32[]{:S(2)}, u32[]{:S(2)}) collective-permute-start(s32[1]{0:T(128)} %param.9), channel_id=1, source_target_pairs={{0,1},{1,0},{2,3},{3,2},{4,5},{5,4},{6,7},{7,6},{8,9},{9,8},{10,11... | collective-permute-start | bytes 20 | tf_op jit(solution)/shard_map/ppermute | solution.py:24
  1.2 5.5 %collective-permute-start.1 = (bf16[32,1024]{1,0:T(8,128)(2,1)}, bf16[32,1024]{1,0:T(8,128)(2,1)S(1)}, u32[]{:S(2)}, u32[]{:S(2)}) collective-permute-start(bf16[32,1024]{1,0:T(8,128)(2,1)} %weight.1), channel_id=1, source_target_pairs={{0,2},{1,3},{2,0},{3,1},{4,6},{5,7},{6,4},{7,5},{8,10},{9,11},{10,... | collective-permute-start | bytes 196616 | tf_op jit(solution)/shard_map/ppermute | solution.py:24
  3.8 16.0 %collective-permute-start.3 = (bf16[256,1024]{1,0:T(8,128)(2,1)}, bf16[256,1024]{1,0:T(8,128)(2,1)S(1)}, u32[]{:S(2)}, u32[]{:S(2)}) collective-permute-start(bf16[256,1024]{1,0:T(8,128)(2,1)} %features_in.1), channel_id=1, source_target_pairs={{0,3},{1,2},{2,1},{3,0},{4,7},{5,6},{6,5},{7,4},{8,11},{9,10},{10,... | collective-permute-start | bytes 1572872 | tf_op jit(solution)/shard_map/ppermute | solution.py:24
  4.7 7.9 %collective-permute-start.2 = (bf16[256,1024]{1,0:T(8,128)(2,1)}, bf16[256,1024]{1,0:T(8,128)(2,1)S(1)}, u32[]{:S(2)}, u32[]{:S(2)}) collective-permute-start(bf16[256,1024]{1,0:T(8,128)(2,1)} %features_in.1), channel_id=1, source_target_pairs={{0,1},{1,0},{2,3},{3,2},{4,5},{5,4},{6,7},{7,6},{8,9},{9,8},{10,11... | collective-permute-start | bytes 1572872 | tf_op jit(solution)/shard_map/ppermute | solution.py:24
  5.0 0.8 %copy-start.4 = (bf16[32,1024]{1,0:T(8,128)(2,1)S(1)}, bf16[32,1024]{1,0:T(8,128)(2,1)}, u32[]{:S(2)}) copy-start(bf16[32,1024]{1,0:T(8,128)(2,1)} %weight.1) | copy-start | bytes 196612
  6.7 9.5 %collective-permute-start.9 = (bf16[64,1024]{1,0:T(8,128)(2,1)S(1)}, bf16[64,1024]{1,0:T(8,128)(2,1)S(1)}, u32[]{:S(2)}, u32[]{:S(2)}) collective-permute-start(bf16[64,1024]{1,0:T(8,128)(2,1)S(1)} %pad_maximum_fusion.1.refs_0_), channel_id=1, source_target_pairs={{0,16},{1,17},{2,18},{3,19},{4,20},{5,21},{6,22},{7,23},{8,24},{9,... | collective-permute-start | bytes 393224 | tf_op jit(solution)/shard_map/ppermute | solution.py:24
  9.6 6.6 %collective-permute-start.7 = (bf16[64,1024]{1,0:T(8,128)(2,1)S(1)}, bf16[64,1024]{1,0:T(8,128)(2,1)S(1)}, u32[]{:S(2)}, u32[]{:S(2)}) collective-permute-start(bf16[64,1024]{1,0:T(8,128)(2,1)S(1)} %pad_maximum_fusion.1.refs_0_), channel_id=1, source_target_pairs={{0,4},{1,5},{2,6},{3,7},{4,0},{5,1},{6,2},{7,3},{8,12},{9,13},{10,... | collective-permute-start | bytes 393224 | tf_op jit(solution)/shard_map/ppermute | solution.py:24
  11.1 9.0 %collective-permute-start.8 = (bf16[64,1024]{1,0:T(8,128)(2,1)S(1)}, bf16[64,1024]{1,0:T(8,128)(2,1)S(1)}, u32[]{:S(2)}, u32[]{:S(2)}) collective-permute-start(bf16[64,1024]{1,0:T(8,128)(2,1)S(1)} %pad_maximum_fusion.1.refs_0_), channel_id=1, source_target_pairs={{0,12},{1,13},{2,14},{3,15},{4,8},{5,9},{6,10},{7,11},{8,4},{9,5},... | collective-permute-start | bytes 393224 | tf_op jit(solution)/shard_map/ppermute | solution.py:24
  12.6 8.6 %collective-permute-start.6 = (bf16[64,1024]{1,0:T(8,128)(2,1)S(1)}, bf16[64,1024]{1,0:T(8,128)(2,1)S(1)}, u32[]{:S(2)}, u32[]{:S(2)}) collective-permute-start(bf16[64,1024]{1,0:T(8,128)(2,1)S(1)} %pad_maximum_fusion.1.refs_0_), channel_id=1, source_target_pairs={{0,8},{1,9},{2,10},{3,11},{4,12},{5,13},{6,14},{7,15},{8,0},{9,1},... | collective-permute-start | bytes 393224 | tf_op jit(solution)/shard_map/ppermute | solution.py:24
  16.2 10.0 %collective-permute-start.12 = (bf16[64,1024]{1,0:T(8,128)(2,1)S(1)}, bf16[64,1024]{1,0:T(8,128)(2,1)S(1)}, u32[]{:S(2)}, u32[]{:S(2)}) collective-permute-start(bf16[64,1024]{1,0:T(8,128)(2,1)S(1)} %collective-permute-done.9.refs_1_), channel_id=1, source_target_pairs={{0,4},{1,5},{2,6},{3,7},{4,0},{5,1},{6,2},{7,3},{8,12},{9,13},{10,... | collective-permute-start | bytes 393224 | tf_op jit(solution)/shard_map/ppermute | solution.py:24
  17.8 8.4 %collective-permute-start.11 = (bf16[64,1024]{1,0:T(8,128)(2,1)S(1)}, bf16[64,1024]{1,0:T(8,128)(2,1)S(1)}, u32[]{:S(2)}, u32[]{:S(2)}) collective-permute-start(bf16[64,1024]{1,0:T(8,128)(2,1)S(1)} %collective-permute-done.9.refs_1_), channel_id=1, source_target_pairs={{0,12},{1,13},{2,14},{3,15},{4,8},{5,9},{6,10},{7,11},{8,4},{9,5},... | collective-permute-start | bytes 393224 | tf_op jit(solution)/shard_map/ppermute | solution.py:24
  20.1 2.4 %collective-permute-start.4 = (bf16[256,1024]{1,0:T(8,128)(2,1)S(1)}, bf16[256,1024]{1,0:T(8,128)(2,1)S(1)}, u32[]{:S(2)}, u32[]{:S(2)}) collective-permute-start(bf16[256,1024]{1,0:T(8,128)(2,1)S(1)} %aggregate.1.refs_0_), channel_id=1, source_target_pairs={{0,1},{1,0},{2,3},{3,2},{4,5},{5,4},{6,7},{7,6},{8,9},{9,8},{10,11... | collective-permute-start | bytes 1572872 | tf_op jit(solution)/shard_map/ppermute | solution.py:24
  20.2 2.3 %collective-permute-start.5 = (bf16[512,256]{1,0:T(8,128)(2,1)S(1)}, bf16[512,256]{1,0:T(8,128)(2,1)S(1)}, u32[]{:S(2)}, u32[]{:S(2)}) collective-permute-start(bf16[512,256]{1,0:T(8,128)(2,1)S(1)} %get-tuple-element.36), channel_id=1, source_target_pairs={{0,1},{1,0},{2,3},{3,2},{4,5},{5,4},{6,7},{7,6},{8,9},{9,8},{10,11... | collective-permute-start | bytes 786440 | tf_op jit(solution)/shard_map/ppermute | solution.py:24
  21.3 5.0 %collective-permute-start.10 = (bf16[64,1024]{1,0:T(8,128)(2,1)S(1)}, bf16[64,1024]{1,0:T(8,128)(2,1)S(1)}, u32[]{:S(2)}, u32[]{:S(2)}) collective-permute-start(bf16[64,1024]{1,0:T(8,128)(2,1)S(1)} %collective-permute-done.9.refs_1_), channel_id=1, source_target_pairs={{0,8},{1,9},{2,10},{3,11},{4,12},{5,13},{6,14},{7,15},{8,0},{9,1},... | collective-permute-start | bytes 393224 | tf_op jit(solution)/shard_map/ppermute | solution.py:24
  23.3 7.7 %collective-permute-start.14 = (bf16[128,1024]{1,0:T(8,128)(2,1)S(1)}, bf16[128,1024]{1,0:T(8,128)(2,1)S(1)}, u32[]{:S(2)}, u32[]{:S(2)}) collective-permute-start(bf16[128,1024]{1,0:T(8,128)(2,1)S(1)} %get-tuple-element.40), channel_id=1, source_target_pairs={{0,2},{1,5},{2,0},{3,7},{4,6},{5,1},{6,4},{7,3},{8,10},{9,13},{10,... | collective-permute-start | bytes 786440 | tf_op jit(solution)/shard_map/ppermute | solution.py:24
  27.1 6.0 %collective-permute-start.17 = (bf16[64,1024]{1,0:T(8,128)(2,1)S(1)}, bf16[64,1024]{1,0:T(8,128)(2,1)S(1)}, u32[]{:S(2)}, u32[]{:S(2)}) collective-permute-start(bf16[64,1024]{1,0:T(8,128)(2,1)S(1)} %get-tuple-element.42), channel_id=1, source_target_pairs={{0,2},{1,5},{2,0},{3,7},{4,6},{5,1},{6,4},{7,3},{8,10},{9,13},{10,... | collective-permute-start | bytes 393224 | tf_op jit(solution)/shard_map/ppermute | solution.py:24
  28.5 6.8 %collective-permute-start.16 = (bf16[64,1024]{1,0:T(8,128)(2,1)S(1)}, bf16[64,1024]{1,0:T(8,128)(2,1)S(1)}, u32[]{:S(2)}, u32[]{:S(2)}) collective-permute-start(bf16[64,1024]{1,0:T(8,128)(2,1)S(1)} %get-tuple-element.55), channel_id=1, source_target_pairs={{0,2},{1,5},{2,0},{3,7},{4,6},{5,1},{6,4},{7,3},{8,10},{9,13},{10,... | collective-permute-start | bytes 393224 | tf_op jit(solution)/shard_map/ppermute | solution.py:24
  30.9 4.5 %collective-permute-start.13 = (bf16[512,256]{1,0:T(8,128)(2,1)S(1)}, bf16[512,256]{1,0:T(8,128)(2,1)S(1)}, u32[]{:S(2)}, u32[]{:S(2)}) collective-permute-start(bf16[512,256]{1,0:T(8,128)(2,1)S(1)} %pad_maximum_fusion), channel_id=1, source_target_pairs={{0,1},{1,0},{2,3},{3,2},{4,5},{5,4},{6,7},{7,6},{8,9},{9,8},{10,11... | collective-permute-start | bytes 786440 | tf_op jit(solution)/shard_map/ppermute | solution.py:24
  31.1 10.5 %collective-permute-start.15 = (bf16[64,1024]{1,0:T(8,128)(2,1)S(1)}, bf16[64,1024]{1,0:T(8,128)(2,1)S(1)}, u32[]{:S(2)}, u32[]{:S(2)}) collective-permute-start(bf16[64,1024]{1,0:T(8,128)(2,1)S(1)} %add.35), channel_id=1, source_target_pairs={{0,4},{1,3},{2,6},{3,1},{4,0},{5,7},{6,2},{7,5},{8,12},{9,11},{10,... | collective-permute-start | bytes 393224 | tf_op jit(solution)/shard_map/ppermute | solution.py:24
  33.1 4.3 %collective-permute-start.20 = (bf16[32,1024]{1,0:T(8,128)(2,1)S(1)}, bf16[32,1024]{1,0:T(8,128)(2,1)S(1)}, u32[]{:S(2)}, u32[]{:S(2)}) collective-permute-start(bf16[32,1024]{1,0:T(8,128)(2,1)S(1)} %add.39), channel_id=1, source_target_pairs={{0,4},{1,3},{2,6},{3,1},{4,0},{5,7},{6,2},{7,5},{8,12},{9,11},{10,... | collective-permute-start | bytes 196616 | tf_op jit(solution)/shard_map/ppermute | solution.py:24
  34.2 4.3 %collective-permute-start.18 = (bf16[32,1024]{1,0:T(8,128)(2,1)S(1)}, bf16[32,1024]{1,0:T(8,128)(2,1)S(1)}, u32[]{:S(2)}, u32[]{:S(2)}) collective-permute-start(bf16[32,1024]{1,0:T(8,128)(2,1)S(1)} %add.37), channel_id=1, source_target_pairs={{0,4},{1,3},{2,6},{3,1},{4,0},{5,7},{6,2},{7,5},{8,12},{9,11},{10,... | collective-permute-start | bytes 196616 | tf_op jit(solution)/shard_map/ppermute | solution.py:24
  38.6 6.5 %collective-permute-start.19 = (bf16[32,1024]{1,0:T(8,128)(2,1)S(1)}, bf16[32,1024]{1,0:T(8,128)(2,1)S(1)}, u32[]{:S(2)}, u32[]{:S(2)}) collective-permute-start(bf16[32,1024]{1,0:T(8,128)(2,1)S(1)} %add.38), channel_id=1, source_target_pairs={{0,24},{1,25},{2,26},{3,27},{4,28},{5,29},{6,30},{7,31},{8,16},{9,... | collective-permute-start | bytes 196616 | tf_op jit(solution)/shard_map/ppermute | solution.py:24
  40.9 5.7 %collective-permute-start.21 = (bf16[32,1024]{1,0:T(8,128)(2,1)S(1)}, bf16[32,1024]{1,0:T(8,128)(2,1)S(1)}, u32[]{:S(2)}, u32[]{:S(2)}) collective-permute-start(bf16[32,1024]{1,0:T(8,128)(2,1)S(1)} %add.40), channel_id=1, source_target_pairs={{0,16},{1,17},{2,18},{3,19},{4,20},{5,21},{6,22},{7,23},{8,24},{9,... | collective-permute-start | bytes 196616 | tf_op jit(solution)/shard_map/ppermute | solution.py:24
  41.6 5.1 %collective-permute-start.22 = (bf16[32,1024]{1,0:T(8,128)(2,1)S(1)}, bf16[32,1024]{1,0:T(8,128)(2,1)S(1)}, u32[]{:S(2)}, u32[]{:S(2)}) collective-permute-start(bf16[32,1024]{1,0:T(8,128)(2,1)S(1)} %add.41), channel_id=1, source_target_pairs={{0,8},{1,9},{2,10},{3,11},{4,12},{5,13},{6,14},{7,15},{8,0},{9,1},... | collective-permute-start | bytes 196616 | tf_op jit(solution)/shard_map/ppermute | solution.py:24

commit v5 on v4

--- a/solution.py
+++ b/solution.py
@@ -364,9 +364,10 @@
     output = into_place([own_e0, own_e1, own_l0, own_l1, from_other], place)
 
     got_8 = swap(add(keep_e, rows, rows, got_e[rows:], BF16), ALONG_Z[1])
-    got_24, got_16 = after(got_24, output), after(got_16, output)
+    send_16 = add(keep_l, rows, rows, after(got_16, output), BF16)
+    got_16 = swap(send_16, ALONG_Z[3])
+    got_24 = after(got_24, output, send_16)
     got_24 = swap(add(keep_l, 0, rows, got_24, BF16), ALONG_Z[2])
-    got_16 = swap(add(keep_l, rows, rows, got_16, BF16), ALONG_Z[3])
     mine = keep_e[:rows] + got_e[:rows].astype(F32)
     return output, mine + sum(v.astype(F32) for v in (got_24, got_16, got_8))
 

time: 47.5 us -> 46.6 us (0.981)
  starting transfers between devices: 27.2 us -> 26.6 us
    ppermute x23, starting transfers between devices: 27.2 us -> 26.6 us  [swap(): lax.ppermute(value, AXES, [(i, i ^ masks[i % 2]) for i in range(total)])]
  transfers between devices with their start and end apart: 23 -> 23, of which waited for: 8 -> 7; matrix products, arithmetic and copies ran while one was open for 0% -> 0% of each run, Pallas kernels for 18% -> 19%
where the time goes in v5:
time: 46.6 us; the launch traced here: 46.5 us
  starting transfers between devices  26.6 us (57%)
  Pallas kernels  8.66 us (19%)
  waiting for transfers between devices  7.97 us (17%)
  between operations  1.56 us (3%)
  local copies, waits for them, and re-layouts  0.89 us (2%)
  other arithmetic  0.72 us (2%)
    ppermute x23, starting transfers between devices, swap(): lax.ppermute(value, AXES, [(i, i ^ masks[i % 2]) for i in range(total)])  26.6 us
    ppermute x23, waiting for transfers between devices, swap(): lax.ppermute(value, AXES, [(i, i ^ masks[i % 2]) for i in range(total)])  7.97 us
    pallas_call x4, Pallas kernels, layer(): pl.pallas_call(body, out_shape=[jax.ShapeDtypeStruct((count, nodes), BF16...  3.33 us
    pallas_call x1, Pallas kernels, prepare(): pl.pallas_call(prepare_body, out_shape=[jax.ShapeDtypeStruct((nodes, widt...  2.39 us
    pallas_call x1, Pallas kernels, into_place(): pl.pallas_call(into_place_body, out_shape=jax.ShapeDtypeStruct((parts[0]....  1.79 us
  transfers between devices with their start and end apart: 23, of which 7 were waited for; matrix products, arithmetic and copies ran while one was open for 0% of the time, Pallas kernels for 19%

profile of v5, /device:TPU:0, one launch (start us, length us, event | category | flops | bytes accessed | tf_op | source)
XLA Modules:
  0.0 46.5 jit_solution(17646892366347641827)
XLA Ops:
  0.7 0.5 %collective-permute-start = (s32[1]{0:T(128)}, s32[1]{0:T(128)}, u32[]{:S(2)}, u32[]{:S(2)}) collective-permute-start(s32[1]{0:T(128)} %param.9), channel_id=1, source_target_pairs={{0,1},{1,0},{2,3},{3,2},{4,5},{5,4},{6,7},{7,6},{8,9},{9,8},{10,11... | collective-permute-start | bytes 20 | tf_op jit(solution)/shard_map/ppermute | solution.py:24
  1.2 2.6 %collective-permute-start.1 = (bf16[32,1024]{1,0:T(8,128)(2,1)}, bf16[32,1024]{1,0:T(8,128)(2,1)S(1)}, u32[]{:S(2)}, u32[]{:S(2)}) collective-permute-start(bf16[32,1024]{1,0:T(8,128)(2,1)} %weight.1), channel_id=1, source_target_pairs={{0,2},{1,3},{2,0},{3,1},{4,6},{5,7},{6,4},{7,5},{8,10},{9,11},{10,... | collective-permute-start | bytes 196616 | tf_op jit(solution)/shard_map/ppermute | solution.py:24
  3.8 0.0 collective-permute-done.near_block
  3.8 1.0 %collective-permute-start.3 = (bf16[256,1024]{1,0:T(8,128)(2,1)}, bf16[256,1024]{1,0:T(8,128)(2,1)S(1)}, u32[]{:S(2)}, u32[]{:S(2)}) collective-permute-start(bf16[256,1024]{1,0:T(8,128)(2,1)} %features_in.1), channel_id=1, source_target_pairs={{0,3},{1,2},{2,1},{3,0},{4,7},{5,6},{6,5},{7,4},{8,11},{9,10},{10,... | collective-permute-start | bytes 1572872 | tf_op jit(solution)/shard_map/ppermute | solution.py:24
  4.7 0.3 collective-permute-start.2
  5.0 0.8 %copy-done.4 = bf16[32,1024]{1,0:T(8,128)(2,1)S(1)} copy-done((bf16[32,1024]{1,0:T(8,128)(2,1)S(1)}, bf16[32,1024]{1,0:T(8,128)(2,1)}, u32[]{:S(2)}) %copy-start.4) | copy-done | bytes 65560
  5.9 0.6 %hold.1 = bf16[32,1024]{1,0:T(8,128)(2,1)S(1)} custom-call(bf16[32,1024]{1,0:T(8,128)(2,1)S(1)} %copy-done.4, s32[1]{0:T(128)} %collective-permute-done.near_block), custom_call_target="tpu_custom_call" | custom-call | flops 20000000000 | tf_op jit(solution)/shard_map/hold/pallas_call | solution.py:136
  6.5 0.2 collective-permute-done.1
  6.7 2.9 %collective-permute-start.9 = (bf16[64,1024]{1,0:T(8,128)(2,1)S(1)}, bf16[64,1024]{1,0:T(8,128)(2,1)S(1)}, u32[]{:S(2)}, u32[]{:S(2)}) collective-permute-start(bf16[64,1024]{1,0:T(8,128)(2,1)S(1)} %pad_maximum_fusion.1.refs_0_), channel_id=1, source_target_pairs={{0,16},{1,17},{2,18},{3,19},{4,20},{5,21},{6,22},{7,23},{8,24},{9,... | collective-permute-start | bytes 393224 | tf_op jit(solution)/shard_map/ppermute | solution.py:24
  9.6 1.5 %collective-permute-start.7 = (bf16[64,1024]{1,0:T(8,128)(2,1)S(1)}, bf16[64,1024]{1,0:T(8,128)(2,1)S(1)}, u32[]{:S(2)}, u32[]{:S(2)}) collective-permute-start(bf16[64,1024]{1,0:T(8,128)(2,1)S(1)} %pad_maximum_fusion.1.refs_0_), channel_id=1, source_target_pairs={{0,4},{1,5},{2,6},{3,7},{4,0},{5,1},{6,2},{7,3},{8,12},{9,13},{10,... | collective-permute-start | bytes 393224 | tf_op jit(solution)/shard_map/ppermute | solution.py:24
  11.1 1.5 %collective-permute-start.8 = (bf16[64,1024]{1,0:T(8,128)(2,1)S(1)}, bf16[64,1024]{1,0:T(8,128)(2,1)S(1)}, u32[]{:S(2)}, u32[]{:S(2)}) collective-permute-start(bf16[64,1024]{1,0:T(8,128)(2,1)S(1)} %pad_maximum_fusion.1.refs_0_), channel_id=1, source_target_pairs={{0,12},{1,13},{2,14},{3,15},{4,8},{5,9},{6,10},{7,11},{8,4},{9,5},... | collective-permute-start | bytes 393224 | tf_op jit(solution)/shard_map/ppermute | solution.py:24
  12.6 0.0 collective-permute-done.2.near_block
  12.6 0.5 collective-permute-start.6
  13.8 2.4 %prepare.1 = (f32[256,1024]{1,0:T(8,128)S(1)}, bf16[256,256]{1,0:T(8,128)(2,1)S(1)}, bf16[512,256]{1,0:T(8,128)(2,1)S(1)}, bf16[512,256]{1,0:T(8,128)(2,1)S(1)}, bf16[1024,1024]{1,0:T(8,128)(2,1)S(1)}) custom-call(s32[1]{0:T(128)} %bitcast.me_ref, s32[1,3]{1,0:T(1,128)S(1)} %copy-done.3, s32[1]{0:T(128)S(6)} %copy.8.count, ...), custom_call_target="tpu_custom_call" | custom-call | tf_op jit(solution)/shard_map/prepare/pallas_call | solution.py:202
  16.2 0.0 collective-permute-done.7.refs_2_
  16.2 1.6 %collective-permute-start.12 = (bf16[64,1024]{1,0:T(8,128)(2,1)S(1)}, bf16[64,1024]{1,0:T(8,128)(2,1)S(1)}, u32[]{:S(2)}, u32[]{:S(2)}) collective-permute-start(bf16[64,1024]{1,0:T(8,128)(2,1)S(1)} %collective-permute-done.9.refs_1_), channel_id=1, source_target_pairs={{0,4},{1,5},{2,6},{3,7},{4,0},{5,1},{6,2},{7,3},{8,12},{9,13},{10,... | collective-permute-start | bytes 393224 | tf_op jit(solution)/shard_map/ppermute | solution.py:24
  17.8 2.0 %collective-permute-start.11 = (bf16[64,1024]{1,0:T(8,128)(2,1)S(1)}, bf16[64,1024]{1,0:T(8,128)(2,1)S(1)}, u32[]{:S(2)}, u32[]{:S(2)}) collective-permute-start(bf16[64,1024]{1,0:T(8,128)(2,1)S(1)} %collective-permute-done.9.refs_1_), channel_id=1, source_target_pairs={{0,12},{1,13},{2,14},{3,15},{4,8},{5,9},{6,10},{7,11},{8,4},{9,5},... | collective-permute-start | bytes 393224 | tf_op jit(solution)/shard_map/ppermute | solution.py:24
  19.8 0.3 aggregate.1.refs_0_
  20.1 0.1 collective-permute-start.4
  20.2 0.0 collective-permute-done.8.refs_3_
  20.2 0.5 %collective-permute-start.5 = (bf16[512,256]{1,0:T(8,128)(2,1)S(1)}, bf16[512,256]{1,0:T(8,128)(2,1)S(1)}, u32[]{:S(2)}, u32[]{:S(2)}) collective-permute-start(bf16[512,256]{1,0:T(8,128)(2,1)S(1)} %get-tuple-element.36), channel_id=1, source_target_pairs={{0,1},{1,0},{2,3},{3,2},{4,5},{5,4},{6,7},{7,6},{8,9},{9,8},{10,11... | collective-permute-start | bytes 786440 | tf_op jit(solution)/shard_map/ppermute | solution.py:24
  20.7 0.6 %collective-permute-done.6.refs_1_ = bf16[64,1024]{1,0:T(8,128)(2,1)S(1)} collective-permute-done((bf16[64,1024]{1,0:T(8,128)(2,1)S(1)}, bf16[64,1024]{1,0:T(8,128)(2,1)S(1)}, u32[]{:S(2)}, u32[]{:S(2)}) %collective-permute-start.6) | collective-permute-done | bytes 131104 | tf_op jit(solution)/shard_map/ppermute | solution.py:24
  21.3 1.1 %collective-permute-done.5.refs_3_ = bf16[512,256]{1,0:T(8,128)(2,1)S(1)} collective-permute-done((bf16[512,256]{1,0:T(8,128)(2,1)S(1)}, bf16[512,256]{1,0:T(8,128)(2,1)S(1)}, u32[]{:S(2)}, u32[]{:S(2)}) %collective-permute-start.5) | collective-permute-done | bytes 262176 | tf_op jit(solution)/shard_map/ppermute | solution.py:24
  22.4 0.8 %layer.4 = (bf16[128,256]{1,0:T(8,128)(2,1)S(1)}, bf16[128,256]{1,0:T(8,128)(2,1)S(1)}, bf16[128,1024]{1,0:T(8,128)(2,1)S(1)}) custom-call(bf16[256,1024]{1,0:T(8,128)(2,1)S(1)} %aggregate.1.refs_0_, bf16[256,1024]{1,0:T(8,128)(2,1)S(1)} %collective-permute-done.4.refs_1_, bf16[512,256]{1,0:T(8,128)(2,1)S(1)} %get-tuple-element.34.refs_2_, ...), custom_call_target="tpu_custom_call" | custom-call | flops 20000000000 | tf_op jit(solution)/shard_map/layer/pallas_call | solution.py:67
  23.3 1.5 %collective-permute-start.14 = (bf16[128,1024]{1,0:T(8,128)(2,1)S(1)}, bf16[128,1024]{1,0:T(8,128)(2,1)S(1)}, u32[]{:S(2)}, u32[]{:S(2)}) collective-permute-start(bf16[128,1024]{1,0:T(8,128)(2,1)S(1)} %get-tuple-element.40), channel_id=1, source_target_pairs={{0,2},{1,5},{2,0},{3,7},{4,6},{5,1},{6,4},{7,3},{8,10},{9,13},{10,... | collective-permute-start | bytes 786440 | tf_op jit(solution)/shard_map/ppermute | solution.py:24
  24.7 1.5 %collective-permute-done.10.refs_0_ = bf16[64,1024]{1,0:T(8,128)(2,1)S(1)} collective-permute-done((bf16[64,1024]{1,0:T(8,128)(2,1)S(1)}, bf16[64,1024]{1,0:T(8,128)(2,1)S(1)}, u32[]{:S(2)}, u32[]{:S(2)}) %collective-permute-start.10) | collective-permute-done | bytes 131104 | tf_op jit(solution)/shard_map/ppermute | solution.py:24
  26.2 0.0 collective-permute-done.12.refs_3_
  26.3 0.8 %layer.5 = (bf16[128,256]{1,0:T(8,128)(2,1)S(1)}, bf16[128,256]{1,0:T(8,128)(2,1)S(1)}, bf16[64,1024]{1,0:T(8,128)(2,1)S(1)}, bf16[64,1024]{1,0:T(8,128)(2,1)S(1)}) custom-call(bf16[256,1024]{1,0:T(8,128)(2,1)S(1)} %aggregate.1.refs_0_, bf16[256,1024]{1,0:T(8,128)(2,1)S(1)} %collective-permute-done.4.refs_1_, ...), custom_call_target="tpu_custom_call" | custom-call | flops 20000000000 | tf_op jit(solution)/shard_map/layer/pallas_call | solution.py:67
  27.1 1.4 %collective-permute-start.17 = (bf16[64,1024]{1,0:T(8,128)(2,1)S(1)}, bf16[64,1024]{1,0:T(8,128)(2,1)S(1)}, u32[]{:S(2)}, u32[]{:S(2)}) collective-permute-start(bf16[64,1024]{1,0:T(8,128)(2,1)S(1)} %get-tuple-element.42), channel_id=1, source_target_pairs={{0,2},{1,5},{2,0},{3,7},{4,6},{5,1},{6,4},{7,3},{8,10},{9,13},{10,... | collective-permute-start | bytes 393224 | tf_op jit(solution)/shard_map/ppermute | solution.py:24
  28.5 0.7 %collective-permute-start.16 = (bf16[64,1024]{1,0:T(8,128)(2,1)S(1)}, bf16[64,1024]{1,0:T(8,128)(2,1)S(1)}, u32[]{:S(2)}, u32[]{:S(2)}) collective-permute-start(bf16[64,1024]{1,0:T(8,128)(2,1)S(1)} %get-tuple-element.55), channel_id=1, source_target_pairs={{0,2},{1,5},{2,0},{3,7},{4,6},{5,1},{6,4},{7,3},{8,10},{9,13},{10,... | collective-permute-start | bytes 393224 | tf_op jit(solution)/shard_map/ppermute | solution.py:24
  29.2 0.8 %layer.7 = (bf16[128,256]{1,0:T(8,128)(2,1)S(1)}, bf16[128,256]{1,0:T(8,128)(2,1)S(1)}, f32[128,1024]{1,0:T(8,128)S(1)}) custom-call(bf16[256,1024]{1,0:T(8,128)(2,1)S(1)} %aggregate.1.refs_0_, bf16[256,1024]{1,0:T(8,128)(2,1)S(1)} %collective-permute-done.4.refs_1_, bf16[512,256]{1,0:T(8,128)(2,1)S(1)} %get-tuple-element.34.refs_2_, ...), custom_call_target="tpu_custom_call" | custom-call | flops 20000000000 | tf_op jit(solution)/shard_map/layer/pallas_call | solution.py:67
  30.0 0.8 %layer.6 = (bf16[128,256]{1,0:T(8,128)(2,1)S(1)}, bf16[128,256]{1,0:T(8,128)(2,1)S(1)}, f32[128,1024]{1,0:T(8,128)S(1)}) custom-call(bf16[256,1024]{1,0:T(8,128)(2,1)S(1)} %aggregate.1.refs_0_, bf16[256,1024]{1,0:T(8,128)(2,1)S(1)} %collective-permute-done.4.refs_1_, bf16[512,256]{1,0:T(8,128)(2,1)S(1)} %get-tuple-element.34.refs_2_, ...), custom_call_target="tpu_custom_call" | custom-call | flops 20000000000 | tf_op jit(solution)/shard_map/layer/pallas_call | solution.py:67
  30.9 0.1 collective-permute-start.13
  31.0 0.0 collective-permute-done.14
  31.1 2.0 %collective-permute-start.15 = (bf16[64,1024]{1,0:T(8,128)(2,1)S(1)}, bf16[64,1024]{1,0:T(8,128)(2,1)S(1)}, u32[]{:S(2)}, u32[]{:S(2)}) collective-permute-start(bf16[64,1024]{1,0:T(8,128)(2,1)S(1)} %add.35), channel_id=1, source_target_pairs={{0,4},{1,3},{2,6},{3,1},{4,0},{5,7},{6,2},{7,5},{8,12},{9,11},{10,... | collective-permute-start | bytes 393224 | tf_op jit(solution)/shard_map/ppermute | solution.py:24
  33.1 1.1 %collective-permute-start.19 = (bf16[32,1024]{1,0:T(8,128)(2,1)S(1)}, bf16[32,1024]{1,0:T(8,128)(2,1)S(1)}, u32[]{:S(2)}, u32[]{:S(2)}) collective-permute-start(bf16[32,1024]{1,0:T(8,128)(2,1)S(1)} %add.38), channel_id=1, source_target_pairs={{0,4},{1,3},{2,6},{3,1},{4,0},{5,7},{6,2},{7,5},{8,12},{9,11},{10,... | collective-permute-start | bytes 196616 | tf_op jit(solution)/shard_map/ppermute | solution.py:24
  34.2 1.1 %collective-permute-start.18 = (bf16[32,1024]{1,0:T(8,128)(2,1)S(1)}, bf16[32,1024]{1,0:T(8,128)(2,1)S(1)}, u32[]{:S(2)}, u32[]{:S(2)}) collective-permute-start(bf16[32,1024]{1,0:T(8,128)(2,1)S(1)} %add.37), channel_id=1, source_target_pairs={{0,4},{1,3},{2,6},{3,1},{4,0},{5,7},{6,2},{7,5},{8,12},{9,11},{10,... | collective-permute-start | bytes 196616 | tf_op jit(solution)/shard_map/ppermute | solution.py:24
  35.4 0.0 collective-permute-done.13.refs_4_
  35.4 1.8 %into_place.1 = bf16[256,1024]{1,0:T(8,128)(2,1)} custom-call(bf16[128,256]{1,0:T(8,128)(2,1)S(1)} %get-tuple-element.44.refs_0_, bf16[128,256]{1,0:T(8,128)(2,1)S(1)} %get-tuple-element.45.refs_1_, bf16[128,256]{1,0:T(8,128)(2,1)S(1)} %get-tuple-element.46.refs_2_, bf16[128,256]{1,0:T(8,128)(2,1)S(1)} %get-tuple-element.47.refs_3_, ...), custom_call_target="tpu_custom_call" | custom-call | tf_op jit(solution)/shard_map/into_place/pallas_call | solution.py:283
  37.2 0.3 collective-permute-done.19.got_ref
  37.5 1.3 %collective-permute-start.21 = (bf16[32,1024]{1,0:T(8,128)(2,1)S(1)}, bf16[32,1024]{1,0:T(8,128)(2,1)S(1)}, u32[]{:S(2)}, u32[]{:S(2)}) collective-permute-start(bf16[32,1024]{1,0:T(8,128)(2,1)S(1)} %add.39), channel_id=1, source_target_pairs={{0,16},{1,17},{2,18},{3,19},{4,20},{5,21},{6,22},{7,23},{8,24},{9,... | collective-permute-start | bytes 196616 | tf_op jit(solution)/shard_map/ppermute | solution.py:24
  38.8 0.0 collective-permute-done.18.got_ref
  38.8 2.5 %collective-permute-start.20 = (bf16[32,1024]{1,0:T(8,128)(2,1)S(1)}, bf16[32,1024]{1,0:T(8,128)(2,1)S(1)}, u32[]{:S(2)}, u32[]{:S(2)}) collective-permute-start(bf16[32,1024]{1,0:T(8,128)(2,1)S(1)} %add.40), channel_id=1, source_target_pairs={{0,24},{1,25},{2,26},{3,27},{4,28},{5,29},{6,30},{7,31},{8,16},{9,... | collective-permute-start | bytes 196616 | tf_op jit(solution)/shard_map/ppermute | solution.py:24
  41.4 0.1 collective-permute-start.22
  41.5 3.6 %collective-permute-done.20 = bf16[32,1024]{1,0:T(8,128)(2,1)S(1)} collective-permute-done((bf16[32,1024]{1,0:T(8,128)(2,1)S(1)}, bf16[32,1024]{1,0:T(8,128)(2,1)S(1)}, u32[]{:S(2)}, u32[]{:S(2)}) %collective-permute-start.20) | collective-permute-done | bytes 65568 | tf_op jit(solution)/shard_map/ppermute | solution.py:24
  45.1 0.0 collective-permute-done.21
  45.1 0.7 %collective-permute-done.22 = bf16[32,1024]{1,0:T(8,128)(2,1)S(1)} collective-permute-done((bf16[32,1024]{1,0:T(8,128)(2,1)S(1)}, bf16[32,1024]{1,0:T(8,128)(2,1)S(1)}, u32[]{:S(2)}, u32[]{:S(2)}) %collective-permute-start.22) | collective-permute-done | bytes 65568 | tf_op jit(solution)/shard_map/ppermute | solution.py:24
  45.8 0.7 %fusion = f32[32,1024]{1,0:T(8,128)} fusion(f32[64,1024]{1,0:T(8,128)S(1)} %add.34.kept_ref, bf16[32,1024]{1,0:T(8,128)(2,1)S(1)} %collective-permute-done.22, bf16[32,1024]{1,0:T(8,128)(2,1)S(1)} %collective-permute-done.21, bf16[32,1024]{1,0:T(8,128)(2,1)S(1)} %collective-permute-done.20, bf16[64,1024]{1,0:T(8,128)(2,1)S(1)} %collective-permute-done.15), kind=kLoop, calls=%fused_computation.2 | loop fusion | flops 262144 | bytes 524288 | tf_op jit(solution)/shard_map/add | solution.py:372
  (32 shorter events, 0.3 us)
Async XLA Ops:
  0.6 13.1 %copy-start.1 = (bf16[256,1024]{1,0:T(8,128)(2,1)S(1)}, bf16[256,1024]{1,0:T(8,128)(2,1)}, u32[]{:S(2)}) copy-start(bf16[256,1024]{1,0:T(8,128)(2,1)} %features_in.1) | copy-start | bytes 1572868
  0.6 13.1 %copy-start = (bf16[256,1024]{1,0:T(8,128)(2,1)S(1)}, bf16[256,1024]{1,0:T(8,128)(2,1)}, u32[]{:S(2)}) copy-start(bf16[256,1024]{1,0:T(8,128)(2,1)} %cotangent_in.1) | copy-start | bytes 1572868
  0.7 13.1 %copy-start.3 = (s32[1,3]{1,0:T(1,128)S(1)}, s32[1,3]{1,0:T(1,128)}, u32[]{:S(2)}) copy-start(s32[1,3]{1,0:T(1,128)} %cols.1) | copy-start | bytes 40
  0.7 13.1 %copy-start.2 = (bf16[1,3,256,256]{3,2,1,0:T(8,128)(2,1)S(1)}, bf16[1,3,256,256]{3,2,1,0:T(8,128)(2,1)}, u32[]{:S(2)}) copy-start(bf16[1,3,256,256]{3,2,1,0:T(8,128)(2,1)} %tiles_in.1) | copy-start | bytes 1179652
  0.7 3.1 %collective-permute-start = (s32[1]{0:T(128)}, s32[1]{0:T(128)}, u32[]{:S(2)}, u32[]{:S(2)}) collective-permute-start(s32[1]{0:T(128)} %param.9), channel_id=1, source_target_pairs={{0,1},{1,0},{2,3},{3,2},{4,5},{5,4},{6,7},{7,6},{8,9},{9,8},{10,11... | collective-permute-start | bytes 20 | tf_op jit(solution)/shard_map/ppermute | solution.py:24
  1.2 5.5 %collective-permute-start.1 = (bf16[32,1024]{1,0:T(8,128)(2,1)}, bf16[32,1024]{1,0:T(8,128)(2,1)S(1)}, u32[]{:S(2)}, u32[]{:S(2)}) collective-permute-start(bf16[32,1024]{1,0:T(8,128)(2,1)} %weight.1), channel_id=1, source_target_pairs={{0,2},{1,3},{2,0},{3,1},{4,6},{5,7},{6,4},{7,5},{8,10},{9,11},{10,... | collective-permute-start | bytes 196616 | tf_op jit(solution)/shard_map/ppermute | solution.py:24
  3.8 16.0 %collective-permute-start.3 = (bf16[256,1024]{1,0:T(8,128)(2,1)}, bf16[256,1024]{1,0:T(8,128)(2,1)S(1)}, u32[]{:S(2)}, u32[]{:S(2)}) collective-permute-start(bf16[256,1024]{1,0:T(8,128)(2,1)} %features_in.1), channel_id=1, source_target_pairs={{0,3},{1,2},{2,1},{3,0},{4,7},{5,6},{6,5},{7,4},{8,11},{9,10},{10,... | collective-permute-start | bytes 1572872 | tf_op jit(solution)/shard_map/ppermute | solution.py:24
  4.7 7.9 %collective-permute-start.2 = (bf16[256,1024]{1,0:T(8,128)(2,1)}, bf16[256,1024]{1,0:T(8,128)(2,1)S(1)}, u32[]{:S(2)}, u32[]{:S(2)}) collective-permute-start(bf16[256,1024]{1,0:T(8,128)(2,1)} %features_in.1), channel_id=1, source_target_pairs={{0,1},{1,0},{2,3},{3,2},{4,5},{5,4},{6,7},{7,6},{8,9},{9,8},{10,11... | collective-permute-start | bytes 1572872 | tf_op jit(solution)/shard_map/ppermute | solution.py:24
  5.0 0.8 %copy-start.4 = (bf16[32,1024]{1,0:T(8,128)(2,1)S(1)}, bf16[32,1024]{1,0:T(8,128)(2,1)}, u32[]{:S(2)}) copy-start(bf16[32,1024]{1,0:T(8,128)(2,1)} %weight.1) | copy-start | bytes 196612
  6.7 9.5 %collective-permute-start.9 = (bf16[64,1024]{1,0:T(8,128)(2,1)S(1)}, bf16[64,1024]{1,0:T(8,128)(2,1)S(1)}, u32[]{:S(2)}, u32[]{:S(2)}) collective-permute-start(bf16[64,1024]{1,0:T(8,128)(2,1)S(1)} %pad_maximum_fusion.1.refs_0_), channel_id=1, source_target_pairs={{0,16},{1,17},{2,18},{3,19},{4,20},{5,21},{6,22},{7,23},{8,24},{9,... | collective-permute-start | bytes 393224 | tf_op jit(solution)/shard_map/ppermute | solution.py:24
  9.6 6.6 %collective-permute-start.7 = (bf16[64,1024]{1,0:T(8,128)(2,1)S(1)}, bf16[64,1024]{1,0:T(8,128)(2,1)S(1)}, u32[]{:S(2)}, u32[]{:S(2)}) collective-permute-start(bf16[64,1024]{1,0:T(8,128)(2,1)S(1)} %pad_maximum_fusion.1.refs_0_), channel_id=1, source_target_pairs={{0,4},{1,5},{2,6},{3,7},{4,0},{5,1},{6,2},{7,3},{8,12},{9,13},{10,... | collective-permute-start | bytes 393224 | tf_op jit(solution)/shard_map/ppermute | solution.py:24
  11.1 9.0 %collective-permute-start.8 = (bf16[64,1024]{1,0:T(8,128)(2,1)S(1)}, bf16[64,1024]{1,0:T(8,128)(2,1)S(1)}, u32[]{:S(2)}, u32[]{:S(2)}) collective-permute-start(bf16[64,1024]{1,0:T(8,128)(2,1)S(1)} %pad_maximum_fusion.1.refs_0_), channel_id=1, source_target_pairs={{0,12},{1,13},{2,14},{3,15},{4,8},{5,9},{6,10},{7,11},{8,4},{9,5},... | collective-permute-start | bytes 393224 | tf_op jit(solution)/shard_map/ppermute | solution.py:24
  12.6 8.6 %collective-permute-start.6 = (bf16[64,1024]{1,0:T(8,128)(2,1)S(1)}, bf16[64,1024]{1,0:T(8,128)(2,1)S(1)}, u32[]{:S(2)}, u32[]{:S(2)}) collective-permute-start(bf16[64,1024]{1,0:T(8,128)(2,1)S(1)} %pad_maximum_fusion.1.refs_0_), channel_id=1, source_target_pairs={{0,8},{1,9},{2,10},{3,11},{4,12},{5,13},{6,14},{7,15},{8,0},{9,1},... | collective-permute-start | bytes 393224 | tf_op jit(solution)/shard_map/ppermute | solution.py:24
  16.2 10.0 %collective-permute-start.12 = (bf16[64,1024]{1,0:T(8,128)(2,1)S(1)}, bf16[64,1024]{1,0:T(8,128)(2,1)S(1)}, u32[]{:S(2)}, u32[]{:S(2)}) collective-permute-start(bf16[64,1024]{1,0:T(8,128)(2,1)S(1)} %collective-permute-done.9.refs_1_), channel_id=1, source_target_pairs={{0,4},{1,5},{2,6},{3,7},{4,0},{5,1},{6,2},{7,3},{8,12},{9,13},{10,... | collective-permute-start | bytes 393224 | tf_op jit(solution)/shard_map/ppermute | solution.py:24
  17.8 8.4 %collective-permute-start.11 = (bf16[64,1024]{1,0:T(8,128)(2,1)S(1)}, bf16[64,1024]{1,0:T(8,128)(2,1)S(1)}, u32[]{:S(2)}, u32[]{:S(2)}) collective-permute-start(bf16[64,1024]{1,0:T(8,128)(2,1)S(1)} %collective-permute-done.9.refs_1_), channel_id=1, source_target_pairs={{0,12},{1,13},{2,14},{3,15},{4,8},{5,9},{6,10},{7,11},{8,4},{9,5},... | collective-permute-start | bytes 393224 | tf_op jit(solution)/shard_map/ppermute | solution.py:24
  20.1 2.4 %collective-permute-start.4 = (bf16[256,1024]{1,0:T(8,128)(2,1)S(1)}, bf16[256,1024]{1,0:T(8,128)(2,1)S(1)}, u32[]{:S(2)}, u32[]{:S(2)}) collective-permute-start(bf16[256,1024]{1,0:T(8,128)(2,1)S(1)} %aggregate.1.refs_0_), channel_id=1, source_target_pairs={{0,1},{1,0},{2,3},{3,2},{4,5},{5,4},{6,7},{7,6},{8,9},{9,8},{10,11... | collective-permute-start | bytes 1572872 | tf_op jit(solution)/shard_map/ppermute | solution.py:24
  20.2 2.3 %collective-permute-start.5 = (bf16[512,256]{1,0:T(8,128)(2,1)S(1)}, bf16[512,256]{1,0:T(8,128)(2,1)S(1)}, u32[]{:S(2)}, u32[]{:S(2)}) collective-permute-start(bf16[512,256]{1,0:T(8,128)(2,1)S(1)} %get-tuple-element.36), channel_id=1, source_target_pairs={{0,1},{1,0},{2,3},{3,2},{4,5},{5,4},{6,7},{7,6},{8,9},{9,8},{10,11... | collective-permute-start | bytes 786440 | tf_op jit(solution)/shard_map/ppermute | solution.py:24
  21.3 5.0 %collective-permute-start.10 = (bf16[64,1024]{1,0:T(8,128)(2,1)S(1)}, bf16[64,1024]{1,0:T(8,128)(2,1)S(1)}, u32[]{:S(2)}, u32[]{:S(2)}) collective-permute-start(bf16[64,1024]{1,0:T(8,128)(2,1)S(1)} %collective-permute-done.9.refs_1_), channel_id=1, source_target_pairs={{0,8},{1,9},{2,10},{3,11},{4,12},{5,13},{6,14},{7,15},{8,0},{9,1},... | collective-permute-start | bytes 393224 | tf_op jit(solution)/shard_map/ppermute | solution.py:24
  23.3 7.7 %collective-permute-start.14 = (bf16[128,1024]{1,0:T(8,128)(2,1)S(1)}, bf16[128,1024]{1,0:T(8,128)(2,1)S(1)}, u32[]{:S(2)}, u32[]{:S(2)}) collective-permute-start(bf16[128,1024]{1,0:T(8,128)(2,1)S(1)} %get-tuple-element.40), channel_id=1, source_target_pairs={{0,2},{1,5},{2,0},{3,7},{4,6},{5,1},{6,4},{7,3},{8,10},{9,13},{10,... | collective-permute-start | bytes 786440 | tf_op jit(solution)/shard_map/ppermute | solution.py:24
  27.1 6.0 %collective-permute-start.17 = (bf16[64,1024]{1,0:T(8,128)(2,1)S(1)}, bf16[64,1024]{1,0:T(8,128)(2,1)S(1)}, u32[]{:S(2)}, u32[]{:S(2)}) collective-permute-start(bf16[64,1024]{1,0:T(8,128)(2,1)S(1)} %get-tuple-element.42), channel_id=1, source_target_pairs={{0,2},{1,5},{2,0},{3,7},{4,6},{5,1},{6,4},{7,3},{8,10},{9,13},{10,... | collective-permute-start | bytes 393224 | tf_op jit(solution)/shard_map/ppermute | solution.py:24
  28.5 6.8 %collective-permute-start.16 = (bf16[64,1024]{1,0:T(8,128)(2,1)S(1)}, bf16[64,1024]{1,0:T(8,128)(2,1)S(1)}, u32[]{:S(2)}, u32[]{:S(2)}) collective-permute-start(bf16[64,1024]{1,0:T(8,128)(2,1)S(1)} %get-tuple-element.55), channel_id=1, source_target_pairs={{0,2},{1,5},{2,0},{3,7},{4,6},{5,1},{6,4},{7,3},{8,10},{9,13},{10,... | collective-permute-start | bytes 393224 | tf_op jit(solution)/shard_map/ppermute | solution.py:24
  30.9 4.5 %collective-permute-start.13 = (bf16[512,256]{1,0:T(8,128)(2,1)S(1)}, bf16[512,256]{1,0:T(8,128)(2,1)S(1)}, u32[]{:S(2)}, u32[]{:S(2)}) collective-permute-start(bf16[512,256]{1,0:T(8,128)(2,1)S(1)} %pad_maximum_fusion), channel_id=1, source_target_pairs={{0,1},{1,0},{2,3},{3,2},{4,5},{5,4},{6,7},{7,6},{8,9},{9,8},{10,11... | collective-permute-start | bytes 786440 | tf_op jit(solution)/shard_map/ppermute | solution.py:24
  31.1 10.3 %collective-permute-start.15 = (bf16[64,1024]{1,0:T(8,128)(2,1)S(1)}, bf16[64,1024]{1,0:T(8,128)(2,1)S(1)}, u32[]{:S(2)}, u32[]{:S(2)}) collective-permute-start(bf16[64,1024]{1,0:T(8,128)(2,1)S(1)} %add.35), channel_id=1, source_target_pairs={{0,4},{1,3},{2,6},{3,1},{4,0},{5,7},{6,2},{7,5},{8,12},{9,11},{10,... | collective-permute-start | bytes 393224 | tf_op jit(solution)/shard_map/ppermute | solution.py:24
  33.1 4.3 %collective-permute-start.19 = (bf16[32,1024]{1,0:T(8,128)(2,1)S(1)}, bf16[32,1024]{1,0:T(8,128)(2,1)S(1)}, u32[]{:S(2)}, u32[]{:S(2)}) collective-permute-start(bf16[32,1024]{1,0:T(8,128)(2,1)S(1)} %add.38), channel_id=1, source_target_pairs={{0,4},{1,3},{2,6},{3,1},{4,0},{5,7},{6,2},{7,5},{8,12},{9,11},{10,... | collective-permute-start | bytes 196616 | tf_op jit(solution)/shard_map/ppermute | solution.py:24
  34.2 4.6 %collective-permute-start.18 = (bf16[32,1024]{1,0:T(8,128)(2,1)S(1)}, bf16[32,1024]{1,0:T(8,128)(2,1)S(1)}, u32[]{:S(2)}, u32[]{:S(2)}) collective-permute-start(bf16[32,1024]{1,0:T(8,128)(2,1)S(1)} %add.37), channel_id=1, source_target_pairs={{0,4},{1,3},{2,6},{3,1},{4,0},{5,7},{6,2},{7,5},{8,12},{9,11},{10,... | collective-permute-start | bytes 196616 | tf_op jit(solution)/shard_map/ppermute | solution.py:24
  37.5 7.6 %collective-permute-start.21 = (bf16[32,1024]{1,0:T(8,128)(2,1)S(1)}, bf16[32,1024]{1,0:T(8,128)(2,1)S(1)}, u32[]{:S(2)}, u32[]{:S(2)}) collective-permute-start(bf16[32,1024]{1,0:T(8,128)(2,1)S(1)} %add.39), channel_id=1, source_target_pairs={{0,16},{1,17},{2,18},{3,19},{4,20},{5,21},{6,22},{7,23},{8,24},{9,... | collective-permute-start | bytes 196616 | tf_op jit(solution)/shard_map/ppermute | solution.py:24
  38.8 6.2 %collective-permute-start.20 = (bf16[32,1024]{1,0:T(8,128)(2,1)S(1)}, bf16[32,1024]{1,0:T(8,128)(2,1)S(1)}, u32[]{:S(2)}, u32[]{:S(2)}) collective-permute-start(bf16[32,1024]{1,0:T(8,128)(2,1)S(1)} %add.40), channel_id=1, source_target_pairs={{0,24},{1,25},{2,26},{3,27},{4,28},{5,29},{6,30},{7,31},{8,16},{9,... | collective-permute-start | bytes 196616 | tf_op jit(solution)/shard_map/ppermute | solution.py:24
  41.4 4.4 %collective-permute-start.22 = (bf16[32,1024]{1,0:T(8,128)(2,1)S(1)}, bf16[32,1024]{1,0:T(8,128)(2,1)S(1)}, u32[]{:S(2)}, u32[]{:S(2)}) collective-permute-start(bf16[32,1024]{1,0:T(8,128)(2,1)S(1)} %add.41), channel_id=1, source_target_pairs={{0,8},{1,9},{2,10},{3,11},{4,12},{5,13},{6,14},{7,15},{8,0},{9,1},... | collective-permute-start | bytes 196616 | tf_op jit(solution)/shard_map/ppermute | solution.py:24

commit v6 on v4

--- a/solution.py
+++ b/solution.py
@@ -364,8 +364,9 @@
     output = into_place([own_e0, own_e1, own_l0, own_l1, from_other], place)
 
     got_8 = swap(add(keep_e, rows, rows, got_e[rows:], BF16), ALONG_Z[1])
-    got_24, got_16 = after(got_24, output), after(got_16, output)
-    got_24 = swap(add(keep_l, 0, rows, got_24, BF16), ALONG_Z[2])
+    send_24 = add(keep_l, 0, rows, after(got_24, output), BF16)
+    got_24 = swap(send_24, ALONG_Z[2])
+    got_16 = after(got_16, output, send_24)
     got_16 = swap(add(keep_l, rows, rows, got_16, BF16), ALONG_Z[3])
     mine = keep_e[:rows] + got_e[:rows].astype(F32)
     return output, mine + sum(v.astype(F32) for v in (got_24, got_16, got_8))

time: 47.5 us -> 46.6 us (0.981)
  waiting for transfers between devices: 8.29 us -> 7.32 us
    ppermute x23, waiting for transfers between devices: 8.29 us -> 7.32 us  [swap(): lax.ppermute(value, AXES, [(i, i ^ masks[i % 2]) for i in range(total)])]
  transfers between devices with their start and end apart: 23 -> 23, of which waited for: 8 -> 6; matrix products, arithmetic and copies ran while one was open for 0% -> 0% of each run, Pallas kernels for 18% -> 19%
where the time goes in v6:
time: 46.6 us; the launch traced here: 46.4 us
  starting transfers between devices  27.3 us (59%)
  Pallas kernels  8.66 us (19%)
  waiting for transfers between devices  7.32 us (16%)
  between operations  1.56 us (3%)
  local copies, waits for them, and re-layouts  0.89 us (2%)
  other arithmetic  0.73 us (2%)
    ppermute x23, starting transfers between devices, swap(): lax.ppermute(value, AXES, [(i, i ^ masks[i % 2]) for i in range(total)])  27.3 us
    ppermute x23, waiting for transfers between devices, swap(): lax.ppermute(value, AXES, [(i, i ^ masks[i % 2]) for i in range(total)])  7.32 us
    pallas_call x4, Pallas kernels, layer(): pl.pallas_call(body, out_shape=[jax.ShapeDtypeStruct((count, nodes), BF16...  3.33 us
    pallas_call x1, Pallas kernels, prepare(): pl.pallas_call(prepare_body, out_shape=[jax.ShapeDtypeStruct((nodes, widt...  2.39 us
    pallas_call x1, Pallas kernels, into_place(): pl.pallas_call(into_place_body, out_shape=jax.ShapeDtypeStruct((parts[0]....  1.79 us
  transfers between devices with their start and end apart: 23, of which 6 were waited for; matrix products, arithmetic and copies ran while one was open for 0% of the time, Pallas kernels for 19%

profile of v6, /device:TPU:0, one launch (start us, length us, event | category | flops | bytes accessed | tf_op | source)
XLA Modules:
  0.0 46.4 jit_solution(5195835688098428896)
XLA Ops:
  0.7 0.5 %collective-permute-start = (s32[1]{0:T(128)}, s32[1]{0:T(128)}, u32[]{:S(2)}, u32[]{:S(2)}) collective-permute-start(s32[1]{0:T(128)} %param.9), channel_id=1, source_target_pairs={{0,1},{1,0},{2,3},{3,2},{4,5},{5,4},{6,7},{7,6},{8,9},{9,8},{10,11... | collective-permute-start | bytes 20 | tf_op jit(solution)/shard_map/ppermute | solution.py:24
  1.2 2.6 %collective-permute-start.1 = (bf16[32,1024]{1,0:T(8,128)(2,1)}, bf16[32,1024]{1,0:T(8,128)(2,1)S(1)}, u32[]{:S(2)}, u32[]{:S(2)}) collective-permute-start(bf16[32,1024]{1,0:T(8,128)(2,1)} %weight.1), channel_id=1, source_target_pairs={{0,2},{1,3},{2,0},{3,1},{4,6},{5,7},{6,4},{7,5},{8,10},{9,11},{10,... | collective-permute-start | bytes 196616 | tf_op jit(solution)/shard_map/ppermute | solution.py:24
  3.8 0.0 collective-permute-done.near_block
  3.8 1.0 %collective-permute-start.3 = (bf16[256,1024]{1,0:T(8,128)(2,1)}, bf16[256,1024]{1,0:T(8,128)(2,1)S(1)}, u32[]{:S(2)}, u32[]{:S(2)}) collective-permute-start(bf16[256,1024]{1,0:T(8,128)(2,1)} %features_in.1), channel_id=1, source_target_pairs={{0,3},{1,2},{2,1},{3,0},{4,7},{5,6},{6,5},{7,4},{8,11},{9,10},{10,... | collective-permute-start | bytes 1572872 | tf_op jit(solution)/shard_map/ppermute | solution.py:24
  4.7 0.3 collective-permute-start.2
  5.0 0.8 %copy-done.4 = bf16[32,1024]{1,0:T(8,128)(2,1)S(1)} copy-done((bf16[32,1024]{1,0:T(8,128)(2,1)S(1)}, bf16[32,1024]{1,0:T(8,128)(2,1)}, u32[]{:S(2)}) %copy-start.4) | copy-done | bytes 65560
  5.9 0.6 %hold.1 = bf16[32,1024]{1,0:T(8,128)(2,1)S(1)} custom-call(bf16[32,1024]{1,0:T(8,128)(2,1)S(1)} %copy-done.4, s32[1]{0:T(128)} %collective-permute-done.near_block), custom_call_target="tpu_custom_call" | custom-call | flops 20000000000 | tf_op jit(solution)/shard_map/hold/pallas_call | solution.py:136
  6.5 0.2 collective-permute-done.1
  6.7 2.9 %collective-permute-start.9 = (bf16[64,1024]{1,0:T(8,128)(2,1)S(1)}, bf16[64,1024]{1,0:T(8,128)(2,1)S(1)}, u32[]{:S(2)}, u32[]{:S(2)}) collective-permute-start(bf16[64,1024]{1,0:T(8,128)(2,1)S(1)} %pad_maximum_fusion.1.refs_0_), channel_id=1, source_target_pairs={{0,16},{1,17},{2,18},{3,19},{4,20},{5,21},{6,22},{7,23},{8,24},{9,... | collective-permute-start | bytes 393224 | tf_op jit(solution)/shard_map/ppermute | solution.py:24
  9.6 1.5 %collective-permute-start.7 = (bf16[64,1024]{1,0:T(8,128)(2,1)S(1)}, bf16[64,1024]{1,0:T(8,128)(2,1)S(1)}, u32[]{:S(2)}, u32[]{:S(2)}) collective-permute-start(bf16[64,1024]{1,0:T(8,128)(2,1)S(1)} %pad_maximum_fusion.1.refs_0_), channel_id=1, source_target_pairs={{0,4},{1,5},{2,6},{3,7},{4,0},{5,1},{6,2},{7,3},{8,12},{9,13},{10,... | collective-permute-start | bytes 393224 | tf_op jit(solution)/shard_map/ppermute | solution.py:24
  11.1 1.5 %collective-permute-start.8 = (bf16[64,1024]{1,0:T(8,128)(2,1)S(1)}, bf16[64,1024]{1,0:T(8,128)(2,1)S(1)}, u32[]{:S(2)}, u32[]{:S(2)}) collective-permute-start(bf16[64,1024]{1,0:T(8,128)(2,1)S(1)} %pad_maximum_fusion.1.refs_0_), channel_id=1, source_target_pairs={{0,12},{1,13},{2,14},{3,15},{4,8},{5,9},{6,10},{7,11},{8,4},{9,5},... | collective-permute-start | bytes 393224 | tf_op jit(solution)/shard_map/ppermute | solution.py:24
  12.6 0.5 collective-permute-start.6
  13.8 2.4 %prepare.1 = (f32[256,1024]{1,0:T(8,128)S(1)}, bf16[256,256]{1,0:T(8,128)(2,1)S(1)}, bf16[512,256]{1,0:T(8,128)(2,1)S(1)}, bf16[512,256]{1,0:T(8,128)(2,1)S(1)}, bf16[1024,1024]{1,0:T(8,128)(2,1)S(1)}) custom-call(s32[1]{0:T(128)} %bitcast.me_ref, s32[1,3]{1,0:T(1,128)S(1)} %copy-done.3, s32[1]{0:T(128)S(6)} %copy.8.count, ...), custom_call_target="tpu_custom_call" | custom-call | tf_op jit(solution)/shard_map/prepare/pallas_call | solution.py:202
  16.2 0.0 collective-permute-done.9.refs_1_
  16.2 1.6 %collective-permute-start.12 = (bf16[64,1024]{1,0:T(8,128)(2,1)S(1)}, bf16[64,1024]{1,0:T(8,128)(2,1)S(1)}, u32[]{:S(2)}, u32[]{:S(2)}) collective-permute-start(bf16[64,1024]{1,0:T(8,128)(2,1)S(1)} %collective-permute-done.9.refs_1_), channel_id=1, source_target_pairs={{0,4},{1,5},{2,6},{3,7},{4,0},{5,1},{6,2},{7,3},{8,12},{9,13},{10,... | collective-permute-start | bytes 393224 | tf_op jit(solution)/shard_map/ppermute | solution.py:24
  17.8 2.0 %collective-permute-start.11 = (bf16[64,1024]{1,0:T(8,128)(2,1)S(1)}, bf16[64,1024]{1,0:T(8,128)(2,1)S(1)}, u32[]{:S(2)}, u32[]{:S(2)}) collective-permute-start(bf16[64,1024]{1,0:T(8,128)(2,1)S(1)} %collective-permute-done.9.refs_1_), channel_id=1, source_target_pairs={{0,12},{1,13},{2,14},{3,15},{4,8},{5,9},{6,10},{7,11},{8,4},{9,5},... | collective-permute-start | bytes 393224 | tf_op jit(solution)/shard_map/ppermute | solution.py:24
  19.8 0.0 collective-permute-done.3.block
  19.8 0.3 aggregate.1.refs_0_
  20.1 0.1 collective-permute-start.4
  20.2 0.0 collective-permute-done.8.refs_3_
  20.2 0.5 %collective-permute-start.5 = (bf16[512,256]{1,0:T(8,128)(2,1)S(1)}, bf16[512,256]{1,0:T(8,128)(2,1)S(1)}, u32[]{:S(2)}, u32[]{:S(2)}) collective-permute-start(bf16[512,256]{1,0:T(8,128)(2,1)S(1)} %get-tuple-element.36), channel_id=1, source_target_pairs={{0,1},{1,0},{2,3},{3,2},{4,5},{5,4},{6,7},{7,6},{8,9},{9,8},{10,11... | collective-permute-start | bytes 786440 | tf_op jit(solution)/shard_map/ppermute | solution.py:24
  20.7 0.6 %collective-permute-done.6.refs_1_ = bf16[64,1024]{1,0:T(8,128)(2,1)S(1)} collective-permute-done((bf16[64,1024]{1,0:T(8,128)(2,1)S(1)}, bf16[64,1024]{1,0:T(8,128)(2,1)S(1)}, u32[]{:S(2)}, u32[]{:S(2)}) %collective-permute-start.6) | collective-permute-done | bytes 131104 | tf_op jit(solution)/shard_map/ppermute | solution.py:24
  21.3 1.1 %collective-permute-done.5.refs_3_ = bf16[512,256]{1,0:T(8,128)(2,1)S(1)} collective-permute-done((bf16[512,256]{1,0:T(8,128)(2,1)S(1)}, bf16[512,256]{1,0:T(8,128)(2,1)S(1)}, u32[]{:S(2)}, u32[]{:S(2)}) %collective-permute-start.5) | collective-permute-done | bytes 262176 | tf_op jit(solution)/shard_map/ppermute | solution.py:24
  22.4 0.8 %layer.4 = (bf16[128,256]{1,0:T(8,128)(2,1)S(1)}, bf16[128,256]{1,0:T(8,128)(2,1)S(1)}, bf16[128,1024]{1,0:T(8,128)(2,1)S(1)}) custom-call(bf16[256,1024]{1,0:T(8,128)(2,1)S(1)} %aggregate.1.refs_0_, bf16[256,1024]{1,0:T(8,128)(2,1)S(1)} %collective-permute-done.4.refs_1_, bf16[512,256]{1,0:T(8,128)(2,1)S(1)} %get-tuple-element.34.refs_2_, ...), custom_call_target="tpu_custom_call" | custom-call | flops 20000000000 | tf_op jit(solution)/shard_map/layer/pallas_call | solution.py:67
  23.3 1.5 %collective-permute-start.14 = (bf16[128,1024]{1,0:T(8,128)(2,1)S(1)}, bf16[128,1024]{1,0:T(8,128)(2,1)S(1)}, u32[]{:S(2)}, u32[]{:S(2)}) collective-permute-start(bf16[128,1024]{1,0:T(8,128)(2,1)S(1)} %get-tuple-element.40), channel_id=1, source_target_pairs={{0,2},{1,5},{2,0},{3,7},{4,6},{5,1},{6,4},{7,3},{8,10},{9,13},{10,... | collective-permute-start | bytes 786440 | tf_op jit(solution)/shard_map/ppermute | solution.py:24
  24.7 1.5 %collective-permute-done.10.refs_0_ = bf16[64,1024]{1,0:T(8,128)(2,1)S(1)} collective-permute-done((bf16[64,1024]{1,0:T(8,128)(2,1)S(1)}, bf16[64,1024]{1,0:T(8,128)(2,1)S(1)}, u32[]{:S(2)}, u32[]{:S(2)}) %collective-permute-start.10) | collective-permute-done | bytes 131104 | tf_op jit(solution)/shard_map/ppermute | solution.py:24
  26.2 0.0 collective-permute-done.11.refs_2_
  26.3 0.8 %layer.5 = (bf16[128,256]{1,0:T(8,128)(2,1)S(1)}, bf16[128,256]{1,0:T(8,128)(2,1)S(1)}, bf16[64,1024]{1,0:T(8,128)(2,1)S(1)}, bf16[64,1024]{1,0:T(8,128)(2,1)S(1)}) custom-call(bf16[256,1024]{1,0:T(8,128)(2,1)S(1)} %aggregate.1.refs_0_, bf16[256,1024]{1,0:T(8,128)(2,1)S(1)} %collective-permute-done.4.refs_1_, ...), custom_call_target="tpu_custom_call" | custom-call | flops 20000000000 | tf_op jit(solution)/shard_map/layer/pallas_call | solution.py:67
  27.1 1.4 %collective-permute-start.17 = (bf16[64,1024]{1,0:T(8,128)(2,1)S(1)}, bf16[64,1024]{1,0:T(8,128)(2,1)S(1)}, u32[]{:S(2)}, u32[]{:S(2)}) collective-permute-start(bf16[64,1024]{1,0:T(8,128)(2,1)S(1)} %get-tuple-element.42), channel_id=1, source_target_pairs={{0,2},{1,5},{2,0},{3,7},{4,6},{5,1},{6,4},{7,3},{8,10},{9,13},{10,... | collective-permute-start | bytes 393224 | tf_op jit(solution)/shard_map/ppermute | solution.py:24
  28.5 0.7 %collective-permute-start.16 = (bf16[64,1024]{1,0:T(8,128)(2,1)S(1)}, bf16[64,1024]{1,0:T(8,128)(2,1)S(1)}, u32[]{:S(2)}, u32[]{:S(2)}) collective-permute-start(bf16[64,1024]{1,0:T(8,128)(2,1)S(1)} %get-tuple-element.55), channel_id=1, source_target_pairs={{0,2},{1,5},{2,0},{3,7},{4,6},{5,1},{6,4},{7,3},{8,10},{9,13},{10,... | collective-permute-start | bytes 393224 | tf_op jit(solution)/shard_map/ppermute | solution.py:24
  29.2 0.8 %layer.7 = (bf16[128,256]{1,0:T(8,128)(2,1)S(1)}, bf16[128,256]{1,0:T(8,128)(2,1)S(1)}, f32[128,1024]{1,0:T(8,128)S(1)}) custom-call(bf16[256,1024]{1,0:T(8,128)(2,1)S(1)} %aggregate.1.refs_0_, bf16[256,1024]{1,0:T(8,128)(2,1)S(1)} %collective-permute-done.4.refs_1_, bf16[512,256]{1,0:T(8,128)(2,1)S(1)} %get-tuple-element.34.refs_2_, ...), custom_call_target="tpu_custom_call" | custom-call | flops 20000000000 | tf_op jit(solution)/shard_map/layer/pallas_call | solution.py:67
  30.0 0.8 %layer.6 = (bf16[128,256]{1,0:T(8,128)(2,1)S(1)}, bf16[128,256]{1,0:T(8,128)(2,1)S(1)}, f32[128,1024]{1,0:T(8,128)S(1)}) custom-call(bf16[256,1024]{1,0:T(8,128)(2,1)S(1)} %aggregate.1.refs_0_, bf16[256,1024]{1,0:T(8,128)(2,1)S(1)} %collective-permute-done.4.refs_1_, bf16[512,256]{1,0:T(8,128)(2,1)S(1)} %get-tuple-element.34.refs_2_, ...), custom_call_target="tpu_custom_call" | custom-call | flops 20000000000 | tf_op jit(solution)/shard_map/layer/pallas_call | solution.py:67
  30.9 0.1 collective-permute-start.13
  31.1 2.0 %collective-permute-start.15 = (bf16[64,1024]{1,0:T(8,128)(2,1)S(1)}, bf16[64,1024]{1,0:T(8,128)(2,1)S(1)}, u32[]{:S(2)}, u32[]{:S(2)}) collective-permute-start(bf16[64,1024]{1,0:T(8,128)(2,1)S(1)} %add.35), channel_id=1, source_target_pairs={{0,4},{1,3},{2,6},{3,1},{4,0},{5,7},{6,2},{7,5},{8,12},{9,11},{10,... | collective-permute-start | bytes 393224 | tf_op jit(solution)/shard_map/ppermute | solution.py:24
  33.1 0.0 collective-permute-done.17
  33.1 1.1 %collective-permute-start.18 = (bf16[32,1024]{1,0:T(8,128)(2,1)S(1)}, bf16[32,1024]{1,0:T(8,128)(2,1)S(1)}, u32[]{:S(2)}, u32[]{:S(2)}) collective-permute-start(bf16[32,1024]{1,0:T(8,128)(2,1)S(1)} %add.37), channel_id=1, source_target_pairs={{0,4},{1,3},{2,6},{3,1},{4,0},{5,7},{6,2},{7,5},{8,12},{9,11},{10,... | collective-permute-start | bytes 196616 | tf_op jit(solution)/shard_map/ppermute | solution.py:24
  34.2 1.1 %collective-permute-start.20 = (bf16[32,1024]{1,0:T(8,128)(2,1)S(1)}, bf16[32,1024]{1,0:T(8,128)(2,1)S(1)}, u32[]{:S(2)}, u32[]{:S(2)}) collective-permute-start(bf16[32,1024]{1,0:T(8,128)(2,1)S(1)} %add.39), channel_id=1, source_target_pairs={{0,4},{1,3},{2,6},{3,1},{4,0},{5,7},{6,2},{7,5},{8,12},{9,11},{10,... | collective-permute-start | bytes 196616 | tf_op jit(solution)/shard_map/ppermute | solution.py:24
  35.3 0.0 collective-permute-done.16.got_ref
  35.4 1.8 %into_place.1 = bf16[256,1024]{1,0:T(8,128)(2,1)} custom-call(bf16[128,256]{1,0:T(8,128)(2,1)S(1)} %get-tuple-element.44.refs_0_, bf16[128,256]{1,0:T(8,128)(2,1)S(1)} %get-tuple-element.45.refs_1_, bf16[128,256]{1,0:T(8,128)(2,1)S(1)} %get-tuple-element.46.refs_2_, bf16[128,256]{1,0:T(8,128)(2,1)S(1)} %get-tuple-element.47.refs_3_, ...), custom_call_target="tpu_custom_call" | custom-call | tf_op jit(solution)/shard_map/into_place/pallas_call | solution.py:283
  37.2 0.3 collective-permute-done.18.got_ref
  37.5 2.3 %collective-permute-start.19 = (bf16[32,1024]{1,0:T(8,128)(2,1)S(1)}, bf16[32,1024]{1,0:T(8,128)(2,1)S(1)}, u32[]{:S(2)}, u32[]{:S(2)}) collective-permute-start(bf16[32,1024]{1,0:T(8,128)(2,1)S(1)} %add.38), channel_id=1, source_target_pairs={{0,24},{1,25},{2,26},{3,27},{4,28},{5,29},{6,30},{7,31},{8,16},{9,... | collective-permute-start | bytes 196616 | tf_op jit(solution)/shard_map/ppermute | solution.py:24
  39.8 0.0 collective-permute-done.20.got_ref
  39.8 0.7 %collective-permute-start.21 = (bf16[32,1024]{1,0:T(8,128)(2,1)S(1)}, bf16[32,1024]{1,0:T(8,128)(2,1)S(1)}, u32[]{:S(2)}, u32[]{:S(2)}) collective-permute-start(bf16[32,1024]{1,0:T(8,128)(2,1)S(1)} %add.40), channel_id=1, source_target_pairs={{0,16},{1,17},{2,18},{3,19},{4,20},{5,21},{6,22},{7,23},{8,24},{9,... | collective-permute-start | bytes 196616 | tf_op jit(solution)/shard_map/ppermute | solution.py:24
  40.5 0.0 collective-permute-done.15
  40.5 1.6 %collective-permute-start.22 = (bf16[32,1024]{1,0:T(8,128)(2,1)S(1)}, bf16[32,1024]{1,0:T(8,128)(2,1)S(1)}, u32[]{:S(2)}, u32[]{:S(2)}) collective-permute-start(bf16[32,1024]{1,0:T(8,128)(2,1)S(1)} %add.41), channel_id=1, source_target_pairs={{0,8},{1,9},{2,10},{3,11},{4,12},{5,13},{6,14},{7,15},{8,0},{9,1},... | collective-permute-start | bytes 196616 | tf_op jit(solution)/shard_map/ppermute | solution.py:24
  42.1 3.6 %collective-permute-done.21 = bf16[32,1024]{1,0:T(8,128)(2,1)S(1)} collective-permute-done((bf16[32,1024]{1,0:T(8,128)(2,1)S(1)}, bf16[32,1024]{1,0:T(8,128)(2,1)S(1)}, u32[]{:S(2)}, u32[]{:S(2)}) %collective-permute-start.21) | collective-permute-done | bytes 65568 | tf_op jit(solution)/shard_map/ppermute | solution.py:24
  45.7 0.0 collective-permute-done.19
  45.7 0.7 %fusion = f32[32,1024]{1,0:T(8,128)} fusion(f32[64,1024]{1,0:T(8,128)S(1)} %add.34.kept_ref, bf16[32,1024]{1,0:T(8,128)(2,1)S(1)} %collective-permute-done.22, bf16[32,1024]{1,0:T(8,128)(2,1)S(1)} %collective-permute-done.21, bf16[32,1024]{1,0:T(8,128)(2,1)S(1)} %collective-permute-done.19, bf16[64,1024]{1,0:T(8,128)(2,1)S(1)} %collective-permute-done.15), kind=kLoop, calls=%fused_computation.2 | loop fusion | flops 262144 | bytes 524288 | tf_op jit(solution)/shard_map/add | solution.py:372
  (32 shorter events, 0.3 us)
Async XLA Ops:
  0.6 13.1 %copy-start.1 = (bf16[256,1024]{1,0:T(8,128)(2,1)S(1)}, bf16[256,1024]{1,0:T(8,128)(2,1)}, u32[]{:S(2)}) copy-start(bf16[256,1024]{1,0:T(8,128)(2,1)} %features_in.1) | copy-start | bytes 1572868
  0.6 13.1 %copy-start = (bf16[256,1024]{1,0:T(8,128)(2,1)S(1)}, bf16[256,1024]{1,0:T(8,128)(2,1)}, u32[]{:S(2)}) copy-start(bf16[256,1024]{1,0:T(8,128)(2,1)} %cotangent_in.1) | copy-start | bytes 1572868
  0.7 13.1 %copy-start.3 = (s32[1,3]{1,0:T(1,128)S(1)}, s32[1,3]{1,0:T(1,128)}, u32[]{:S(2)}) copy-start(s32[1,3]{1,0:T(1,128)} %cols.1) | copy-start | bytes 40
  0.7 13.1 %copy-start.2 = (bf16[1,3,256,256]{3,2,1,0:T(8,128)(2,1)S(1)}, bf16[1,3,256,256]{3,2,1,0:T(8,128)(2,1)}, u32[]{:S(2)}) copy-start(bf16[1,3,256,256]{3,2,1,0:T(8,128)(2,1)} %tiles_in.1) | copy-start | bytes 1179652
  0.7 3.1 %collective-permute-start = (s32[1]{0:T(128)}, s32[1]{0:T(128)}, u32[]{:S(2)}, u32[]{:S(2)}) collective-permute-start(s32[1]{0:T(128)} %param.9), channel_id=1, source_target_pairs={{0,1},{1,0},{2,3},{3,2},{4,5},{5,4},{6,7},{7,6},{8,9},{9,8},{10,11... | collective-permute-start | bytes 20 | tf_op jit(solution)/shard_map/ppermute | solution.py:24
  1.2 5.5 %collective-permute-start.1 = (bf16[32,1024]{1,0:T(8,128)(2,1)}, bf16[32,1024]{1,0:T(8,128)(2,1)S(1)}, u32[]{:S(2)}, u32[]{:S(2)}) collective-permute-start(bf16[32,1024]{1,0:T(8,128)(2,1)} %weight.1), channel_id=1, source_target_pairs={{0,2},{1,3},{2,0},{3,1},{4,6},{5,7},{6,4},{7,5},{8,10},{9,11},{10,... | collective-permute-start | bytes 196616 | tf_op jit(solution)/shard_map/ppermute | solution.py:24
  3.8 16.0 %collective-permute-start.3 = (bf16[256,1024]{1,0:T(8,128)(2,1)}, bf16[256,1024]{1,0:T(8,128)(2,1)S(1)}, u32[]{:S(2)}, u32[]{:S(2)}) collective-permute-start(bf16[256,1024]{1,0:T(8,128)(2,1)} %features_in.1), channel_id=1, source_target_pairs={{0,3},{1,2},{2,1},{3,0},{4,7},{5,6},{6,5},{7,4},{8,11},{9,10},{10,... | collective-permute-start | bytes 1572872 | tf_op jit(solution)/shard_map/ppermute | solution.py:24
  4.7 7.9 %collective-permute-start.2 = (bf16[256,1024]{1,0:T(8,128)(2,1)}, bf16[256,1024]{1,0:T(8,128)(2,1)S(1)}, u32[]{:S(2)}, u32[]{:S(2)}) collective-permute-start(bf16[256,1024]{1,0:T(8,128)(2,1)} %features_in.1), channel_id=1, source_target_pairs={{0,1},{1,0},{2,3},{3,2},{4,5},{5,4},{6,7},{7,6},{8,9},{9,8},{10,11... | collective-permute-start | bytes 1572872 | tf_op jit(solution)/shard_map/ppermute | solution.py:24
  5.0 0.8 %copy-start.4 = (bf16[32,1024]{1,0:T(8,128)(2,1)S(1)}, bf16[32,1024]{1,0:T(8,128)(2,1)}, u32[]{:S(2)}) copy-start(bf16[32,1024]{1,0:T(8,128)(2,1)} %weight.1) | copy-start | bytes 196612
  6.7 9.5 %collective-permute-start.9 = (bf16[64,1024]{1,0:T(8,128)(2,1)S(1)}, bf16[64,1024]{1,0:T(8,128)(2,1)S(1)}, u32[]{:S(2)}, u32[]{:S(2)}) collective-permute-start(bf16[64,1024]{1,0:T(8,128)(2,1)S(1)} %pad_maximum_fusion.1.refs_0_), channel_id=1, source_target_pairs={{0,16},{1,17},{2,18},{3,19},{4,20},{5,21},{6,22},{7,23},{8,24},{9,... | collective-permute-start | bytes 393224 | tf_op jit(solution)/shard_map/ppermute | solution.py:24
  9.6 6.6 %collective-permute-start.7 = (bf16[64,1024]{1,0:T(8,128)(2,1)S(1)}, bf16[64,1024]{1,0:T(8,128)(2,1)S(1)}, u32[]{:S(2)}, u32[]{:S(2)}) collective-permute-start(bf16[64,1024]{1,0:T(8,128)(2,1)S(1)} %pad_maximum_fusion.1.refs_0_), channel_id=1, source_target_pairs={{0,4},{1,5},{2,6},{3,7},{4,0},{5,1},{6,2},{7,3},{8,12},{9,13},{10,... | collective-permute-start | bytes 393224 | tf_op jit(solution)/shard_map/ppermute | solution.py:24
  11.1 9.0 %collective-permute-start.8 = (bf16[64,1024]{1,0:T(8,128)(2,1)S(1)}, bf16[64,1024]{1,0:T(8,128)(2,1)S(1)}, u32[]{:S(2)}, u32[]{:S(2)}) collective-permute-start(bf16[64,1024]{1,0:T(8,128)(2,1)S(1)} %pad_maximum_fusion.1.refs_0_), channel_id=1, source_target_pairs={{0,12},{1,13},{2,14},{3,15},{4,8},{5,9},{6,10},{7,11},{8,4},{9,5},... | collective-permute-start | bytes 393224 | tf_op jit(solution)/shard_map/ppermute | solution.py:24
  12.6 8.6 %collective-permute-start.6 = (bf16[64,1024]{1,0:T(8,128)(2,1)S(1)}, bf16[64,1024]{1,0:T(8,128)(2,1)S(1)}, u32[]{:S(2)}, u32[]{:S(2)}) collective-permute-start(bf16[64,1024]{1,0:T(8,128)(2,1)S(1)} %pad_maximum_fusion.1.refs_0_), channel_id=1, source_target_pairs={{0,8},{1,9},{2,10},{3,11},{4,12},{5,13},{6,14},{7,15},{8,0},{9,1},... | collective-permute-start | bytes 393224 | tf_op jit(solution)/shard_map/ppermute | solution.py:24
  16.2 10.0 %collective-permute-start.12 = (bf16[64,1024]{1,0:T(8,128)(2,1)S(1)}, bf16[64,1024]{1,0:T(8,128)(2,1)S(1)}, u32[]{:S(2)}, u32[]{:S(2)}) collective-permute-start(bf16[64,1024]{1,0:T(8,128)(2,1)S(1)} %collective-permute-done.9.refs_1_), channel_id=1, source_target_pairs={{0,4},{1,5},{2,6},{3,7},{4,0},{5,1},{6,2},{7,3},{8,12},{9,13},{10,... | collective-permute-start | bytes 393224 | tf_op jit(solution)/shard_map/ppermute | solution.py:24
  17.8 8.4 %collective-permute-start.11 = (bf16[64,1024]{1,0:T(8,128)(2,1)S(1)}, bf16[64,1024]{1,0:T(8,128)(2,1)S(1)}, u32[]{:S(2)}, u32[]{:S(2)}) collective-permute-start(bf16[64,1024]{1,0:T(8,128)(2,1)S(1)} %collective-permute-done.9.refs_1_), channel_id=1, source_target_pairs={{0,12},{1,13},{2,14},{3,15},{4,8},{5,9},{6,10},{7,11},{8,4},{9,5},... | collective-permute-start | bytes 393224 | tf_op jit(solution)/shard_map/ppermute | solution.py:24
  20.1 2.4 %collective-permute-start.4 = (bf16[256,1024]{1,0:T(8,128)(2,1)S(1)}, bf16[256,1024]{1,0:T(8,128)(2,1)S(1)}, u32[]{:S(2)}, u32[]{:S(2)}) collective-permute-start(bf16[256,1024]{1,0:T(8,128)(2,1)S(1)} %aggregate.1.refs_0_), channel_id=1, source_target_pairs={{0,1},{1,0},{2,3},{3,2},{4,5},{5,4},{6,7},{7,6},{8,9},{9,8},{10,11... | collective-permute-start | bytes 1572872 | tf_op jit(solution)/shard_map/ppermute | solution.py:24
  20.2 2.3 %collective-permute-start.5 = (bf16[512,256]{1,0:T(8,128)(2,1)S(1)}, bf16[512,256]{1,0:T(8,128)(2,1)S(1)}, u32[]{:S(2)}, u32[]{:S(2)}) collective-permute-start(bf16[512,256]{1,0:T(8,128)(2,1)S(1)} %get-tuple-element.36), channel_id=1, source_target_pairs={{0,1},{1,0},{2,3},{3,2},{4,5},{5,4},{6,7},{7,6},{8,9},{9,8},{10,11... | collective-permute-start | bytes 786440 | tf_op jit(solution)/shard_map/ppermute | solution.py:24
  21.3 5.0 %collective-permute-start.10 = (bf16[64,1024]{1,0:T(8,128)(2,1)S(1)}, bf16[64,1024]{1,0:T(8,128)(2,1)S(1)}, u32[]{:S(2)}, u32[]{:S(2)}) collective-permute-start(bf16[64,1024]{1,0:T(8,128)(2,1)S(1)} %collective-permute-done.9.refs_1_), channel_id=1, source_target_pairs={{0,8},{1,9},{2,10},{3,11},{4,12},{5,13},{6,14},{7,15},{8,0},{9,1},... | collective-permute-start | bytes 393224 | tf_op jit(solution)/shard_map/ppermute | solution.py:24
  23.3 7.7 %collective-permute-start.14 = (bf16[128,1024]{1,0:T(8,128)(2,1)S(1)}, bf16[128,1024]{1,0:T(8,128)(2,1)S(1)}, u32[]{:S(2)}, u32[]{:S(2)}) collective-permute-start(bf16[128,1024]{1,0:T(8,128)(2,1)S(1)} %get-tuple-element.40), channel_id=1, source_target_pairs={{0,2},{1,5},{2,0},{3,7},{4,6},{5,1},{6,4},{7,3},{8,10},{9,13},{10,... | collective-permute-start | bytes 786440 | tf_op jit(solution)/shard_map/ppermute | solution.py:24
  27.1 6.0 %collective-permute-start.17 = (bf16[64,1024]{1,0:T(8,128)(2,1)S(1)}, bf16[64,1024]{1,0:T(8,128)(2,1)S(1)}, u32[]{:S(2)}, u32[]{:S(2)}) collective-permute-start(bf16[64,1024]{1,0:T(8,128)(2,1)S(1)} %get-tuple-element.42), channel_id=1, source_target_pairs={{0,2},{1,5},{2,0},{3,7},{4,6},{5,1},{6,4},{7,3},{8,10},{9,13},{10,... | collective-permute-start | bytes 393224 | tf_op jit(solution)/shard_map/ppermute | solution.py:24
  28.5 6.8 %collective-permute-start.16 = (bf16[64,1024]{1,0:T(8,128)(2,1)S(1)}, bf16[64,1024]{1,0:T(8,128)(2,1)S(1)}, u32[]{:S(2)}, u32[]{:S(2)}) collective-permute-start(bf16[64,1024]{1,0:T(8,128)(2,1)S(1)} %get-tuple-element.55), channel_id=1, source_target_pairs={{0,2},{1,5},{2,0},{3,7},{4,6},{5,1},{6,4},{7,3},{8,10},{9,13},{10,... | collective-permute-start | bytes 393224 | tf_op jit(solution)/shard_map/ppermute | solution.py:24
  30.9 4.5 %collective-permute-start.13 = (bf16[512,256]{1,0:T(8,128)(2,1)S(1)}, bf16[512,256]{1,0:T(8,128)(2,1)S(1)}, u32[]{:S(2)}, u32[]{:S(2)}) collective-permute-start(bf16[512,256]{1,0:T(8,128)(2,1)S(1)} %pad_maximum_fusion), channel_id=1, source_target_pairs={{0,1},{1,0},{2,3},{3,2},{4,5},{5,4},{6,7},{7,6},{8,9},{9,8},{10,11... | collective-permute-start | bytes 786440 | tf_op jit(solution)/shard_map/ppermute | solution.py:24
  31.1 9.4 %collective-permute-start.15 = (bf16[64,1024]{1,0:T(8,128)(2,1)S(1)}, bf16[64,1024]{1,0:T(8,128)(2,1)S(1)}, u32[]{:S(2)}, u32[]{:S(2)}) collective-permute-start(bf16[64,1024]{1,0:T(8,128)(2,1)S(1)} %add.35), channel_id=1, source_target_pairs={{0,4},{1,3},{2,6},{3,1},{4,0},{5,7},{6,2},{7,5},{8,12},{9,11},{10,... | collective-permute-start | bytes 393224 | tf_op jit(solution)/shard_map/ppermute | solution.py:24
  33.1 4.3 %collective-permute-start.18 = (bf16[32,1024]{1,0:T(8,128)(2,1)S(1)}, bf16[32,1024]{1,0:T(8,128)(2,1)S(1)}, u32[]{:S(2)}, u32[]{:S(2)}) collective-permute-start(bf16[32,1024]{1,0:T(8,128)(2,1)S(1)} %add.37), channel_id=1, source_target_pairs={{0,4},{1,3},{2,6},{3,1},{4,0},{5,7},{6,2},{7,5},{8,12},{9,11},{10,... | collective-permute-start | bytes 196616 | tf_op jit(solution)/shard_map/ppermute | solution.py:24
  34.2 5.6 %collective-permute-start.20 = (bf16[32,1024]{1,0:T(8,128)(2,1)S(1)}, bf16[32,1024]{1,0:T(8,128)(2,1)S(1)}, u32[]{:S(2)}, u32[]{:S(2)}) collective-permute-start(bf16[32,1024]{1,0:T(8,128)(2,1)S(1)} %add.39), channel_id=1, source_target_pairs={{0,4},{1,3},{2,6},{3,1},{4,0},{5,7},{6,2},{7,5},{8,12},{9,11},{10,... | collective-permute-start | bytes 196616 | tf_op jit(solution)/shard_map/ppermute | solution.py:24
  37.5 8.3 %collective-permute-start.19 = (bf16[32,1024]{1,0:T(8,128)(2,1)S(1)}, bf16[32,1024]{1,0:T(8,128)(2,1)S(1)}, u32[]{:S(2)}, u32[]{:S(2)}) collective-permute-start(bf16[32,1024]{1,0:T(8,128)(2,1)S(1)} %add.38), channel_id=1, source_target_pairs={{0,24},{1,25},{2,26},{3,27},{4,28},{5,29},{6,30},{7,31},{8,16},{9,... | collective-permute-start | bytes 196616 | tf_op jit(solution)/shard_map/ppermute | solution.py:24
  39.8 5.9 %collective-permute-start.21 = (bf16[32,1024]{1,0:T(8,128)(2,1)S(1)}, bf16[32,1024]{1,0:T(8,128)(2,1)S(1)}, u32[]{:S(2)}, u32[]{:S(2)}) collective-permute-start(bf16[32,1024]{1,0:T(8,128)(2,1)S(1)} %add.40), channel_id=1, source_target_pairs={{0,16},{1,17},{2,18},{3,19},{4,20},{5,21},{6,22},{7,23},{8,24},{9,... | collective-permute-start | bytes 196616 | tf_op jit(solution)/shard_map/ppermute | solution.py:24
  40.5 5.2 %collective-permute-start.22 = (bf16[32,1024]{1,0:T(8,128)(2,1)S(1)}, bf16[32,1024]{1,0:T(8,128)(2,1)S(1)}, u32[]{:S(2)}, u32[]{:S(2)}) collective-permute-start(bf16[32,1024]{1,0:T(8,128)(2,1)S(1)} %add.41), channel_id=1, source_target_pairs={{0,8},{1,9},{2,10},{3,11},{4,12},{5,13},{6,14},{7,15},{8,0},{9,1},... | collective-permute-start | bytes 196616 | tf_op jit(solution)/shard_map/ppermute | solution.py:24

commit v7 on v6

--- a/solution.py
+++ b/solution.py
@@ -291,9 +291,9 @@
     )(*parts, place)
 
 
-def add(kept, first, count, got, kind, cost=BRIEF):
+def add(kept, first, count, got, kind, cost=BRIEF, got_first=0):
     def body(kept_ref, got_ref, out):
-        out[...] = (kept_ref[pl.ds(first, count), :] + got_ref[...].astype(F32)).astype(kind)
+        out[...] = (kept_ref[pl.ds(first, count), :] + got_ref[pl.ds(got_first, count), :].astype(F32)).astype(kind)
 
     return pl.pallas_call(
         body,
@@ -351,19 +351,19 @@
     own_e0, other_e0, keep_e = layer(operands + [w_e], 0, 0, 2 * half, [F32])
     own_l0, other_l0, keep_l = layer(operands + [w_l], 0, 4 * half, 2 * half, [F32])
 
-    send = add(keep_e, half, half, got_e[half:], BF16)
-    keep_e = add(keep_e, 0, half, got_e[:half], F32)
+    send = add(keep_e, half, half, got_e, BF16, got_first=half)
+    keep_e = add(keep_e, 0, half, got_e, F32)
     got_e = swap(send, Y, X)
 
-    got_24 = swap(add(keep_l, half, rows, got_1[:rows], BF16), Y, X)
-    got_16 = swap(add(keep_l, half + rows, rows, got_1[rows:], BF16), Y, X)
+    got_24 = swap(add(keep_l, half, rows, got_1, BF16), Y, X)
+    got_16 = swap(add(keep_l, half + rows, rows, got_1, BF16, got_first=rows), Y, X)
     keep_l = add(keep_l, 0, half, got_0, F32)
 
     others = jnp.concatenate([other_e0, other_e1, other_l0, other_l1])
     from_other = swap(others, CORE)
     output = into_place([own_e0, own_e1, own_l0, own_l1, from_other], place)
 
-    got_8 = swap(add(keep_e, rows, rows, got_e[rows:], BF16), ALONG_Z[1])
+    got_8 = swap(add(keep_e, rows, rows, got_e, BF16, got_first=rows), ALONG_Z[1])
     send_24 = add(keep_l, 0, rows, after(got_24, output), BF16)
     got_24 = swap(send_24, ALONG_Z[2])
     got_16 = after(got_16, output, send_24)

time: 46.6 us -> 48.5 us (1.041)
  waiting for transfers between devices: 7.32 us -> 8.62 us
  starting transfers between devices: 27.3 us -> 28 us
    ppermute x23, waiting for transfers between devices: 7.32 us -> 8.62 us  [swap(): lax.ppermute(value, AXES, [(i, i ^ masks[i % 2]) for i in range(total)])]
    ppermute x23, starting transfers between devices: 27.3 us -> 28 us  [swap(): lax.ppermute(value, AXES, [(i, i ^ masks[i % 2]) for i in range(total)])]
  transfers between devices with their start and end apart: 23 -> 23, of which waited for: 6 -> 7; matrix products, arithmetic and copies ran while one was open for 0% -> 0% of each run, Pallas kernels for 19% -> 18%
where the time goes in v7:
time: 48.5 us; the launch traced here: 48.3 us
  starting transfers between devices  28 us (58%)
  waiting for transfers between devices  8.62 us (18%)
  Pallas kernels  8.62 us (18%)
  between operations  1.53 us (3%)
  local copies, waits for them, and re-layouts  0.86 us (2%)
  other arithmetic  0.73 us (2%)
    ppermute x23, starting transfers between devices, swap(): lax.ppermute(value, AXES, [(i, i ^ masks[i % 2]) for i in range(total)])  28 us
    ppermute x23, waiting for transfers between devices, swap(): lax.ppermute(value, AXES, [(i, i ^ masks[i % 2]) for i in range(total)])  8.62 us
    pallas_call x4, Pallas kernels, layer(): pl.pallas_call(body, out_shape=[jax.ShapeDtypeStruct((count, nodes), BF16...  3.33 us
    pallas_call x1, Pallas kernels, prepare(): pl.pallas_call(prepare_body, out_shape=[jax.ShapeDtypeStruct((nodes, widt...  2.39 us
    pallas_call x1, Pallas kernels, into_place(): pl.pallas_call(into_place_body, out_shape=jax.ShapeDtypeStruct((parts[0]....  1.8 us
  transfers between devices with their start and end apart: 23, of which 7 were waited for; matrix products, arithmetic and copies ran while one was open for 0% of the time, Pallas kernels for 18%

profile of v7, /device:TPU:0, one launch (start us, length us, event | category | flops | bytes accessed | tf_op | source)
XLA Modules:
  0.0 48.3 jit_solution(5648168527658852740)
XLA Ops:
  0.7 0.5 %collective-permute-start = (s32[1]{0:T(128)}, s32[1]{0:T(128)}, u32[]{:S(2)}, u32[]{:S(2)}) collective-permute-start(s32[1]{0:T(128)} %param.9), channel_id=1, source_target_pairs={{0,1},{1,0},{2,3},{3,2},{4,5},{5,4},{6,7},{7,6},{8,9},{9,8},{10,11... | collective-permute-start | bytes 20 | tf_op jit(solution)/shard_map/ppermute | solution.py:24
  1.2 2.6 %collective-permute-start.1 = (bf16[32,1024]{1,0:T(8,128)(2,1)}, bf16[32,1024]{1,0:T(8,128)(2,1)S(1)}, u32[]{:S(2)}, u32[]{:S(2)}) collective-permute-start(bf16[32,1024]{1,0:T(8,128)(2,1)} %weight.1), channel_id=1, source_target_pairs={{0,2},{1,3},{2,0},{3,1},{4,6},{5,7},{6,4},{7,5},{8,10},{9,11},{10,... | collective-permute-start | bytes 196616 | tf_op jit(solution)/shard_map/ppermute | solution.py:24
  3.8 1.1 %collective-permute-start.3 = (bf16[256,1024]{1,0:T(8,128)(2,1)}, bf16[256,1024]{1,0:T(8,128)(2,1)S(1)}, u32[]{:S(2)}, u32[]{:S(2)}) collective-permute-start(bf16[256,1024]{1,0:T(8,128)(2,1)} %features_in.1), channel_id=1, source_target_pairs={{0,3},{1,2},{2,1},{3,0},{4,7},{5,6},{6,5},{7,4},{8,11},{9,10},{10,... | collective-permute-start | bytes 1572872 | tf_op jit(solution)/shard_map/ppermute | solution.py:24
  4.9 0.3 collective-permute-start.2
  5.2 0.8 %copy-done.4 = bf16[32,1024]{1,0:T(8,128)(2,1)S(1)} copy-done((bf16[32,1024]{1,0:T(8,128)(2,1)S(1)}, bf16[32,1024]{1,0:T(8,128)(2,1)}, u32[]{:S(2)}) %copy-start.4) | copy-done | bytes 65560
  6.0 0.6 %hold.1 = bf16[32,1024]{1,0:T(8,128)(2,1)S(1)} custom-call(bf16[32,1024]{1,0:T(8,128)(2,1)S(1)} %copy-done.4, s32[1]{0:T(128)} %collective-permute-done.near_block), custom_call_target="tpu_custom_call" | custom-call | flops 20000000000 | tf_op jit(solution)/shard_map/hold/pallas_call | solution.py:136
  6.6 0.1 collective-permute-done.1
  6.7 2.9 %collective-permute-start.9 = (bf16[64,1024]{1,0:T(8,128)(2,1)S(1)}, bf16[64,1024]{1,0:T(8,128)(2,1)S(1)}, u32[]{:S(2)}, u32[]{:S(2)}) collective-permute-start(bf16[64,1024]{1,0:T(8,128)(2,1)S(1)} %pad_maximum_fusion.1.refs_0_), channel_id=1, source_target_pairs={{0,16},{1,17},{2,18},{3,19},{4,20},{5,21},{6,22},{7,23},{8,24},{9,... | collective-permute-start | bytes 393224 | tf_op jit(solution)/shard_map/ppermute | solution.py:24
  9.6 1.5 %collective-permute-start.7 = (bf16[64,1024]{1,0:T(8,128)(2,1)S(1)}, bf16[64,1024]{1,0:T(8,128)(2,1)S(1)}, u32[]{:S(2)}, u32[]{:S(2)}) collective-permute-start(bf16[64,1024]{1,0:T(8,128)(2,1)S(1)} %pad_maximum_fusion.1.refs_0_), channel_id=1, source_target_pairs={{0,4},{1,5},{2,6},{3,7},{4,0},{5,1},{6,2},{7,3},{8,12},{9,13},{10,... | collective-permute-start | bytes 393224 | tf_op jit(solution)/shard_map/ppermute | solution.py:24
  11.1 1.5 %collective-permute-start.8 = (bf16[64,1024]{1,0:T(8,128)(2,1)S(1)}, bf16[64,1024]{1,0:T(8,128)(2,1)S(1)}, u32[]{:S(2)}, u32[]{:S(2)}) collective-permute-start(bf16[64,1024]{1,0:T(8,128)(2,1)S(1)} %pad_maximum_fusion.1.refs_0_), channel_id=1, source_target_pairs={{0,12},{1,13},{2,14},{3,15},{4,8},{5,9},{6,10},{7,11},{8,4},{9,5},... | collective-permute-start | bytes 393224 | tf_op jit(solution)/shard_map/ppermute | solution.py:24
  12.6 0.0 collective-permute-done.2.near_block
  12.6 0.5 collective-permute-start.6
  13.8 2.4 %prepare.1 = (f32[256,1024]{1,0:T(8,128)S(1)}, bf16[256,256]{1,0:T(8,128)(2,1)S(1)}, bf16[512,256]{1,0:T(8,128)(2,1)S(1)}, bf16[512,256]{1,0:T(8,128)(2,1)S(1)}, bf16[1024,1024]{1,0:T(8,128)(2,1)S(1)}) custom-call(s32[1]{0:T(128)} %bitcast.me_ref, s32[1,3]{1,0:T(1,128)S(1)} %copy-done.3, s32[1]{0:T(128)S(6)} %copy.8.count, ...), custom_call_target="tpu_custom_call" | custom-call | tf_op jit(solution)/shard_map/prepare/pallas_call | solution.py:202
  16.2 0.0 collective-permute-done.9.refs_1_
  16.2 0.0 collective-permute-done.7.refs_2_
  16.2 1.6 %collective-permute-start.12 = (bf16[64,1024]{1,0:T(8,128)(2,1)S(1)}, bf16[64,1024]{1,0:T(8,128)(2,1)S(1)}, u32[]{:S(2)}, u32[]{:S(2)}) collective-permute-start(bf16[64,1024]{1,0:T(8,128)(2,1)S(1)} %collective-permute-done.9.refs_1_), channel_id=1, source_target_pairs={{0,4},{1,5},{2,6},{3,7},{4,0},{5,1},{6,2},{7,3},{8,12},{9,13},{10,... | collective-permute-start | bytes 393224 | tf_op jit(solution)/shard_map/ppermute | solution.py:24
  17.8 2.1 %collective-permute-start.11 = (bf16[64,1024]{1,0:T(8,128)(2,1)S(1)}, bf16[64,1024]{1,0:T(8,128)(2,1)S(1)}, u32[]{:S(2)}, u32[]{:S(2)}) collective-permute-start(bf16[64,1024]{1,0:T(8,128)(2,1)S(1)} %collective-permute-done.9.refs_1_), channel_id=1, source_target_pairs={{0,12},{1,13},{2,14},{3,15},{4,8},{5,9},{6,10},{7,11},{8,4},{9,5},... | collective-permute-start | bytes 393224 | tf_op jit(solution)/shard_map/ppermute | solution.py:24
  19.9 0.0 collective-permute-done.3.block
  19.9 0.3 aggregate.1.refs_0_
  20.2 0.1 collective-permute-start.4
  20.3 0.0 collective-permute-done.8.refs_3_
  20.3 0.5 %collective-permute-start.5 = (bf16[512,256]{1,0:T(8,128)(2,1)S(1)}, bf16[512,256]{1,0:T(8,128)(2,1)S(1)}, u32[]{:S(2)}, u32[]{:S(2)}) collective-permute-start(bf16[512,256]{1,0:T(8,128)(2,1)S(1)} %get-tuple-element.36), channel_id=1, source_target_pairs={{0,1},{1,0},{2,3},{3,2},{4,5},{5,4},{6,7},{7,6},{8,9},{9,8},{10,11... | collective-permute-start | bytes 786440 | tf_op jit(solution)/shard_map/ppermute | solution.py:24
  20.8 0.6 %collective-permute-done.6.refs_1_ = bf16[64,1024]{1,0:T(8,128)(2,1)S(1)} collective-permute-done((bf16[64,1024]{1,0:T(8,128)(2,1)S(1)}, bf16[64,1024]{1,0:T(8,128)(2,1)S(1)}, u32[]{:S(2)}, u32[]{:S(2)}) %collective-permute-start.6) | collective-permute-done | bytes 131104 | tf_op jit(solution)/shard_map/ppermute | solution.py:24
  21.4 0.0 collective-permute-start.10
  21.4 1.2 %collective-permute-done.5.refs_3_ = bf16[512,256]{1,0:T(8,128)(2,1)S(1)} collective-permute-done((bf16[512,256]{1,0:T(8,128)(2,1)S(1)}, bf16[512,256]{1,0:T(8,128)(2,1)S(1)}, u32[]{:S(2)}, u32[]{:S(2)}) %collective-permute-start.5) | collective-permute-done | bytes 262176 | tf_op jit(solution)/shard_map/ppermute | solution.py:24
  22.6 0.8 %layer.4 = (bf16[128,256]{1,0:T(8,128)(2,1)S(1)}, bf16[128,256]{1,0:T(8,128)(2,1)S(1)}, bf16[128,1024]{1,0:T(8,128)(2,1)S(1)}) custom-call(bf16[256,1024]{1,0:T(8,128)(2,1)S(1)} %aggregate.1.refs_0_, bf16[256,1024]{1,0:T(8,128)(2,1)S(1)} %collective-permute-done.4.refs_1_, bf16[512,256]{1,0:T(8,128)(2,1)S(1)} %get-tuple-element.34.refs_2_, ...), custom_call_target="tpu_custom_call" | custom-call | flops 20000000000 | tf_op jit(solution)/shard_map/layer/pallas_call | solution.py:67
  23.4 1.2 %collective-permute-start.14 = (bf16[128,1024]{1,0:T(8,128)(2,1)S(1)}, bf16[128,1024]{1,0:T(8,128)(2,1)S(1)}, u32[]{:S(2)}, u32[]{:S(2)}) collective-permute-start(bf16[128,1024]{1,0:T(8,128)(2,1)S(1)} %get-tuple-element.40), channel_id=1, source_target_pairs={{0,2},{1,5},{2,0},{3,7},{4,6},{5,1},{6,4},{7,3},{8,10},{9,13},{10,... | collective-permute-start | bytes 786440 | tf_op jit(solution)/shard_map/ppermute | solution.py:24
  24.6 1.8 %collective-permute-done.10.refs_0_ = bf16[64,1024]{1,0:T(8,128)(2,1)S(1)} collective-permute-done((bf16[64,1024]{1,0:T(8,128)(2,1)S(1)}, bf16[64,1024]{1,0:T(8,128)(2,1)S(1)}, u32[]{:S(2)}, u32[]{:S(2)}) %collective-permute-start.10) | collective-permute-done | bytes 131104 | tf_op jit(solution)/shard_map/ppermute | solution.py:24
  26.3 0.0 collective-permute-done.12.refs_3_
  26.3 0.0 collective-permute-done.11.refs_2_
  26.4 0.8 %layer.5 = (bf16[128,256]{1,0:T(8,128)(2,1)S(1)}, bf16[128,256]{1,0:T(8,128)(2,1)S(1)}, bf16[64,1024]{1,0:T(8,128)(2,1)S(1)}, bf16[64,1024]{1,0:T(8,128)(2,1)S(1)}) custom-call(bf16[256,1024]{1,0:T(8,128)(2,1)S(1)} %aggregate.1.refs_0_, bf16[256,1024]{1,0:T(8,128)(2,1)S(1)} %collective-permute-done.4.refs_1_, ...), custom_call_target="tpu_custom_call" | custom-call | flops 20000000000 | tf_op jit(solution)/shard_map/layer/pallas_call | solution.py:67
  27.2 0.8 %layer.7 = (bf16[128,256]{1,0:T(8,128)(2,1)S(1)}, bf16[128,256]{1,0:T(8,128)(2,1)S(1)}, f32[128,1024]{1,0:T(8,128)S(1)}) custom-call(bf16[256,1024]{1,0:T(8,128)(2,1)S(1)} %aggregate.1.refs_0_, bf16[256,1024]{1,0:T(8,128)(2,1)S(1)} %collective-permute-done.4.refs_1_, bf16[512,256]{1,0:T(8,128)(2,1)S(1)} %get-tuple-element.34.refs_2_, ...), custom_call_target="tpu_custom_call" | custom-call | flops 20000000000 | tf_op jit(solution)/shard_map/layer/pallas_call | solution.py:67
  28.1 0.8 %layer.6 = (bf16[128,256]{1,0:T(8,128)(2,1)S(1)}, bf16[128,256]{1,0:T(8,128)(2,1)S(1)}, f32[128,1024]{1,0:T(8,128)S(1)}) custom-call(bf16[256,1024]{1,0:T(8,128)(2,1)S(1)} %aggregate.1.refs_0_, bf16[256,1024]{1,0:T(8,128)(2,1)S(1)} %collective-permute-done.4.refs_1_, bf16[512,256]{1,0:T(8,128)(2,1)S(1)} %get-tuple-element.34.refs_2_, ...), custom_call_target="tpu_custom_call" | custom-call | flops 20000000000 | tf_op jit(solution)/shard_map/layer/pallas_call | solution.py:67
  28.9 0.1 collective-permute-start.13
  29.0 1.3 %collective-permute-start.17 = (bf16[64,1024]{1,0:T(8,128)(2,1)S(1)}, bf16[64,1024]{1,0:T(8,128)(2,1)S(1)}, u32[]{:S(2)}, u32[]{:S(2)}) collective-permute-start(bf16[64,1024]{1,0:T(8,128)(2,1)S(1)} %get-tuple-element.42), channel_id=1, source_target_pairs={{0,2},{1,5},{2,0},{3,7},{4,6},{5,1},{6,4},{7,3},{8,10},{9,13},{10,... | collective-permute-start | bytes 393224 | tf_op jit(solution)/shard_map/ppermute | solution.py:24
  30.3 0.8 %collective-permute-start.16 = (bf16[64,1024]{1,0:T(8,128)(2,1)S(1)}, bf16[64,1024]{1,0:T(8,128)(2,1)S(1)}, u32[]{:S(2)}, u32[]{:S(2)}) collective-permute-start(bf16[64,1024]{1,0:T(8,128)(2,1)S(1)} %get-tuple-element.55), channel_id=1, source_target_pairs={{0,2},{1,5},{2,0},{3,7},{4,6},{5,1},{6,4},{7,3},{8,10},{9,13},{10,... | collective-permute-start | bytes 393224 | tf_op jit(solution)/shard_map/ppermute | solution.py:24
  31.1 0.0 collective-permute-done.14.got_ref
  31.1 2.0 %collective-permute-start.15 = (bf16[64,1024]{1,0:T(8,128)(2,1)S(1)}, bf16[64,1024]{1,0:T(8,128)(2,1)S(1)}, u32[]{:S(2)}, u32[]{:S(2)}) collective-permute-start(bf16[64,1024]{1,0:T(8,128)(2,1)S(1)} %add.35), channel_id=1, source_target_pairs={{0,4},{1,3},{2,6},{3,1},{4,0},{5,7},{6,2},{7,5},{8,12},{9,11},{10,... | collective-permute-start | bytes 393224 | tf_op jit(solution)/shard_map/ppermute | solution.py:24
  33.2 0.9 %collective-permute-done.17.got_ref = bf16[64,1024]{1,0:T(8,128)(2,1)S(1)} collective-permute-done((bf16[64,1024]{1,0:T(8,128)(2,1)S(1)}, bf16[64,1024]{1,0:T(8,128)(2,1)S(1)}, u32[]{:S(2)}, u32[]{:S(2)}) %collective-permute-start.17) | collective-permute-done | bytes 131104 | tf_op jit(solution)/shard_map/ppermute | solution.py:24
  34.1 2.4 %collective-permute-start.18 = (bf16[32,1024]{1,0:T(8,128)(2,1)S(1)}, bf16[32,1024]{1,0:T(8,128)(2,1)S(1)}, u32[]{:S(2)}, u32[]{:S(2)}) collective-permute-start(bf16[32,1024]{1,0:T(8,128)(2,1)S(1)} %add.37), channel_id=1, source_target_pairs={{0,4},{1,3},{2,6},{3,1},{4,0},{5,7},{6,2},{7,5},{8,12},{9,11},{10,... | collective-permute-start | bytes 196616 | tf_op jit(solution)/shard_map/ppermute | solution.py:24
  36.5 0.1 collective-permute-start.20
  36.6 0.3 collective-permute-done.16.got_ref
  37.0 1.8 %into_place.1 = bf16[256,1024]{1,0:T(8,128)(2,1)} custom-call(bf16[128,256]{1,0:T(8,128)(2,1)S(1)} %get-tuple-element.44.refs_0_, bf16[128,256]{1,0:T(8,128)(2,1)S(1)} %get-tuple-element.45.refs_1_, bf16[128,256]{1,0:T(8,128)(2,1)S(1)} %get-tuple-element.46.refs_2_, bf16[128,256]{1,0:T(8,128)(2,1)S(1)} %get-tuple-element.47.refs_3_, ...), custom_call_target="tpu_custom_call" | custom-call | tf_op jit(solution)/shard_map/into_place/pallas_call | solution.py:283
  38.8 3.1 %collective-permute-start.19 = (bf16[32,1024]{1,0:T(8,128)(2,1)S(1)}, bf16[32,1024]{1,0:T(8,128)(2,1)S(1)}, u32[]{:S(2)}, u32[]{:S(2)}) collective-permute-start(bf16[32,1024]{1,0:T(8,128)(2,1)S(1)} %add.38), channel_id=1, source_target_pairs={{0,24},{1,25},{2,26},{3,27},{4,28},{5,29},{6,30},{7,31},{8,16},{9,... | collective-permute-start | bytes 196616 | tf_op jit(solution)/shard_map/ppermute | solution.py:24
  41.9 0.3 collective-permute-start.21
  42.2 1.6 %collective-permute-start.22 = (bf16[32,1024]{1,0:T(8,128)(2,1)S(1)}, bf16[32,1024]{1,0:T(8,128)(2,1)S(1)}, u32[]{:S(2)}, u32[]{:S(2)}) collective-permute-start(bf16[32,1024]{1,0:T(8,128)(2,1)S(1)} %add.41), channel_id=1, source_target_pairs={{0,8},{1,9},{2,10},{3,11},{4,12},{5,13},{6,14},{7,15},{8,0},{9,1},... | collective-permute-start | bytes 196616 | tf_op jit(solution)/shard_map/ppermute | solution.py:24
  43.8 3.8 %collective-permute-done.21 = bf16[32,1024]{1,0:T(8,128)(2,1)S(1)} collective-permute-done((bf16[32,1024]{1,0:T(8,128)(2,1)S(1)}, bf16[32,1024]{1,0:T(8,128)(2,1)S(1)}, u32[]{:S(2)}, u32[]{:S(2)}) %collective-permute-start.21) | collective-permute-done | bytes 65568 | tf_op jit(solution)/shard_map/ppermute | solution.py:24
  47.6 0.7 %fusion = f32[32,1024]{1,0:T(8,128)} fusion(f32[64,1024]{1,0:T(8,128)S(1)} %add.34.kept_ref, bf16[32,1024]{1,0:T(8,128)(2,1)S(1)} %collective-permute-done.22, bf16[32,1024]{1,0:T(8,128)(2,1)S(1)} %collective-permute-done.21, bf16[32,1024]{1,0:T(8,128)(2,1)S(1)} %collective-permute-done.19, bf16[64,1024]{1,0:T(8,128)(2,1)S(1)} %collective-permute-done.15.got_ref), kind=kLoop, calls=%fused_computation.2 | loop fusion | flops 262144 | bytes 524288 | tf_op jit(solution)/shard_map/add | solution.py:372
  (29 shorter events, 0.3 us)
Async XLA Ops:
  0.6 13.1 %copy-start.1 = (bf16[256,1024]{1,0:T(8,128)(2,1)S(1)}, bf16[256,1024]{1,0:T(8,128)(2,1)}, u32[]{:S(2)}) copy-start(bf16[256,1024]{1,0:T(8,128)(2,1)} %features_in.1) | copy-start | bytes 1572868
  0.6 13.1 %copy-start = (bf16[256,1024]{1,0:T(8,128)(2,1)S(1)}, bf16[256,1024]{1,0:T(8,128)(2,1)}, u32[]{:S(2)}) copy-start(bf16[256,1024]{1,0:T(8,128)(2,1)} %cotangent_in.1) | copy-start | bytes 1572868
  0.7 13.1 %copy-start.3 = (s32[1,3]{1,0:T(1,128)S(1)}, s32[1,3]{1,0:T(1,128)}, u32[]{:S(2)}) copy-start(s32[1,3]{1,0:T(1,128)} %cols.1) | copy-start | bytes 40
  0.7 13.1 %copy-start.2 = (bf16[1,3,256,256]{3,2,1,0:T(8,128)(2,1)S(1)}, bf16[1,3,256,256]{3,2,1,0:T(8,128)(2,1)}, u32[]{:S(2)}) copy-start(bf16[1,3,256,256]{3,2,1,0:T(8,128)(2,1)} %tiles_in.1) | copy-start | bytes 1179652
  0.7 3.1 %collective-permute-start = (s32[1]{0:T(128)}, s32[1]{0:T(128)}, u32[]{:S(2)}, u32[]{:S(2)}) collective-permute-start(s32[1]{0:T(128)} %param.9), channel_id=1, source_target_pairs={{0,1},{1,0},{2,3},{3,2},{4,5},{5,4},{6,7},{7,6},{8,9},{9,8},{10,11... | collective-permute-start | bytes 20 | tf_op jit(solution)/shard_map/ppermute | solution.py:24
  1.2 5.5 %collective-permute-start.1 = (bf16[32,1024]{1,0:T(8,128)(2,1)}, bf16[32,1024]{1,0:T(8,128)(2,1)S(1)}, u32[]{:S(2)}, u32[]{:S(2)}) collective-permute-start(bf16[32,1024]{1,0:T(8,128)(2,1)} %weight.1), channel_id=1, source_target_pairs={{0,2},{1,3},{2,0},{3,1},{4,6},{5,7},{6,4},{7,5},{8,10},{9,11},{10,... | collective-permute-start | bytes 196616 | tf_op jit(solution)/shard_map/ppermute | solution.py:24
  3.8 16.1 %collective-permute-start.3 = (bf16[256,1024]{1,0:T(8,128)(2,1)}, bf16[256,1024]{1,0:T(8,128)(2,1)S(1)}, u32[]{:S(2)}, u32[]{:S(2)}) collective-permute-start(bf16[256,1024]{1,0:T(8,128)(2,1)} %features_in.1), channel_id=1, source_target_pairs={{0,3},{1,2},{2,1},{3,0},{4,7},{5,6},{6,5},{7,4},{8,11},{9,10},{10,... | collective-permute-start | bytes 1572872 | tf_op jit(solution)/shard_map/ppermute | solution.py:24
  4.9 7.8 %collective-permute-start.2 = (bf16[256,1024]{1,0:T(8,128)(2,1)}, bf16[256,1024]{1,0:T(8,128)(2,1)S(1)}, u32[]{:S(2)}, u32[]{:S(2)}) collective-permute-start(bf16[256,1024]{1,0:T(8,128)(2,1)} %features_in.1), channel_id=1, source_target_pairs={{0,1},{1,0},{2,3},{3,2},{4,5},{5,4},{6,7},{7,6},{8,9},{9,8},{10,11... | collective-permute-start | bytes 1572872 | tf_op jit(solution)/shard_map/ppermute | solution.py:24
  5.2 0.8 %copy-start.4 = (bf16[32,1024]{1,0:T(8,128)(2,1)S(1)}, bf16[32,1024]{1,0:T(8,128)(2,1)}, u32[]{:S(2)}) copy-start(bf16[32,1024]{1,0:T(8,128)(2,1)} %weight.1) | copy-start | bytes 196612
  6.7 9.5 %collective-permute-start.9 = (bf16[64,1024]{1,0:T(8,128)(2,1)S(1)}, bf16[64,1024]{1,0:T(8,128)(2,1)S(1)}, u32[]{:S(2)}, u32[]{:S(2)}) collective-permute-start(bf16[64,1024]{1,0:T(8,128)(2,1)S(1)} %pad_maximum_fusion.1.refs_0_), channel_id=1, source_target_pairs={{0,16},{1,17},{2,18},{3,19},{4,20},{5,21},{6,22},{7,23},{8,24},{9,... | collective-permute-start | bytes 393224 | tf_op jit(solution)/shard_map/ppermute | solution.py:24
  9.6 6.6 %collective-permute-start.7 = (bf16[64,1024]{1,0:T(8,128)(2,1)S(1)}, bf16[64,1024]{1,0:T(8,128)(2,1)S(1)}, u32[]{:S(2)}, u32[]{:S(2)}) collective-permute-start(bf16[64,1024]{1,0:T(8,128)(2,1)S(1)} %pad_maximum_fusion.1.refs_0_), channel_id=1, source_target_pairs={{0,4},{1,5},{2,6},{3,7},{4,0},{5,1},{6,2},{7,3},{8,12},{9,13},{10,... | collective-permute-start | bytes 393224 | tf_op jit(solution)/shard_map/ppermute | solution.py:24
  11.1 9.2 %collective-permute-start.8 = (bf16[64,1024]{1,0:T(8,128)(2,1)S(1)}, bf16[64,1024]{1,0:T(8,128)(2,1)S(1)}, u32[]{:S(2)}, u32[]{:S(2)}) collective-permute-start(bf16[64,1024]{1,0:T(8,128)(2,1)S(1)} %pad_maximum_fusion.1.refs_0_), channel_id=1, source_target_pairs={{0,12},{1,13},{2,14},{3,15},{4,8},{5,9},{6,10},{7,11},{8,4},{9,5},... | collective-permute-start | bytes 393224 | tf_op jit(solution)/shard_map/ppermute | solution.py:24
  12.6 8.7 %collective-permute-start.6 = (bf16[64,1024]{1,0:T(8,128)(2,1)S(1)}, bf16[64,1024]{1,0:T(8,128)(2,1)S(1)}, u32[]{:S(2)}, u32[]{:S(2)}) collective-permute-start(bf16[64,1024]{1,0:T(8,128)(2,1)S(1)} %pad_maximum_fusion.1.refs_0_), channel_id=1, source_target_pairs={{0,8},{1,9},{2,10},{3,11},{4,12},{5,13},{6,14},{7,15},{8,0},{9,1},... | collective-permute-start | bytes 393224 | tf_op jit(solution)/shard_map/ppermute | solution.py:24
  16.2 10.1 %collective-permute-start.12 = (bf16[64,1024]{1,0:T(8,128)(2,1)S(1)}, bf16[64,1024]{1,0:T(8,128)(2,1)S(1)}, u32[]{:S(2)}, u32[]{:S(2)}) collective-permute-start(bf16[64,1024]{1,0:T(8,128)(2,1)S(1)} %collective-permute-done.9.refs_1_), channel_id=1, source_target_pairs={{0,4},{1,5},{2,6},{3,7},{4,0},{5,1},{6,2},{7,3},{8,12},{9,13},{10,... | collective-permute-start | bytes 393224 | tf_op jit(solution)/shard_map/ppermute | solution.py:24
  17.8 8.5 %collective-permute-start.11 = (bf16[64,1024]{1,0:T(8,128)(2,1)S(1)}, bf16[64,1024]{1,0:T(8,128)(2,1)S(1)}, u32[]{:S(2)}, u32[]{:S(2)}) collective-permute-start(bf16[64,1024]{1,0:T(8,128)(2,1)S(1)} %collective-permute-done.9.refs_1_), channel_id=1, source_target_pairs={{0,12},{1,13},{2,14},{3,15},{4,8},{5,9},{6,10},{7,11},{8,4},{9,5},... | collective-permute-start | bytes 393224 | tf_op jit(solution)/shard_map/ppermute | solution.py:24
  20.2 2.4 %collective-permute-start.4 = (bf16[256,1024]{1,0:T(8,128)(2,1)S(1)}, bf16[256,1024]{1,0:T(8,128)(2,1)S(1)}, u32[]{:S(2)}, u32[]{:S(2)}) collective-permute-start(bf16[256,1024]{1,0:T(8,128)(2,1)S(1)} %aggregate.1.refs_0_), channel_id=1, source_target_pairs={{0,1},{1,0},{2,3},{3,2},{4,5},{5,4},{6,7},{7,6},{8,9},{9,8},{10,11... | collective-permute-start | bytes 1572872 | tf_op jit(solution)/shard_map/ppermute | solution.py:24
  20.3 2.3 %collective-permute-start.5 = (bf16[512,256]{1,0:T(8,128)(2,1)S(1)}, bf16[512,256]{1,0:T(8,128)(2,1)S(1)}, u32[]{:S(2)}, u32[]{:S(2)}) collective-permute-start(bf16[512,256]{1,0:T(8,128)(2,1)S(1)} %get-tuple-element.36), channel_id=1, source_target_pairs={{0,1},{1,0},{2,3},{3,2},{4,5},{5,4},{6,7},{7,6},{8,9},{9,8},{10,11... | collective-permute-start | bytes 786440 | tf_op jit(solution)/shard_map/ppermute | solution.py:24
  21.4 5.0 %collective-permute-start.10 = (bf16[64,1024]{1,0:T(8,128)(2,1)S(1)}, bf16[64,1024]{1,0:T(8,128)(2,1)S(1)}, u32[]{:S(2)}, u32[]{:S(2)}) collective-permute-start(bf16[64,1024]{1,0:T(8,128)(2,1)S(1)} %collective-permute-done.9.refs_1_), channel_id=1, source_target_pairs={{0,8},{1,9},{2,10},{3,11},{4,12},{5,13},{6,14},{7,15},{8,0},{9,1},... | collective-permute-start | bytes 393224 | tf_op jit(solution)/shard_map/ppermute | solution.py:24
  23.4 7.7 %collective-permute-start.14 = (bf16[128,1024]{1,0:T(8,128)(2,1)S(1)}, bf16[128,1024]{1,0:T(8,128)(2,1)S(1)}, u32[]{:S(2)}, u32[]{:S(2)}) collective-permute-start(bf16[128,1024]{1,0:T(8,128)(2,1)S(1)} %get-tuple-element.40), channel_id=1, source_target_pairs={{0,2},{1,5},{2,0},{3,7},{4,6},{5,1},{6,4},{7,3},{8,10},{9,13},{10,... | collective-permute-start | bytes 786440 | tf_op jit(solution)/shard_map/ppermute | solution.py:24
  28.9 8.0 %collective-permute-start.13 = (bf16[512,256]{1,0:T(8,128)(2,1)S(1)}, bf16[512,256]{1,0:T(8,128)(2,1)S(1)}, u32[]{:S(2)}, u32[]{:S(2)}) collective-permute-start(bf16[512,256]{1,0:T(8,128)(2,1)S(1)} %pad_maximum_fusion), channel_id=1, source_target_pairs={{0,1},{1,0},{2,3},{3,2},{4,5},{5,4},{6,7},{7,6},{8,9},{9,8},{10,11... | collective-permute-start | bytes 786440 | tf_op jit(solution)/shard_map/ppermute | solution.py:24
  29.0 5.1 %collective-permute-start.17 = (bf16[64,1024]{1,0:T(8,128)(2,1)S(1)}, bf16[64,1024]{1,0:T(8,128)(2,1)S(1)}, u32[]{:S(2)}, u32[]{:S(2)}) collective-permute-start(bf16[64,1024]{1,0:T(8,128)(2,1)S(1)} %get-tuple-element.42), channel_id=1, source_target_pairs={{0,2},{1,5},{2,0},{3,7},{4,6},{5,1},{6,4},{7,3},{8,10},{9,13},{10,... | collective-permute-start | bytes 393224 | tf_op jit(solution)/shard_map/ppermute | solution.py:24
  30.3 6.6 %collective-permute-start.16 = (bf16[64,1024]{1,0:T(8,128)(2,1)S(1)}, bf16[64,1024]{1,0:T(8,128)(2,1)S(1)}, u32[]{:S(2)}, u32[]{:S(2)}) collective-permute-start(bf16[64,1024]{1,0:T(8,128)(2,1)S(1)} %get-tuple-element.55), channel_id=1, source_target_pairs={{0,2},{1,5},{2,0},{3,7},{4,6},{5,1},{6,4},{7,3},{8,10},{9,13},{10,... | collective-permute-start | bytes 393224 | tf_op jit(solution)/shard_map/ppermute | solution.py:24
  31.1 11.0 %collective-permute-start.15 = (bf16[64,1024]{1,0:T(8,128)(2,1)S(1)}, bf16[64,1024]{1,0:T(8,128)(2,1)S(1)}, u32[]{:S(2)}, u32[]{:S(2)}) collective-permute-start(bf16[64,1024]{1,0:T(8,128)(2,1)S(1)} %add.35), channel_id=1, source_target_pairs={{0,4},{1,3},{2,6},{3,1},{4,0},{5,7},{6,2},{7,5},{8,12},{9,11},{10,... | collective-permute-start | bytes 393224 | tf_op jit(solution)/shard_map/ppermute | solution.py:24
  34.1 4.6 %collective-permute-start.18 = (bf16[32,1024]{1,0:T(8,128)(2,1)S(1)}, bf16[32,1024]{1,0:T(8,128)(2,1)S(1)}, u32[]{:S(2)}, u32[]{:S(2)}) collective-permute-start(bf16[32,1024]{1,0:T(8,128)(2,1)S(1)} %add.37), channel_id=1, source_target_pairs={{0,4},{1,3},{2,6},{3,1},{4,0},{5,7},{6,2},{7,5},{8,12},{9,11},{10,... | collective-permute-start | bytes 196616 | tf_op jit(solution)/shard_map/ppermute | solution.py:24
  36.5 5.3 %collective-permute-start.20 = (bf16[32,1024]{1,0:T(8,128)(2,1)S(1)}, bf16[32,1024]{1,0:T(8,128)(2,1)S(1)}, u32[]{:S(2)}, u32[]{:S(2)}) collective-permute-start(bf16[32,1024]{1,0:T(8,128)(2,1)S(1)} %add.39), channel_id=1, source_target_pairs={{0,4},{1,3},{2,6},{3,1},{4,0},{5,7},{6,2},{7,5},{8,12},{9,11},{10,... | collective-permute-start | bytes 196616 | tf_op jit(solution)/shard_map/ppermute | solution.py:24
  38.8 8.8 %collective-permute-start.19 = (bf16[32,1024]{1,0:T(8,128)(2,1)S(1)}, bf16[32,1024]{1,0:T(8,128)(2,1)S(1)}, u32[]{:S(2)}, u32[]{:S(2)}) collective-permute-start(bf16[32,1024]{1,0:T(8,128)(2,1)S(1)} %add.38), channel_id=1, source_target_pairs={{0,24},{1,25},{2,26},{3,27},{4,28},{5,29},{6,30},{7,31},{8,16},{9,... | collective-permute-start | bytes 196616 | tf_op jit(solution)/shard_map/ppermute | solution.py:24
  41.9 5.8 %collective-permute-start.21 = (bf16[32,1024]{1,0:T(8,128)(2,1)S(1)}, bf16[32,1024]{1,0:T(8,128)(2,1)S(1)}, u32[]{:S(2)}, u32[]{:S(2)}) collective-permute-start(bf16[32,1024]{1,0:T(8,128)(2,1)S(1)} %add.40), channel_id=1, source_target_pairs={{0,16},{1,17},{2,18},{3,19},{4,20},{5,21},{6,22},{7,23},{8,24},{9,... | collective-permute-start | bytes 196616 | tf_op jit(solution)/shard_map/ppermute | solution.py:24
  42.2 5.4 %collective-permute-start.22 = (bf16[32,1024]{1,0:T(8,128)(2,1)S(1)}, bf16[32,1024]{1,0:T(8,128)(2,1)S(1)}, u32[]{:S(2)}, u32[]{:S(2)}) collective-permute-start(bf16[32,1024]{1,0:T(8,128)(2,1)S(1)} %add.41), channel_id=1, source_target_pairs={{0,8},{1,9},{2,10},{3,11},{4,12},{5,13},{6,14},{7,15},{8,0},{9,1},... | collective-permute-start | bytes 196616 | tf_op jit(solution)/shard_map/ppermute | solution.py:24
